TPU v7x, 32 devices: a whole 2x2x4 slice. The times are simulated.
32 devices in a mesh: img: 8 (over z, x), seq: 4 (over y, core).
Axes of the slice: x: 2, y: 2, z: 4, core: 2. Of those that a mesh axis runs over, the one named last changes fastest.
Arguments:
- tokens: bfloat16 [16, 1024, 1152], P('img', 'seq'), may hold values from -6 to 6
- time_embed: bfloat16 [16, 4, 1152], P('img'), may hold values from -6 to 6
- image_lengths: int32 [16, 4], P('img'), may hold values from 0 to 1024, as said below
- grid_turns: int32 [16, 4], P('img'), may hold values from 0 to 7
- ln1_gain: float32 [1152], replicated, may hold values from 0.5 to 1.5
- w_qkv: bfloat16 [1152, 3456], replicated, may hold values from -0.1875 to 0.1875
- w_time_q: bfloat16 [1152, 1152], replicated, may hold values from -0.1875 to 0.1875
- time_value_weight: bfloat16 [1152, 1152], replicated, may hold values from -0.0234375 to 0.0234375
- rel_rows: float32 [16, 63], replicated, may hold values from -3 to 3
- rel_cols: float32 [16, 63], replicated, may hold values from -3 to 3
- output_projection_weight: bfloat16 [1152, 1152], replicated, may hold values from -1.5 to 1.5
- ln2_gain: float32 [1152], replicated, may hold values from 0.5 to 1.5
- w_up: bfloat16 [1152, 4608], replicated, may hold values from -0.1875 to 0.1875
- w_down: bfloat16 [4608, 1152], replicated, may hold values from -0.09375 to 0.09375
- out_grad: bfloat16 [16, 1024, 1152], P('img', 'seq'), may hold values from -6 to 6
Outputs:
- output: bfloat16 [16, 1024, 1152], P('img', 'seq')
- input_grad: bfloat16 [16, 1024, 1152], P('img', 'seq')
- ln1_gain_grad: float32 [1152], P('img')
- w_qkv_grad: float32 [1152, 3456], P('img')
- w_time_q_grad: float32 [1152, 1152], P('img')
- w_time_v_grad: float32 [1152, 1152], P('img')
- rel_rows_grad: float32 [16, 63], replicated
- rel_cols_grad: float32 [16, 63], replicated
- w_proj_grad: float32 [1152, 1152], P('img')
- ln2_gain_grad: float32 [1152], P('img')
- w_up_grad: float32 [1152, 4608], P('img')
- w_down_grad: float32 [4608, 1152], P('img')
- rms_values: float32 [3], replicated
Inputs may be any that keep to these rules, and one draw needn't show every extreme that they name: `image_lengths`: A slot holds one image of 1024 tokens, or one to four images of 256 tokens, or nothing; images come first, the rest of its 1024 tokens is padding. Every group of 2 slots along img has a slot with a 1024-token image, and one group has no empty slot. `grid_turns`: bit 0 flips the grid's rows, bit 1 its columns, bit 2 swaps rows and columns.
All inputs are finite; a program needn't handle non-finite values.
Results may differ from a plain program's by a relative error of at most 0.022.
Values may be sent and summed in bfloat16 or wider, within the bound.
No kernel may reach another device: no remote copies, remote signals or barrier semaphores. Data moves between devices by JAX's collectives and lax.ppermute only.
A program may use at most 384 MiB of HBM per device.

v0:
```python
import functools
import math

import jax
import jax.numpy as jnp
from jax import lax
from jax.experimental import pallas as pl
from jax.experimental.pallas import tpu as pltpu
from jax.sharding import PartitionSpec as P

SIDE = 32
EPS = 1e-06
FAR = -1e30
LANES = 128
BF = jnp.bfloat16
F32 = jnp.float32
VMEM_LIMIT = 56 * 2**20
QUERY_BLOCK = 512
FF_STEP = 512

RC = 2 * SIDE
KEY_MASK = RC
QUERY_MASK = KEY_MASK + 16
IMAGE_HOT = QUERY_MASK + 16
FEATURES = IMAGE_HOT + 16
ANYWHERE = pl.BlockSpec(memory_space=pl.ANY)


def dot(a, b, ca, cb):
    return lax.dot_general(a, b, (((ca,), (cb,)), ((), ())), preferred_element_type=F32)


def params(*semantics):
    return pltpu.CompilerParams(dimension_semantics=semantics, vmem_limit_bytes=VMEM_LIMIT)


CHEAP = pl.CostEstimate(flops=10**6, bytes_accessed=10**5, transcendentals=0)


def features_kernel(len_ref, turn_ref, base_ref, feat_ref, valid_ref, *, span):
    tokens = feat_ref.shape[1]

    def describe(shape, axis):
        index = lax.broadcasted_iota(jnp.int32, shape, axis)
        block = index // span
        pos = index - block * span
        for k in range(tokens // span):
            pos = pos + jnp.where(block == k, base_ref[k], 0)
        ends = []
        total = 0
        for j in range(4):
            total = total + len_ref[j]
            ends.append(total)
        segment = sum((pos >= ends[j]).astype(jnp.int32) for j in range(4))
        return pos, ends, segment

    pos, ends, segment = describe((1, tokens), 1)
    picked = jnp.minimum(segment, 3)
    begin = jnp.zeros_like(pos)
    length = jnp.zeros_like(pos)
    turn = jnp.zeros_like(pos)
    for j in range(4):
        here = picked == j
        begin = jnp.where(here, ends[j] - len_ref[j], begin)
        length = jnp.where(here, len_ref[j], length)
        turn = jnp.where(here, turn_ref[j], turn)
    full = length == SIDE * SIDE
    side = jnp.where(full, SIDE, SIDE // 2)
    u = pos - begin
    bits = SIDE.bit_length() - 1
    r0 = jnp.where(full, u >> bits, u >> (bits - 1))
    c0 = u & (side - 1)
    r1 = jnp.where((turn & 1) == 1, side - 1 - r0, r0)
    c1 = jnp.where(((turn >> 1) & 1) == 1, side - 1 - c0, c0)
    valid = pos < ends[3]
    row = jnp.where(valid, jnp.where(turn >= 4, c1, r1), 0)
    col = jnp.where(valid, jnp.where(turn >= 4, r1, c1), 0)
    which = lax.broadcasted_iota(jnp.int32, (SIDE, tokens), 0)
    few = lax.broadcasted_iota(jnp.int32, (16, tokens), 0)

    def put(start, value):
        feat_ref[start : start + value.shape[0], :] = value.astype(BF)

    put(0, jnp.where(which == row, 1.0, 0.0))
    put(SIDE, jnp.where(which == col, 1.0, 0.0))
    put(KEY_MASK, jnp.where(few == segment, 1.0, 0.0))
    put(QUERY_MASK, jnp.where((few < 5) & (few != segment), FAR, 0.0))
    put(IMAGE_HOT, jnp.where(few == picked, 1.0, 0.0))
    down_pos, down_ends, unused = describe(valid_ref.shape, 0)
    valid_ref[...] = jnp.where(down_pos < down_ends[3], 1.0, 0.0)


def token_features(lengths, turns, bases, span, mine):
    tokens = bases.shape[0] * span
    smem = pl.BlockSpec(memory_space=pltpu.SMEM)
    return pl.pallas_call(
        functools.partial(features_kernel, span=span),
        out_shape=(
            jax.ShapeDtypeStruct((FEATURES, tokens), BF),
            jax.ShapeDtypeStruct((mine, LANES), F32),
        ),
        in_specs=[smem, smem, smem],
        cost_estimate=CHEAP,
        name="token_features",
    )(lengths, turns, bases)


def window(cols):
    return -(-(cols + LANES // 2) // LANES) * LANES


def fetch(part, core, w_ref, room, sems, cols, dm):
    start = part * dm + (core * cols) // LANES * LANES
    start = pl.multiple_of(start, LANES)
    return pltpu.make_async_copy(
        w_ref.at[:, pl.ds(start, room.shape[2])], room.at[part], sems.at[part]
    )


def project_kernel(
    core_ref, a_ref, b_ref, c_ref, d_ref, gain_ref, time_ref, feat_ref, w_ref,
    in_ref, x_ref, qkv_ref, room, wide, sems, *, scale, cols,
):
    part = pl.program_id(0)
    core = core_ref[0]
    dm = in_ref.shape[1]
    width = qkv_ref.shape[2]

    @pl.when(part == 0)
    def _():
        for k in range(3):
            fetch(k, core, w_ref, room, sems, cols, dm).start()
        rows = a_ref.shape[0]
        x_ref[:rows, :] = a_ref[...]
        x_ref[rows:, :] = b_ref[...]
        for k, ref in enumerate((a_ref, b_ref, c_ref, d_ref)):
            x = ref[...].astype(F32)
            centre = x - jnp.mean(x, axis=-1, keepdims=True)
            spread = jnp.mean(centre * centre, axis=-1, keepdims=True)
            normed = centre * lax.rsqrt(spread + EPS) * gain_ref[...]
            in_ref[k * rows : (k + 1) * rows, :] = normed.astype(BF)

    fetch(part, core, w_ref, room, sems, cols, dm).wait()
    wide[...] = dot(room[part], in_ref[...], 0, 1)
    shift = core * cols - (core * cols) // LANES * LANES
    factor = jnp.where(part == 0, scale, 1.0)
    hot = feat_ref[IMAGE_HOT:, :].astype(F32)
    for h in range(cols // width):
        at = pl.multiple_of(shift + h * width, 8)
        x = wide[pl.ds(at, width), :]
        t = time_ref[0, h * width : (h + 1) * width, :]
        for j in range(4):
            x = x + t[:, j : j + 1] * hot[j : j + 1]
        qkv_ref[0, h] = (x * factor).astype(BF)


def project(core, blocks, gain, times, feats, w_qkv, scale, heads):
    rows, dm = blocks[0].shape
    tokens = 4 * rows
    cols = times.shape[1]
    width = cols // heads
    whole = lambda p, t: (0, 0)
    room = window(cols)
    return pl.pallas_call(
        functools.partial(project_kernel, scale=scale, cols=cols),
        grid_spec=pltpu.PrefetchScalarGridSpec(
            num_scalar_prefetch=1,
            grid=(3,),
            in_specs=[pl.BlockSpec((rows, dm), whole)] * 4
            + [
                pl.BlockSpec((1, dm), whole),
                pl.BlockSpec((1, cols, 4), lambda p, t: (p, 0, 0)),
                pl.BlockSpec(feats.shape, whole),
                ANYWHERE,
            ],
            out_specs=[
                pl.BlockSpec((tokens, dm), whole),
                pl.BlockSpec((2 * rows, dm), whole),
                pl.BlockSpec((1, heads, width, tokens), lambda p, t: (p, 0, 0, 0)),
            ],
            scratch_shapes=[
                pltpu.VMEM((3, dm, room), BF),
                pltpu.VMEM((room, tokens), F32),
                pltpu.SemaphoreType.DMA((3,)),
            ],
        ),
        out_shape=[
            jax.ShapeDtypeStruct((tokens, dm), BF),
            jax.ShapeDtypeStruct((2 * rows, dm), BF),
            jax.ShapeDtypeStruct((3, heads, width, tokens), BF),
        ],
        compiler_params=params("arbitrary"),
        cost_estimate=CHEAP,
        name="project",
    )(core, *blocks, gain, times, feats, w_qkv)


def weights_kernel(clock_ref, in_ref, d_ref, out_ref):
    d = jnp.concatenate([d_ref[0, h].astype(F32) for h in range(d_ref.shape[1])], axis=0)
    out_ref[0] = dot(in_ref[...], d.astype(BF), 0, 1).astype(BF)


def project_weights(clock, attn_in, d):
    parts, heads, width, tokens = d.shape
    dm = attn_in.shape[1]
    return pl.pallas_call(
        weights_kernel,
        grid_spec=pltpu.PrefetchScalarGridSpec(
            num_scalar_prefetch=1,
            grid=(parts,),
            in_specs=[
                pl.BlockSpec((tokens, dm), lambda p, t: (0, 0)),
                pl.BlockSpec((1, heads, width, tokens), lambda p, t: (p, 0, 0, 0)),
            ],
            out_specs=pl.BlockSpec((1, dm, heads * width), lambda p, t: (p, 0, 0)),
        ),
        out_shape=jax.ShapeDtypeStruct((parts, dm, heads * width), BF),
        compiler_params=params("arbitrary"),
        cost_estimate=CHEAP,
        name="project_weights",
    )(clock, attn_in, d)


def project_back_kernel(
    clock_ref, core_ref, d_ref, w_ref, mine_ref, far_ref, room, wide, total, sems, *, cols
):
    part = pl.program_id(0)
    core = core_ref[0]
    dm = w_ref.shape[0]
    width = d_ref.shape[2]

    @pl.when(part == 0)
    def _():
        for k in range(3):
            fetch(k, core, w_ref, room, sems, cols, dm).start()
        wide[...] = jnp.zeros_like(wide)

    shift = core * cols - (core * cols) // LANES * LANES
    for h in range(cols // width):
        at = pl.multiple_of(shift + h * width, 8)
        wide[pl.ds(at, width), :] = d_ref[0, h].astype(F32)
    fetch(part, core, w_ref, room, sems, cols, dm).wait()
    term = dot(wide[...].astype(BF), room[part], 0, 1)

    @pl.when(part == 0)
    def _():
        total[...] = term

    @pl.when(part == 1)
    def _():
        total[...] += term

    @pl.when(part == 2)
    def _():
        rows = mine_ref.shape[0]
        mine_ref[...] = total[:rows, :] + term[:rows]
        far_ref[...] = (total[rows:, :] + term[rows:]).astype(BF)


def project_back(clock, core, d, w_qkv, mine):
    parts, heads, width, tokens = d.shape
    dm = w_qkv.shape[0]
    cols = heads * width
    room = window(cols)
    whole = lambda p, t, u: (0, 0)
    return pl.pallas_call(
        functools.partial(project_back_kernel, cols=cols),
        grid_spec=pltpu.PrefetchScalarGridSpec(
            num_scalar_prefetch=2,
            grid=(parts,),
            in_specs=[
                pl.BlockSpec((1, heads, width, tokens), lambda p, t, u: (p, 0, 0, 0)),
                ANYWHERE,
            ],
            out_specs=[pl.BlockSpec((mine, dm), whole), pl.BlockSpec((tokens - mine, dm), whole)],
            scratch_shapes=[
                pltpu.VMEM((3, dm, room), BF),
                pltpu.VMEM((room, tokens), F32),
                pltpu.VMEM((tokens, dm), F32),
                pltpu.SemaphoreType.DMA((3,)),
            ],
        ),
        out_shape=[
            jax.ShapeDtypeStruct((mine, dm), F32),
            jax.ShapeDtypeStruct((tokens - mine, dm), BF),
        ],
        compiler_params=params("arbitrary"),
        cost_estimate=CHEAP,
        name="project_back",
    )(clock, core, d, w_qkv)


def query_block(b, bias, feat_ref, q):
    at = slice(b * QUERY_BLOCK, (b + 1) * QUERY_BLOCK)
    return jnp.concatenate([bias[:, at], feat_ref[QUERY_MASK:IMAGE_HOT, at], q[:, at]], axis=0)


def forward_kernel(clock_ref, p_ref, table_ref, feat_ref, o_ref, lse_ref):
    blocks = p_ref.shape[3] // QUERY_BLOCK
    q, k, v = (p_ref[p, 0] for p in range(3))
    bias = jnp.dot(table_ref[0], feat_ref[:RC], preferred_element_type=F32).astype(BF)
    key = jnp.concatenate([feat_ref[:QUERY_MASK], k], axis=0).T

    def scores(b):
        return jnp.dot(key, query_block(b, bias, feat_ref, q), preferred_element_type=F32)

    ahead = scores(0)
    for b in range(blocks):
        at = slice(b * QUERY_BLOCK, (b + 1) * QUERY_BLOCK)
        s = ahead
        top = jnp.max(s, axis=0, keepdims=True)
        if b + 1 < blocks:
            ahead = scores(b + 1)
        e = jnp.exp(s - top)
        total = jnp.sum(e, axis=0, keepdims=True)
        o = jnp.dot(v, e.astype(BF), preferred_element_type=F32) / total
        o_ref[0, :, at] = o.astype(BF)
        lse_ref[0, :, at] = top + jnp.log(total)


def attend_forward(clock, qkv, tables, feats, first, count):
    parts, heads, width, tokens = qkv.shape
    return pl.pallas_call(
        forward_kernel,
        grid_spec=pltpu.PrefetchScalarGridSpec(
            num_scalar_prefetch=1,
            grid=(count,),
            in_specs=[
                pl.BlockSpec((parts, 1, width, tokens), lambda h, t: (0, first + h, 0, 0)),
                pl.BlockSpec((1, RC, RC), lambda h, t: (first + h, 0, 0)),
                pl.BlockSpec(feats.shape, lambda h, t: (0, 0)),
            ],
            out_specs=[
                pl.BlockSpec((1, width, tokens), lambda h, t: (h, 0, 0)),
                pl.BlockSpec((1, 1, tokens), lambda h, t: (h, 0, 0)),
            ],
        ),
        out_shape=[
            jax.ShapeDtypeStruct((count, width, tokens), BF),
            jax.ShapeDtypeStruct((count, 1, tokens), F32),
        ],
        compiler_params=params("arbitrary"),
        cost_estimate=CHEAP,
        name="attention_forward",
    )(clock, qkv, tables, feats)


def backward_kernel(clock_ref, qkv_ref, o_ref, do_ref, lse_ref, table_ref, feat_ref, *rest, scale):
    d_ref, toe_ref, image_ref = rest[-3:]
    width = o_ref.shape[1]
    tokens = o_ref.shape[2]
    q, k, v = (qkv_ref[p, 0] for p in range(3))
    do = do_ref[0]
    delta = jnp.sum(do.astype(F32) * o_ref[0].astype(F32), axis=0, keepdims=True)
    rc = feat_ref[:RC]
    bias = jnp.dot(table_ref[0], rc, preferred_element_type=F32).astype(BF)
    key_t = jnp.concatenate([feat_ref[:QUERY_MASK], k], axis=0)
    key = key_t.T
    value = v.T
    dk = jnp.zeros((tokens, width), F32)
    dv = jnp.zeros((tokens, width), F32)
    dq_parts, bias_parts = [], []

    def first(b):
        at = slice(b * QUERY_BLOCK, (b + 1) * QUERY_BLOCK)
        s = jnp.dot(key, query_block(b, bias, feat_ref, q), preferred_element_type=F32)
        return s, jnp.dot(value, do[:, at], preferred_element_type=F32)

    ahead = first(0)
    for b in range(tokens // QUERY_BLOCK):
        at = slice(b * QUERY_BLOCK, (b + 1) * QUERY_BLOCK)
        s, dp = ahead
        p = jnp.exp(s - lse_ref[0, :, at])
        ds = (p * (dp - delta[:, at])).astype(BF)
        p = p.astype(BF)
        if (b + 1) * QUERY_BLOCK < tokens:
            ahead = first(b + 1)
        dq = jnp.dot(key_t, ds, preferred_element_type=F32)
        dq_parts.append((dq[QUERY_MASK:] * scale).astype(BF))
        bias_parts.append(dq[:RC].astype(BF))
        dk = dk + dot(ds, q[:, at], 1, 1)
        dv = dv + dot(p, do[:, at], 1, 1)
    toe = dot(rc, jnp.concatenate(bias_parts, axis=1), 1, 1)
    dq = jnp.concatenate(dq_parts, axis=1)
    dk = dk.T.astype(BF)
    dv = dv.T.astype(BF)
    d_ref[0, 0] = dq
    d_ref[1, 0] = dk
    d_ref[2, 0] = dv
    toe_ref[0] = toe
    hot = feat_ref[IMAGE_HOT:]
    image_ref[0, 0] = dot(hot, dq, 1, 1)
    image_ref[1, 0] = dot(hot, dv, 1, 1)


def attend_backward(clock, qkv, o, do, lse, tables, feats, scale, first, count, before):
    parts, heads, width, tokens = qkv.shape
    head3 = lambda h, t: (first + h, 0, 0)
    head4 = lambda h, t: (0, first + h, 0, 0)
    return pl.pallas_call(
        functools.partial(backward_kernel, scale=scale),
        grid_spec=pltpu.PrefetchScalarGridSpec(
            num_scalar_prefetch=1,
            grid=(count,),
            in_specs=[
                pl.BlockSpec((parts, 1, width, tokens), head4),
                pl.BlockSpec((1, width, tokens), head3),
                pl.BlockSpec((1, width, tokens), head3),
                pl.BlockSpec((1, 1, tokens), head3),
                pl.BlockSpec((1, RC, RC), head3),
                pl.BlockSpec(feats.shape, lambda h, t: (0, 0)),
            ]
            + [ANYWHERE] * len(before),
            out_specs=[
                pl.BlockSpec((parts, 1, width, tokens), head4),
                pl.BlockSpec((1, RC, RC), head3),
                pl.BlockSpec((2, 1, 16, width), head4),
            ],
        ),
        out_shape=[
            jax.ShapeDtypeStruct((parts, heads, width, tokens), BF),
            jax.ShapeDtypeStruct((heads, RC, RC), F32),
            jax.ShapeDtypeStruct((2, heads, 16, width), F32),
        ],
        input_output_aliases={7 + k: k for k in range(len(before))},
        compiler_params=params("arbitrary"),
        cost_estimate=CHEAP,
        name="attention_backward",
    )(clock, qkv, o, do, lse, tables, feats, *before)


def rise_kernel(
    m_ref, near_ref, far_ref, valid_ref, up_ref, down_ref,
    two_ref, slope_ref, wd_ref, mt_ref, g_ref,
):
    @pl.when(pl.program_id(0) == 0)
    def _():
        two_ref[...] = jnp.zeros_like(two_ref)
        mt_ref[...] = m_ref[...].T
        half = near_ref.shape[0]
        g_ref[:half, :] = (near_ref[...].astype(F32) * valid_ref[:half, :1]).astype(BF)
        g_ref[half:, :] = (far_ref[...].astype(F32) * valid_ref[half:, :1]).astype(BF)

    def up_of(j):
        return jnp.dot(m_ref[...], up_ref[:, j : j + FF_STEP], preferred_element_type=F32)

    acts = []
    tile = up_ref.shape[1]
    ahead = up_of(0)
    for j in range(0, tile, FF_STEP):
        at = slice(j, j + FF_STEP)
        up = ahead
        if j + FF_STEP < tile:
            ahead = up_of(j + FF_STEP)
        half = 0.5 + 0.5 * lax.erf(up * math.sqrt(0.5))
        slope = half + up * (jnp.exp(-0.5 * up * up) * (1.0 / math.sqrt(2.0 * math.pi)))
        slope_ref[:, at] = slope.astype(BF)
        acts.append((up * half).astype(BF))
    act = jnp.concatenate(acts, axis=1)
    wd_ref[...] = dot(act, g_ref[...], 0, 0).astype(BF)
    two_ref[...] += jnp.dot(act, down_ref[...], preferred_element_type=F32)


def mlp_rise(m, near, far, valid, w_up, w_down, tile):
    rows, dm = m.shape
    ff = w_up.shape[1]
    whole = lambda i: (0, 0)
    return pl.pallas_call(
        rise_kernel,
        grid=(ff // tile,),
        in_specs=[
            pl.BlockSpec((rows, dm), whole),
            pl.BlockSpec(near.shape, whole),
            pl.BlockSpec(far.shape, whole),
            pl.BlockSpec(valid.shape, whole),
            pl.BlockSpec((dm, tile), lambda i: (0, i)),
            pl.BlockSpec((tile, dm), lambda i: (i, 0)),
        ],
        out_specs=[
            pl.BlockSpec((rows, dm), whole),
            pl.BlockSpec((rows, tile), lambda i: (0, i)),
            pl.BlockSpec((tile, dm), lambda i: (i, 0)),
            pl.BlockSpec((dm, rows), whole),
            pl.BlockSpec((rows, dm), whole),
        ],
        out_shape=[
            jax.ShapeDtypeStruct((rows, dm), F32),
            jax.ShapeDtypeStruct((rows, ff), BF),
            jax.ShapeDtypeStruct((ff, dm), BF),
            jax.ShapeDtypeStruct((dm, rows), BF),
            jax.ShapeDtypeStruct((rows, dm), BF),
        ],
        compiler_params=params("arbitrary"),
        cost_estimate=CHEAP,
        name="feed_forward_rise",
    )(m, near, far, valid, w_up, w_down)


def fall_kernel(clock_ref, tile_ref, mt_ref, g_ref, up_ref, down_ref, slope_ref, *rest):
    gm_out, send_ref, own_ref = rest[-3:]
    step = pl.program_id(0)

    @pl.when(step == 0)
    def _():
        gm_out[...] = rest[0][...] if len(rest) > 3 else jnp.zeros_like(gm_out)

    du = (dot(g_ref[...], down_ref[...], 1, 1) * slope_ref[...].astype(F32)).astype(BF)
    gm_out[...] += dot(du, up_ref[...], 1, 1)
    wu = jnp.dot(mt_ref[...], du, preferred_element_type=F32).astype(BF)

    @pl.when(step % 2 == 0)
    def _():
        send_ref[...] = wu

    @pl.when(step % 2 == 1)
    def _():
        own_ref[...] = wu


def mlp_fall(clock, tiles, mt, g, w_up, w_down, slope, tile, first, pairs, before):
    dm, rows = mt.shape
    ff = w_up.shape[1]
    whole = lambda i, u, t: (0, 0)
    column = lambda i, u, t: (0, first + i // 2)
    at = lambda i, t: 2 * (first + i // 2) + t[i % 2]
    return pl.pallas_call(
        fall_kernel,
        grid_spec=pltpu.PrefetchScalarGridSpec(
            num_scalar_prefetch=2,
            grid=(2 * pairs,),
            in_specs=[
                pl.BlockSpec((dm, rows), whole),
                pl.BlockSpec((rows, dm), whole),
                pl.BlockSpec((dm, tile), lambda i, u, t: (0, at(i, t))),
                pl.BlockSpec((tile, dm), lambda i, u, t: (at(i, t), 0)),
                pl.BlockSpec((rows, tile), lambda i, u, t: (0, at(i, t))),
            ]
            + ([pl.BlockSpec((rows, dm), whole), ANYWHERE, ANYWHERE] if before else []),
            out_specs=[
                pl.BlockSpec((rows, dm), whole),
                pl.BlockSpec((dm, tile), column),
                pl.BlockSpec((dm, tile), column),
            ],
        ),
        out_shape=[
            jax.ShapeDtypeStruct((rows, dm), F32),
            jax.ShapeDtypeStruct((dm, ff // 2), BF),
            jax.ShapeDtypeStruct((dm, ff // 2), BF),
        ],
        input_output_aliases={8: 1, 9: 2} if before else {},
        compiler_params=params("arbitrary"),
        cost_estimate=CHEAP,
        name="feed_forward_fall",
    )(clock, tiles, mt, g, w_up, w_down, slope, *before)


def moments(x):
    centre = x - jnp.mean(x, axis=-1, keepdims=True)
    root = lax.rsqrt(jnp.mean(centre * centre, axis=-1, keepdims=True) + EPS)
    return centre * root, root


def norm_backward(d, n, root):
    return root * (
        d - jnp.mean(d, axis=-1, keepdims=True) - n * jnp.mean(d * n, axis=-1, keepdims=True)
    )


def columns(x):
    return jnp.sum(x, axis=0, keepdims=True)


def middle_kernel(
    clock_ref, gm_ref, two_ref, one_ref, h_ref, g_ref, valid_ref, gain_ref,
    out_ref, grad_ref, low_ref, sums_ref,
):
    @pl.when(pl.program_id(0) == 0)
    def _():
        sums_ref[...] = jnp.zeros_like(sums_ref)

    valid = valid_ref[:, :1]
    two, one, h = two_ref[...], one_ref[...], h_ref[...]
    h2 = h + two
    out_ref[...] = (h2 * valid).astype(BF)
    n, root = moments(h)
    gm = gm_ref[...]
    grad = g_ref[...].astype(F32) + norm_backward(gm * gain_ref[...], n, root)
    grad_ref[...] = grad
    low_ref[...] = grad.astype(BF)
    sums_ref[0:1, :] += columns(gm * n)
    sums_ref[1:2, :] += columns(valid * h2 * h2)
    sums_ref[2:3, :] += columns(valid * one * one)
    sums_ref[3:4, :] += columns(valid * two * two)


def middle(clock, gm, two, one, hidden, grads, valid, gain):
    rows, dm = gm.shape
    step = rows // 4
    block = pl.BlockSpec((step, dm), lambda i, t: (i, 0))
    return pl.pallas_call(
        middle_kernel,
        grid_spec=pltpu.PrefetchScalarGridSpec(
            num_scalar_prefetch=1,
            grid=(4,),
            in_specs=[block] * 5
            + [
                pl.BlockSpec((step, LANES), lambda i, t: (i, 0)),
                pl.BlockSpec((1, dm), lambda i, t: (0, 0)),
            ],
            out_specs=[block, block, block, pl.BlockSpec((8, dm), lambda i, t: (0, 0))],
        ),
        out_shape=[
            jax.ShapeDtypeStruct((rows, dm), BF),
            jax.ShapeDtypeStruct((rows, dm), F32),
            jax.ShapeDtypeStruct((rows, dm), BF),
            jax.ShapeDtypeStruct((8, dm), F32),
        ],
        compiler_params=params("arbitrary"),
        cost_estimate=CHEAP,
        name="middle",
    )(clock, gm, two, one, hidden, grads, valid, gain)


def last_kernel(back_ref, far_ref, x_ref, grad_ref, gain_ref, out_ref, sums_ref):
    @pl.when(pl.program_id(0) == 0)
    def _():
        sums_ref[...] = jnp.zeros_like(sums_ref)

    back = back_ref[...] + far_ref[...].astype(F32)
    n, root = moments(x_ref[...].astype(F32))
    out_ref[...] = (grad_ref[...] + norm_backward(back * gain_ref[...], n, root)).astype(BF)
    sums_ref[0:1, :] += columns(back * n)


def last(back, far, x, grad, gain):
    rows, dm = back.shape
    step = rows // 4
    block = pl.BlockSpec((step, dm), lambda i: (i, 0))
    return pl.pallas_call(
        last_kernel,
        grid=(4,),
        in_specs=[block] * 4 + [pl.BlockSpec((1, dm), lambda i: (0, 0))],
        out_specs=[block, pl.BlockSpec((8, dm), lambda i: (0, 0))],
        out_shape=[jax.ShapeDtypeStruct((rows, dm), BF), jax.ShapeDtypeStruct((8, dm), F32)],
        compiler_params=params("arbitrary"),
        cost_estimate=CHEAP,
        name="last",
    )(back, far, x, grad, gain)


class Halving:
    def __init__(self, names, dims, base, piece, prefix=(), suffix=(), column=0):
        self.names, self.dims, self.base, self.piece = names, dims, base, piece
        self.prefix, self.suffix, self.column = prefix, suffix, column
        self.stage, self.arrived, self.result = 0, [], None

    def left(self, stage):
        return [d for d in self.names if d in self.dims[stage + 1 :]]

    def specs(self, gridded):
        stage = self.stage
        open_dims = self.left(stage)

        def index(names, prefix, suffix, column):
            def at(*grid):
                t = grid[-1]
                out = list(prefix)
                for d in names:
                    if d in gridded:
                        out.append(grid[gridded.index(d)])
                    elif d in open_dims:
                        out.append(0)
                    elif stage < len(self.dims) and d == self.dims[stage]:
                        out.append(1 - t[d])
                    else:
                        out.append(t[d])
                return tuple(out) + tuple(suffix) + (0, column)

            return at

        def block(names, prefix, suffix):
            sizes = [2 if d in open_dims and d not in gridded else None for d in names]
            return (None,) * len(prefix) + tuple(sizes) + (None,) * len(suffix) + self.piece

        arrays, specs = [], []
        for array in self.base:
            arrays.append(array)
            specs.append(
                pl.BlockSpec(
                    block(self.names, self.prefix, self.suffix),
                    index(self.names, self.prefix, self.suffix, self.column),
                )
            )
        for s, (array, place) in enumerate(self.arrived):
            arrays.append(array)
            names = self.left(s)
            specs.append(pl.BlockSpec(block(names, (place,), ()), index(names, (place,), (), 0)))
        rest = index(open_dims, (), (), 0)
        inner = tuple(2 if d not in gridded else None for d in open_dims) + self.piece
        return arrays, specs, inner, rest, (2,) * len(open_dims) + self.piece


def sum_kernel(coord_ref, *refs, counts, places):
    outs = refs[sum(counts) :]
    at = 0
    for (out, place), count in zip(places, counts):
        total = refs[at][...].astype(F32)
        for k in range(1, count):
            total = total + refs[at + k][...].astype(F32)
        outs[out][place] = total.astype(BF)
        at += count


def advance(clock, swaps, jobs):
    arrays, in_specs, counts, groups, places = [], [], [], [], []
    stage = jobs[0].stage
    steps = min(2, max(0, len(jobs[0].left(stage)) - 1))
    for job in jobs:
        some, their, inner, rest, shape = job.specs(job.left(stage)[:steps])
        arrays, in_specs = arrays + some, in_specs + their
        counts.append(len(some))
        sent = job.dims[stage] if stage < len(job.dims) else None
        key = (sent, shape)
        found = [k for k, g in enumerate(groups) if g[0] == key]
        if not found:
            groups.append((key, inner, rest, []))
        group = found[0] if found else len(groups) - 1
        places.append((group, len(groups[group][3])))
        groups[group][3].append(job)
    out_specs = [
        pl.BlockSpec((len(g[3]),) + g[1], lambda *grid, f=g[2]: (0,) + f(*grid)) for g in groups
    ]
    sums = pl.pallas_call(
        functools.partial(sum_kernel, counts=counts, places=places),
        grid_spec=pltpu.PrefetchScalarGridSpec(
            num_scalar_prefetch=1,
            grid=(2,) * steps if steps else (1,),
            in_specs=in_specs,
            out_specs=out_specs,
        ),
        out_shape=[jax.ShapeDtypeStruct((len(g[3]),) + g[0][1], BF) for g in groups],
        compiler_params=params(*("arbitrary",) * max(steps, 1)),
        cost_estimate=CHEAP,
        name="sum_pieces",
    )(clock.now, *arrays)
    for (key, inner, rest, members), total in zip(groups, sums):
        if key[0] is not None:
            total = swaps[key[0]](total)
        for k, job in enumerate(members):
            if key[0] is None:
                job.result = total[k]
            else:
                job.arrived.append((total, k))
                job.stage += 1
    clock.passed(*sums)


class Clock:
    def __init__(self, now):
        self.now = now

    def passed(self, *results):
        self.now = lax.optimization_barrier((self.now, *results))[0]

    def tie(self, x):
        return lax.optimization_barrier((x, self.now))[0]


class Gather:
    def __init__(self, clock, part, swaps):
        self.clock, self.part, self.swaps, self.far = clock, part, list(swaps), None

    def tick(self):
        if self.far is not None:
            bit, axis = self.put
            low, high = jnp.where(bit, self.far, self.part), jnp.where(bit, self.part, self.far)
            self.part = jnp.concatenate([low, high], axis=axis)
            self.clock.passed(self.part)
            self.far = None
        if self.swaps:
            swap, bit, axis = self.swaps.pop(0)
            self.put = (bit, axis)
            self.far = swap(self.clock.tie(self.part))

    def finish(self):
        while self.far is not None or self.swaps:
            self.tick()
        return self.part


class Total:
    def __init__(self, clock, part, swaps):
        self.clock, self.part, self.swaps, self.far = clock, part, list(swaps), None

    def tick(self):
        if self.far is not None:
            self.part = self.part + self.far
            self.clock.passed(self.part)
            self.far = None
        if self.swaps:
            self.far = self.swaps.pop(0)(self.clock.tie(self.part))

    def finish(self):
        while self.far is not None or self.swaps:
            self.tick()
        return self.part


def pick(array, index, axis=0):
    return lax.dynamic_index_in_dim(array, index, axis, keepdims=False)


def toeplitz_tables(rel, count):
    d = jnp.arange(2 * count - 1, dtype=jnp.int32)
    t = jnp.arange(count, dtype=jnp.int32)
    hot = (d[:, None, None] == t[None, None, :] - t[None, :, None] + count - 1).astype(BF)
    return jnp.einsum("hd,dtr->htr", rel.astype(BF), hot, preferred_element_type=F32)


def per_device(
    tokens, time_embed, image_lengths, grid_turns, ln1_gain, w_qkv, w_time_q, time_value_weight,
    rel_rows, rel_cols, output_projection_weight, ln2_gain, w_up, w_down, out_grad,
):
    slots, span, dm = tokens.shape
    heads = rel_rows.shape[0]
    width = dm // heads
    ff = w_up.shape[1]
    scale = width ** (-0.5)
    n_seq = lax.axis_size("seq")
    n_img = lax.axis_size("img")
    cores = n_seq // slots
    own_heads = heads // cores
    cols = own_heads * width
    me_img = lax.axis_index("img")
    me_seq = lax.axis_index("seq")
    y = me_seq // cores
    c = me_seq % cores
    mine = slots * span
    rows = dm // n_img
    over_y = [(s, (slots - 1 - s // cores) * cores + s % cores) for s in range(n_seq)]
    over_core = [(s, s // cores * cores + cores - 1 - s % cores) for s in range(n_seq)]

    def swap_y(a):
        return lax.ppermute(a, "seq", over_y)

    def swap_core(a):
        return lax.ppermute(a, "seq", over_core)

    bits = n_img.bit_length() - 1
    on_y, on_core = bits, bits + 1
    swaps = {
        k: functools.partial(
            lax.ppermute, axis_name="img", perm=[(i, i ^ (1 << k)) for i in range(n_img)]
        )
        for k in range(bits)
    }
    swaps[on_y], swaps[on_core] = swap_y, swap_core

    def across_y(parts):
        part = jnp.concatenate(parts, axis=1)
        return part, swap_y(part)

    def across_core(part, far):
        part = jnp.concatenate([jnp.where(y == 0, part, far), jnp.where(y == 0, far, part)], axis=0)
        return part, swap_core(part)

    def both_cores(part, far):
        return jnp.where(c == 0, part, far).astype(F32), jnp.where(c == 0, far, part).astype(F32)

    def order(*first):
        return list(first) + [k for k in range(bits) if k not in first]

    tok_own = pick(tokens, y)
    tok_rx = swap_y(pick(tokens, 1 - y))
    tok_own_far = swap_core(tok_own)
    block = lambda yy, cc: (yy * cores + cc) * span
    bases = jnp.stack([block(y, c), block(1 - y, c), block(y, 1 - c), block(1 - y, 1 - c)])
    feats, valid = token_features(
        pick(image_lengths, y), pick(grid_turns, y), bases.astype(jnp.int32), span, mine
    )
    coords = jnp.stack([(me_img >> k) & 1 for k in range(bits)] + [y, c]).astype(jnp.int32)
    core = c.astype(jnp.int32).reshape(1)
    pair = jnp.stack([1 - c, c]).astype(jnp.int32)
    te = pick(time_embed, y)

    def time_terms(w):
        all_heads = dot(te, w, 1, 0)
        return lax.dynamic_slice_in_dim(all_heads, c * cols, cols, 1).T

    time_q = time_terms(w_time_q)
    times = jnp.stack([time_q, jnp.zeros_like(time_q), time_terms(time_value_weight)])
    row_table = toeplitz_tables(lax.dynamic_slice_in_dim(rel_rows, c * own_heads, own_heads), SIDE)
    col_table = toeplitz_tables(lax.dynamic_slice_in_dim(rel_cols, c * own_heads, own_heads), SIDE)
    gap = jnp.zeros_like(row_table)
    tables = jnp.concatenate(
        [
            jnp.concatenate([row_table, gap], axis=2),
            jnp.concatenate([gap, col_table], axis=2),
        ],
        axis=1,
    ).astype(BF)
    ln1_row, ln2_row = ln1_gain.reshape(1, dm), ln2_gain.reshape(1, dm)
    grad_out = pick(out_grad, 1 - y)
    grad_own = pick(out_grad, y)

    img_bits = [((me_img >> k) & 1) == 1 for k in range(bits)]
    clock = Clock(coords)
    times_all = Gather(
        clock,
        lax.optimization_barrier((time_embed, feats))[0][None],
        [(swaps[k], img_bits[k], 0) for k in range(bits)],
    ).finish()
    clock.passed(feats, times, tables, core, pair, grad_out, grad_own, ln1_row, ln2_row)
    tok_rx = clock.tie(tok_rx)
    grad_rx = swap_y(lax.optimization_barrier((grad_out, tok_rx))[0])
    attn_in, x, qkv = project(
        core, (tok_own, tok_rx, tok_own_far, swap_core(tok_rx)), ln1_row, times, feats, w_qkv,
        scale, own_heads,
    )
    clock.passed(qkv)
    half_heads = own_heads // 2
    o_a, lse_a = attend_forward(clock.now, qkv, tables, feats, 0, half_heads)
    clock.passed(o_a, grad_rx)
    far_a = swap_core(o_a)
    o_b, lse_b = attend_forward(clock.now, qkv, tables, feats, half_heads, half_heads)
    far_b = swap_core(o_b)

    o_own = jnp.concatenate([o_a, o_b], axis=0)
    lse = jnp.concatenate([lse_a, lse_b], axis=0)
    clock.passed(o_b)

    def turned(a):
        a = a.reshape(cols // 2, 2 * mine)
        return jnp.concatenate([a[:, mine:], a[:, :mine]], axis=1)

    o_flat = o_own.reshape(cols, 2 * mine)
    o_far = jnp.concatenate([turned(far_a), turned(far_b)], axis=0)
    attn_all = jnp.concatenate(
        [jnp.where(c == 0, o_flat, o_far), jnp.where(c == 0, o_far, o_flat)], axis=0
    )
    branch_one = dot(attn_all[:, :mine], output_projection_weight, 0, 0)
    hidden_one = x.astype(F32) + branch_one
    mlp_in = (moments(hidden_one)[0] * ln2_gain).astype(BF)

    tile = ff // 6
    two, slope, down, mlp_in_t, grad_branch = mlp_rise(
        mlp_in, grad_own, grad_rx, valid, w_up, w_down, ff // 3
    )
    clock.passed(two)
    down = lax.psum_scatter(down, ("img", "seq"), scatter_dimension=0, tiled=True)
    img_names = list(range(bits))[::-1]
    twos = (2,) * bits
    step = functools.partial(advance, clock, swaps)

    def finish(jobs):
        while jobs[0].result is None:
            step(jobs)

    gm, send, own = mlp_fall(
        clock.now, pair, mlp_in_t, grad_branch, w_up, w_down, slope, tile, 0, 3, ()
    )
    clock.passed(gm)
    output, grad_one, gb_mine, sums = middle(
        clock.now, gm, two, branch_one, hidden_one, grad_branch, valid, ln2_row
    )
    clock.passed(output)
    far_up = swap_core(clock.tie(send))
    gb_all = jnp.concatenate([gb_mine, swap_core(gb_mine)], axis=0)
    out_far = swap_y(output[span:])
    w_proj_rows = lax.dynamic_slice_in_dim(output_projection_weight, c * cols, cols, 0)
    do = dot(w_proj_rows, gb_all, 1, 1).astype(BF).reshape(own_heads, width, 2 * mine)
    gb_cols = lax.dynamic_slice_in_dim(gb_all, c * cols, cols, 1)
    proj_part = dot(attn_all, gb_cols, 1, 0).astype(BF)
    clock.passed(do, proj_part)

    def by_row(dims, arrays, columns_of, column=0, prefix=()):
        shape = twos + (2, rows // 2)
        return Halving(
            img_names + [on_y],
            dims,
            [a.reshape(a.shape[: len(prefix)] + shape + a.shape[-1:]) for a in arrays],
            (rows // 2, columns_of),
            prefix=prefix,
            column=column,
        )

    orders = [order(0, on_y, 1), order(on_y, 1, 0), order(1, 0, on_y)]
    up_half = ff // 4
    jobs_up = [
        by_row(dims, (own, far_up), up_half, k)
        for k, dims in enumerate([order(0, on_y, 1), order(on_y, 0, 1)])
    ]
    job_proj = by_row(orders[2], (proj_part,), cols)
    step(jobs_up + [job_proj])
    grads = attend_backward(
        clock.now, qkv, o_own, do, lse, tables, feats, scale, 0, own_heads, ()
    )
    d, toe, image_grads = grads
    clock.passed(d)
    step(jobs_up)
    part = jnp.transpose(image_grads[:, :, :4], (0, 2, 1, 3)).reshape(8, cols).astype(BF)
    gather = Gather(
        clock,
        part[None, None],
        [(swap_core, c == 1, 3), (swap_y, y == 1, 1)]
        + [(swaps[k], img_bits[k], 0) for k in range(bits)],
    )
    gather.tick()
    w_part = project_weights(clock.now, attn_in, d)
    clock.passed(w_part, out_far)
    jobs_qkv = [by_row(dims, (w_part,), cols, prefix=(p,)) for p, dims in enumerate(orders)]
    step(jobs_qkv)
    jobs_qkv.append(job_proj)
    back, back_far = project_back(clock.now, core, d, w_qkv, mine)
    clock.passed(back)
    step(jobs_up)
    clock.passed(down)
    back_far = swap_core(clock.tie(back_far))
    step(jobs_qkv)
    input_grad, sums_one = last(back, back_far, x, grad_one, ln1_row)
    clock.passed(input_grad)
    reach = jnp.arange(2 * SIDE - 1, dtype=jnp.int32)
    side = jnp.arange(SIDE, dtype=jnp.int32)
    diag = (reach == side[:, None, None] - side[None, :, None] + SIDE - 1).astype(F32)
    rel = jnp.stack([toe[:, :SIDE, :SIDE], toe[:, SIDE:, SIDE:]])
    rel = jnp.einsum("khrt,rtd->khd", rel, diag, precision=lax.Precision.HIGHEST)
    rel_all = lax.dynamic_update_slice(
        jnp.zeros((2, heads, 2 * SIDE - 1), F32), rel, (0, c * own_heads, 0)
    )
    stats = jnp.concatenate([jnp.sum(sums[1:4], axis=1), jnp.sum(valid[:, 0])[None]])
    small = jnp.concatenate([sums_one[0], sums[0], rel_all.reshape(-1), stats])
    def returned(own_rows, far_rows):
        return jnp.stack(
            [jnp.where(y == 0, own_rows, far_rows), jnp.where(y == 0, far_rows, own_rows)]
        )

    small = Total(clock, small, [swap_core, swap_y] + [swaps[k] for k in range(bits)])

    step(jobs_qkv)
    gather.tick()
    output = returned(output[:span], out_far)
    clock.passed(output)
    step(jobs_up)
    small.tick()
    gather.tick()
    down = clock.tie(down)
    step(jobs_qkv)
    in_far = swap_y(clock.tie(input_grad)[span:])
    down_far = swap_y(down)
    small.tick()
    gather.tick()
    finish(jobs_up)
    up_parts, up_far = across_y([clock.tie(job.result) for job in jobs_up])
    finish(jobs_qkv)
    qkv_parts, qkv_far = across_y([job.result for job in jobs_qkv])
    down, down_far = clock.tie(down), clock.tie(down_far)
    down = jnp.where(y == 0, jnp.stack([down, down_far]), jnp.stack([down_far, down]))
    down_far = swap_core(down)
    small.tick()
    gather.tick()
    up_part, up_far = across_core(up_parts, clock.tie(up_far))
    h0, h1 = both_cores(down, down_far)
    w_down_grad = jnp.concatenate([h0[0], h1[0], h0[1], h1[1]], axis=0)
    clock.passed(w_down_grad)
    small.tick()
    gather.tick()
    qkv_part, qkv_far = across_core(qkv_parts, clock.tie(qkv_far))
    u0, u1 = both_cores(up_part, clock.tie(up_far))
    w_up_grad = jnp.concatenate(
        [u[:, k * tile : (k + 1) * tile] for k in range(3) for u in (u0, u1)], axis=1
    )
    clock.passed(w_up_grad)
    small = small.finish()
    factors = gather.finish().reshape(n_img * slots, 8, dm)
    in_far = clock.tie(in_far)

    te_rows = lax.dynamic_slice_in_dim(times_all, me_img * rows, rows, 3)
    w_time_q_grad, w_time_v_grad = (
        lax.dot_general(
            te_rows.reshape(-1, rows),
            factors[:, 4 * k : 4 * k + 4].reshape(-1, dm),
            (((0,), (0,)), ((), ())),
            preferred_element_type=F32,
        )
        for k in range(2)
    )
    ln1_gain_grad = lax.dynamic_slice_in_dim(small, me_img * rows, rows)
    ln2_gain_grad = lax.dynamic_slice_in_dim(small, dm + me_img * rows, rows)
    rel_all = small[2 * dm : -4].reshape(2, heads, 2 * SIDE - 1)
    rms_values = jnp.sqrt(small[-4:-1] / (small[-1] * dm))
    q0, q1 = both_cores(qkv_part, qkv_far)
    w_proj_grad = jnp.concatenate([q[:, 3 * cols :] for q in (q0, q1)], axis=1)
    w_qkv_grad = jnp.concatenate(
        [q[:, p * cols : (p + 1) * cols] for p in range(3) for q in (q0, q1)], axis=1
    )

    return (
        output,
        returned(input_grad[:span], in_far),
        ln1_gain_grad,
        w_qkv_grad,
        w_time_q_grad,
        w_time_v_grad,
        rel_all[0],
        rel_all[1],
        w_proj_grad,
        ln2_gain_grad,
        w_up_grad,
        w_down_grad,
        rms_values,
    )


def solution(mesh):
    return jax.shard_map(
        per_device,
        mesh=mesh,
        in_specs=(
            P("img", "seq", None),
            P("img", None, None),
            P("img", None),
            P("img", None),
        )
        + (P(),) * 10
        + (P("img", "seq", None),),
        out_specs=(
            P("img", "seq", None),
            P("img", "seq", None),
            P("img"),
            P("img", None),
            P("img", None),
            P("img", None),
            P(),
            P(),
            P("img", None),
            P("img"),
            P("img", None),
            P("img", None),
            P(),
        ),
        check_vma=False,
    )
```

profile of v0, /device:TPU:0, one launch (start us, length us, event | category | flops | bytes accessed | tf_op | source)
XLA Modules:
  0.0 418.3 jit_solution(13944060806405020771)
XLA Ops:
  11.5 2.9 collective-permute-start
  14.5 2.1 dynamic-slice_bitcast_fusion
  18.1 2.4 fusion.25
  23.7 2.3 dynamic-slice_bitcast_fusion.2
  27.0 1.6 collective-permute-start.1
  34.5 14.0 %project.1 = (bf16[1024,1152]{1,0:T(8,128)(2,1)}, bf16[512,1152]{1,0:T(8,128)(2,1)}, bf16[3,8,72,1024]{3,2,1,0:T(8,128)(2,1)}) custom-call(s32[1]{0:T(128)} %bitcast.4.core_ref, bf16[256,1152]{1,0:T(8,128)(2,1)} %copy-done.23, bf16[256,1152]{1,0:T(8,128)(2,1)} %collective-permute-done.3.b_ref, bf16[256,1152]{1,0:T(8,128)(2,1)} %collective-permute-done.4.c_ref, ...), custom_call_target="tpu_custom_call" | custom-call | flops 1000000 | bytes 100000 | tf_op jit(solution)/shard_map/project/pallas_call | solution.py:164
  48.5 9.2 %attention_forward.2 = (bf16[4,72,1024]{2,1,0:T(8,128)(2,1)}, f32[4,1,1024]{2,1,0:T(1,128)}) custom-call(s32[5]{0:T(128)} %stack.95.clock_ref.coord_ref, bf16[3,8,72,1024]{3,2,1,0:T(8,128)(2,1)} %get-tuple-element.127.p_ref.qkv_ref, bf16[8,64,64]{2,1,0:T(8,128)(2,1)} %fusion.20.table_ref, bf16[112,1024]{1,0:T(8,128)(2,1)} %get-tuple-element.117.feat_ref), custom_call_target="tpu_custom_call" | custom-call | flops 1000000 | bytes 100000 | tf_op jit(solution)/shard_map/attention_forward/pallas_call | solution.py:323
  57.9 9.3 %attention_forward.3 = (bf16[4,72,1024]{2,1,0:T(8,128)(2,1)}, f32[4,1,1024]{2,1,0:T(1,128)}) custom-call(s32[5]{0:T(128)} %stack.95.clock_ref.coord_ref, bf16[3,8,72,1024]{3,2,1,0:T(8,128)(2,1)} %get-tuple-element.127.p_ref.qkv_ref, bf16[8,64,64]{2,1,0:T(8,128)(2,1)} %fusion.20.table_ref, bf16[112,1024]{1,0:T(8,128)(2,1)} %get-tuple-element.117.feat_ref), custom_call_target="tpu_custom_call" | custom-call | flops 1000000 | bytes 100000 | tf_op jit(solution)/shard_map/attention_forward/pallas_call | solution.py:323
  72.5 3.4 fusion.42
  77.7 27.5 %feed_forward_rise.1 = (f32[512,1152]{1,0:T(8,128)}, bf16[512,4608]{1,0:T(8,128)(2,1)}, bf16[4608,1152]{1,0:T(8,128)(2,1)}, bf16[1152,512]{1,0:T(8,128)(2,1)}, bf16[512,1152]{1,0:T(8,128)(2,1)}) custom-call(bf16[512,1152]{1,0:T(8,128)(2,1)} %multiply_convert_fusion.m_ref, bf16[256,1152]{1,0:T(8,128)(2,1)} %get-tuple-element.249.near_ref, ...), custom_call_target="tpu_custom_call" | custom-call | flops 1000000 | bytes 100000 | tf_op jit(solution)/shard_map/feed_forward_rise/pallas_call | solution.py:468
  105.2 29.7 %feed_forward_fall.1 = (f32[512,1152]{1,0:T(8,128)}, bf16[1152,2304]{1,0:T(8,128)(2,1)}, bf16[1152,2304]{1,0:T(8,128)(2,1)}) custom-call(s32[5]{0:T(128)} %stack.95.clock_ref.coord_ref, s32[2]{0:T(128)} %pad_add_fusion.1.tile_ref, bf16[1152,512]{1,0:T(8,128)(2,1)} %get-tuple-element.138.mt_ref, bf16[512,1152]{1,0:T(8,128)(2,1)} %get-tuple-element.139.g_ref, ...), custom_call_target="tpu_custom_call" | custom-call | flops 1000000 | bytes 100000 | tf_op jit(solution)/shard_map/feed_forward_fall/pallas_call | solution.py:526
  134.9 9.2 %middle.1 = (bf16[512,1152]{1,0:T(8,128)(2,1)}, f32[512,1152]{1,0:T(8,128)}, bf16[512,1152]{1,0:T(8,128)(2,1)}, f32[8,1152]{1,0:T(8,128)}) custom-call(s32[5]{0:T(128)} %stack.95.clock_ref.coord_ref, f32[512,1152]{1,0:T(8,128)} %get-tuple-element.141.gm_ref, f32[512,1152]{1,0:T(8,128)} %get-tuple-element.136.two_ref, ...), custom_call_target="tpu_custom_call" | custom-call | flops 1000000 | bytes 100000 | tf_op jit(solution)/shard_map/middle/pallas_call | solution.py:600
  144.7 1.6 constant_dynamic-update-slice_fusion.3
  146.3 5.8 %collective-permute-done.10 = bf16[512,1152]{1,0:T(8,128)(2,1)S(1)} collective-permute-done((bf16[512,1152]{1,0:T(8,128)(2,1)}, bf16[512,1152]{1,0:T(8,128)(2,1)S(1)}, u32[]{:S(2)}, u32[]{:S(2)}) %collective-permute-start.10) | collective-permute-done | bytes 1179680 | tf_op jit(solution)/shard_map/ppermute | solution.py:847
  153.7 3.2 convolution_convert_fusion
  156.9 2.6 copy.44
  159.5 4.4 %convolution_convert_fusion.1 = bf16[576,1024]{1,0:T(8,128)(2,1)} fusion(bf16[1024,1152]{1,0:T(8,128)(2,1)} %copy-done.31, bf16[1152,1152]{1,0:T(8,128)(2,1)S(1)} %copy-done, s32[]{:T(128)S(6)} %select_n.244), kind=kOutput, calls=%fused_computation.8 | convolution fusion | flops 1359544320 | bytes 4866052 | tf_op jit(solution)/shard_map/dot_general | solution.py:30
  163.9 5.8 %sum_pieces.10 = (bf16[1,2,2,2,72,1152]{5,4,3,2,1,0:T(8,128)(2,1)}, bf16[1,2,2,2,72,1152]{5,4,3,2,1,0:T(8,128)(2,1)}, bf16[1,2,2,2,72,576]{5,4,3,2,1,0:T(8,128)(2,1)}) custom-call(s32[5]{0:T(128)} %stack.95.clock_ref.coord_ref, bf16[2,2,2,2,72,2304]{5,4,3,2,1,0:T(8,128)(2,1)} %bitcast.127, ...), custom_call_target="tpu_custom_call" | custom-call | flops 1000000 | bytes 100000 | tf_op jit(solution)/shard_map/sum_pieces/pallas_call | solution.py:733
  172.8 2.3 collective-permute-start.2
  177.0 8.3 %collective-permute-done.2 = bf16[4,2,4,1152]{3,2,1,0:T(4,128)(2,1)S(1)} collective-permute-done((bf16[4,2,4,1152]{3,2,1,0:T(4,128)(2,1)S(1)}, bf16[4,2,4,1152]{3,2,1,0:T(4,128)(2,1)S(1)}, u32[]{:S(2)}, u32[]{:S(2)}) %collective-permute-start.2) | collective-permute-done | bytes 73760 | tf_op jit(solution)/shard_map/ppermute | solution.py:783
  186.6 27.2 %attention_backward.1 = (bf16[3,8,72,1024]{3,2,1,0:T(8,128)(2,1)}, f32[8,64,64]{2,1,0:T(8,128)}, f32[2,8,16,72]{3,2,1,0:T(8,128)}) custom-call(s32[5]{0:T(128)} %stack.95.clock_ref.coord_ref, bf16[3,8,72,1024]{3,2,1,0:T(8,128)(2,1)} %get-tuple-element.127.p_ref.qkv_ref, bf16[8,72,1024]{2,1,0:T(8,128)(2,1)} %copy-done.10, bf16[8,72,1024]{2,1,0:T(8,128)(2,1)} %bitcast.146, ...), custom_call_target="tpu_custom_call" | custom-call | flops 1000000 | bytes 100000 | tf_op jit(solution)/shard_map/attention_backward/pallas_call | solution.py:400
  216.0 4.0 sum_pieces.11
  221.4 5.2 %collective-permute-done.9 = bf16[256,1152]{1,0:T(8,128)(2,1)S(1)} collective-permute-done((bf16[256,1152]{1,0:T(8,128)(2,1)S(1)}, bf16[256,1152]{1,0:T(8,128)(2,1)S(1)}, u32[]{:S(2)}, u32[]{:S(2)}) %collective-permute-start.9) | collective-permute-done | bytes 589856 | tf_op jit(solution)/shard_map/ppermute | solution.py:844
  228.3 10.0 %project_weights.1 = bf16[3,1152,576]{2,1,0:T(8,128)(2,1)} custom-call(s32[5]{0:T(128)} %stack.95.clock_ref.coord_ref, bf16[1024,1152]{1,0:T(8,128)(2,1)} %get-tuple-element.161.in_ref, bf16[3,8,72,1024]{3,2,1,0:T(8,128)(2,1)} %get-tuple-element.156.d_ref), custom_call_target="tpu_custom_call" | custom-call | flops 1000000 | bytes 100000 | tf_op jit(solution)/shard_map/project_weights/pallas_call | solution.py:206
  238.3 4.6 %sum_pieces.12 = (bf16[1,2,2,2,72,576]{5,4,3,2,1,0:T(8,128)(2,1)}, bf16[1,2,2,2,72,576]{5,4,3,2,1,0:T(8,128)(2,1)}, bf16[1,2,2,2,72,576]{5,4,3,2,1,0:T(8,128)(2,1)}) custom-call(s32[5]{0:T(128)} %stack.95.clock_ref.coord_ref, bf16[3,2,2,2,2,72,576]{6,5,4,3,2,1,0:T(8,128)(2,1)} %bitcast.112, bf16[3,2,2,2,2,72,576]{6,5,4,3,2,1,0:T(8,128)(2,1)} %bitcast.113, ...), custom_call_target="tpu_custom_call" | custom-call | flops 1000000 | bytes 100000 | tf_op jit(solution)/shard_map/sum_pieces/pallas_call | solution.py:733
  245.0 5.3 %collective-permute-done.14.refs_3_ = bf16[1,2,2,72,1152]{4,3,2,1,0:T(8,128)(2,1)S(1)} collective-permute-done((bf16[1,2,2,72,1152]{4,3,2,1,0:T(8,128)(2,1)}, bf16[1,2,2,72,1152]{4,3,2,1,0:T(8,128)(2,1)S(1)}, u32[]{:S(2)}, u32[]{:S(2)}) %collective-permute-start.14) | collective-permute-done | bytes 663584 | tf_op jit(solution)/shard_map/ppermute | solution.py:844
  253.0 13.6 %project_back.1 = (f32[512,1152]{1,0:T(8,128)}, bf16[512,1152]{1,0:T(8,128)(2,1)}) custom-call(s32[5]{0:T(128)} %stack.95.clock_ref.coord_ref, s32[1]{0:T(128)} %bitcast.4.core_ref, bf16[3,8,72,1024]{3,2,1,0:T(8,128)(2,1)} %get-tuple-element.156.d_ref, bf16[1152,3456]{1,0:T(8,128)(2,1)} %w_ref.3), custom_call_target="tpu_custom_call" | custom-call | flops 1000000 | bytes 100000 | tf_op jit(solution)/shard_map/project_back/pallas_call | solution.py:266
  267.5 3.7 sum_pieces.13
  271.2 14.3 %reduce-scatter.2.cloned.1.call-done = bf16[144,1152]{1,0:T(8,128)(2,1)} async-done(((bf16[4608,1152]{1,0:T(8,128)(2,1)}), bf16[144,1152]{1,0:T(8,128)(2,1)}) %reduce-scatter.2.cloned.1.call-update) | async-done | bytes 331792 | tf_op jit(solution)/shard_map/reduce_scatter | solution.py:950
  290.8 3.6 sum_pieces.14
  298.7 5.8 %last.1 = (bf16[512,1152]{1,0:T(8,128)(2,1)}, f32[8,1152]{1,0:T(8,128)}) custom-call(f32[512,1152]{1,0:T(8,128)} %get-tuple-element.167.back_ref, bf16[512,1152]{1,0:T(8,128)(2,1)} %collective-permute-done.16.far_ref, bf16[512,1152]{1,0:T(8,128)(2,1)} %get-tuple-element.134.x_ref, f32[512,1152]{1,0:T(8,128)} %get-tuple-element.174.grad_ref, ...), custom_call_target="tpu_custom_call" | custom-call | flops 1000000 | bytes 100000 | tf_op jit(solution)/shard_map/last/pallas_call | solution.py:639
  304.5 2.2 collective-permute-done.21.refs_2_
  306.7 6.4 %collective-permute-done.22.refs_5_.refs_6_.refs_7_ = bf16[1,2,2,72,576]{4,3,2,1,0:T(8,128)(2,1)S(1)} collective-permute-done((bf16[1,2,2,72,576]{4,3,2,1,0:T(8,128)(2,1)}, bf16[1,2,2,72,576]{4,3,2,1,0:T(8,128)(2,1)S(1)}, u32[]{:S(2)}, u32[]{:S(2)}) %collective-permute-start.22) | collective-permute-done | bytes 331808 | tf_op jit(solution)/shard_map/ppermute | solution.py:748
  314.8 3.4 sum_pieces.15
  319.7 3.3 sum_pieces.16
  331.1 4.2 collective-permute-done.27.refs_3_
  335.2 5.2 %collective-permute-done.29.refs_11_.refs_15_.refs_13_.refs_18_ = bf16[2,2,72,576]{3,2,1,0:T(8,128)(2,1)S(1)} collective-permute-done((bf16[2,2,72,576]{3,2,1,0:T(8,128)(2,1)S(1)}, bf16[2,2,72,576]{3,2,1,0:T(8,128)(2,1)S(1)}, u32[]{:S(2)}, u32[]{:S(2)}) %collective-permute-start.29) | collective-permute-done | bytes 331808 | tf_op jit(solution)/shard_map/ppermute | solution.py:844
  341.2 3.0 sum_pieces.17
  345.9 3.3 sum_pieces.18
  351.6 1.8 collective-permute-start.37
  355.7 3.2 collective-permute-done.37
  359.7 8.0 %collective-permute-done.35.refs_4_.refs_9_.refs_14_.refs_19_ = bf16[4,72,576]{2,1,0:T(8,128)(2,1)S(1)} collective-permute-done((bf16[4,72,576]{2,1,0:T(8,128)(2,1)S(1)}, bf16[4,72,576]{2,1,0:T(8,128)(2,1)S(1)}, u32[]{:S(2)}, u32[]{:S(2)}) %collective-permute-start.35) | collective-permute-done | bytes 331808 | tf_op jit(solution)/shard_map/ppermute | solution.py:748
  368.4 3.2 sum_pieces.19
  372.7 1.6 collective-permute-start.36
  377.7 5.4 %collective-permute-done.43 = bf16[4,2,8,1152]{3,2,1,0:T(8,128)(2,1)S(1)} collective-permute-done((bf16[4,2,8,1152]{3,2,1,0:T(8,128)(2,1)}, bf16[4,2,8,1152]{3,2,1,0:T(8,128)(2,1)S(1)}, u32[]{:S(2)}, u32[]{:S(2)}) %collective-permute-start.43) | collective-permute-done | bytes 147488 | tf_op jit(solution)/shard_map/ppermute | solution.py:783
  389.6 1.7 pad_maximum_fusion
  396.8 3.2 collective-permute-done.41
  407.2 4.0 concatenate.104
  (273 shorter events, 94.3 us)
Async XLA Ops:
  7.2 278.3 %reduce-scatter.2.cloned.1.call-start = ((), (), s32[]{:S(2)}) async-start(), calls=%async_computation.1 | async-start | bytes 10948608 | tf_op jit(solution)/shard_map/reduce_scatter | solution.py:950
  11.5 15.5 %collective-permute-start = (bf16[1,2,4,1152]{3,2,1,0:T(4,128)(2,1)}, bf16[1,2,4,1152]{3,2,1,0:T(4,128)(2,1)S(1)}, u32[]{:S(2)}, u32[]{:S(2)}) collective-permute-start(bf16[1,2,4,1152]{3,2,1,0:T(4,128)(2,1)} %bitcast.149), channel_id=1, source_target_pairs={{0,4},{4,0},{8,12},{12,8},{16,20},{20,16},{24,28},{28,24},{1,5},{5... | collective-permute-start | bytes 55304 | tf_op jit(solution)/shard_map/ppermute | solution.py:783
  16.6 15.1 %collective-permute-start.3 = (bf16[256,1152]{1,0:T(8,128)(2,1)}, bf16[256,1152]{1,0:T(8,128)(2,1)}, u32[]{:S(2)}, u32[]{:S(2)}) collective-permute-start(bf16[256,1152]{1,0:T(8,128)(2,1)} %get-tuple-element.247), channel_id=1, source_target_pairs={{0,2},{1,3},{2,0},{3,1},{4,6},{5,7},{6,4},{7,5},{8,10},{9,11},{10,... | collective-permute-start | bytes 1769480 | tf_op jit(solution)/shard_map/ppermute | solution.py:844
  18.1 16.4 %collective-permute-start.4 = (bf16[256,1152]{1,0:T(8,128)(2,1)S(1)}, bf16[256,1152]{1,0:T(8,128)(2,1)}, u32[]{:S(2)}, u32[]{:S(2)}) collective-permute-start(bf16[256,1152]{1,0:T(8,128)(2,1)S(1)} %get-tuple-element.248.a_ref), channel_id=1, source_target_pairs={{0,1},{1,0},{2,3},{3,2},{4,5},{5,4},{6,7},{7,6},{8,9},{9,8},{10,11... | collective-permute-start | bytes 1769480 | tf_op jit(solution)/shard_map/ppermute | solution.py:847
  27.0 4.0 collective-permute-start.1
  31.7 2.8 collective-permute-start.5
  31.7 26.2 %collective-permute-start.6 = (bf16[256,1152]{1,0:T(8,128)(2,1)}, bf16[256,1152]{1,0:T(8,128)(2,1)}, u32[]{:S(2)}, u32[]{:S(2)}) collective-permute-start(bf16[256,1152]{1,0:T(8,128)(2,1)} %get-tuple-element.130), channel_id=1, source_target_pairs={{0,2},{1,3},{2,0},{3,1},{4,6},{5,7},{6,4},{7,5},{8,10},{9,11},{10,... | collective-permute-start | bytes 1769480 | tf_op jit(solution)/shard_map/ppermute | solution.py:844
  57.7 12.0 %collective-permute-start.7 = (bf16[4,72,1024]{2,1,0:T(8,128)(2,1)}, bf16[4,72,1024]{2,1,0:T(8,128)(2,1)S(1)}, u32[]{:S(2)}, u32[]{:S(2)}) collective-permute-start(bf16[4,72,1024]{2,1,0:T(8,128)(2,1)} %get-tuple-element.129), channel_id=1, source_target_pairs={{0,1},{1,0},{2,3},{3,2},{4,5},{5,4},{6,7},{7,6},{8,9},{9,8},{10,11... | collective-permute-start | bytes 1769480 | tf_op jit(solution)/shard_map/ppermute | solution.py:847
  67.2 2.6 collective-permute-start.8
  144.1 19.8 %collective-permute-start.11 = (bf16[1152,2304]{1,0:T(8,128)(2,1)}, bf16[1152,2304]{1,0:T(8,128)(2,1)}, u32[]{:S(2)}, u32[]{:S(2)}) collective-permute-start(bf16[1152,2304]{1,0:T(8,128)(2,1)} %get-tuple-element.149), channel_id=1, source_target_pairs={{0,1},{1,0},{2,3},{3,2},{4,5},{5,4},{6,7},{7,6},{8,9},{9,8},{10,11... | collective-permute-start | bytes 15925256 | tf_op jit(solution)/shard_map/ppermute | solution.py:847
  144.4 7.7 %collective-permute-start.10 = (bf16[512,1152]{1,0:T(8,128)(2,1)}, bf16[512,1152]{1,0:T(8,128)(2,1)S(1)}, u32[]{:S(2)}, u32[]{:S(2)}) collective-permute-start(bf16[512,1152]{1,0:T(8,128)(2,1)} %get-tuple-element.145), channel_id=1, source_target_pairs={{0,1},{1,0},{2,3},{3,2},{4,5},{5,4},{6,7},{7,6},{8,9},{9,8},{10,11... | collective-permute-start | bytes 3538952 | tf_op jit(solution)/shard_map/ppermute | solution.py:847
  169.7 44.2 %collective-permute-start.12 = (bf16[1,2,2,2,72,1152]{5,4,3,2,1,0:T(8,128)(2,1)}, bf16[1,2,2,2,72,1152]{5,4,3,2,1,0:T(8,128)(2,1)S(1)}, u32[]{:S(2)}, u32[]{:S(2)}) collective-permute-start(bf16[1,2,2,2,72,1152]{5,4,3,2,1,0:T(8,128)(2,1)} %get-tuple-element.150), channel_id=1, source_target_pairs={{0,4},{4,0},{8,12},{12,8},{16,20},{20,16},{24,28},{28,24},{1,5},{5... | collective-permute-start | bytes 3981320 | tf_op jit(solution)/shard_map/ppermute | solution.py:748
  170.8 43.1 %collective-permute-start.13 = (bf16[1,2,2,2,72,1152]{5,4,3,2,1,0:T(8,128)(2,1)}, bf16[1,2,2,2,72,1152]{5,4,3,2,1,0:T(8,128)(2,1)S(1)}, u32[]{:S(2)}, u32[]{:S(2)}) collective-permute-start(bf16[1,2,2,2,72,1152]{5,4,3,2,1,0:T(8,128)(2,1)} %get-tuple-element.151), channel_id=1, source_target_pairs={{0,2},{1,3},{2,0},{3,1},{4,6},{5,7},{6,4},{7,5},{8,10},{9,11},{10,... | collective-permute-start | bytes 3981320 | tf_op jit(solution)/shard_map/ppermute | solution.py:844
  172.8 12.4 %collective-permute-start.2 = (bf16[4,2,4,1152]{3,2,1,0:T(4,128)(2,1)S(1)}, bf16[4,2,4,1152]{3,2,1,0:T(4,128)(2,1)S(1)}, u32[]{:S(2)}, u32[]{:S(2)}) collective-permute-start(bf16[4,2,4,1152]{3,2,1,0:T(4,128)(2,1)S(1)} %pad_maximum_fusion.10), channel_id=1, source_target_pairs={{0,16},{4,20},{8,24},{12,28},{16,0},{20,4},{24,8},{28,12},{1,17},{... | collective-permute-start | bytes 221192 | tf_op jit(solution)/shard_map/ppermute | solution.py:783
  176.3 50.3 %collective-permute-start.9 = (bf16[256,1152]{1,0:T(8,128)(2,1)S(1)}, bf16[256,1152]{1,0:T(8,128)(2,1)S(1)}, u32[]{:S(2)}, u32[]{:S(2)}) collective-permute-start(bf16[256,1152]{1,0:T(8,128)(2,1)S(1)} %slice.158), channel_id=1, source_target_pairs={{0,2},{1,3},{2,0},{3,1},{4,6},{5,7},{6,4},{7,5},{8,10},{9,11},{10,... | collective-permute-start | bytes 1769480 | tf_op jit(solution)/shard_map/ppermute | solution.py:844
  220.0 30.4 %collective-permute-start.14 = (bf16[1,2,2,72,1152]{4,3,2,1,0:T(8,128)(2,1)}, bf16[1,2,2,72,1152]{4,3,2,1,0:T(8,128)(2,1)S(1)}, u32[]{:S(2)}, u32[]{:S(2)}) collective-permute-start(bf16[1,2,2,72,1152]{4,3,2,1,0:T(8,128)(2,1)} %get-tuple-element.158), channel_id=1, source_target_pairs={{0,2},{1,3},{2,0},{3,1},{4,6},{5,7},{6,4},{7,5},{8,10},{9,11},{10,... | collective-permute-start | bytes 1990664 | tf_op jit(solution)/shard_map/ppermute | solution.py:844
  220.0 46.6 %collective-permute-start.15 = (bf16[1,2,2,72,1152]{4,3,2,1,0:T(8,128)(2,1)}, bf16[1,2,2,72,1152]{4,3,2,1,0:T(8,128)(2,1)S(1)}, u32[]{:S(2)}, u32[]{:S(2)}) collective-permute-start(bf16[1,2,2,72,1152]{4,3,2,1,0:T(8,128)(2,1)} %get-tuple-element.159), channel_id=1, source_target_pairs={{0,4},{4,0},{8,12},{12,8},{16,20},{20,16},{24,28},{28,24},{1,5},{5... | collective-permute-start | bytes 1990664 | tf_op jit(solution)/shard_map/ppermute | solution.py:748
  226.7 60.8 %collective-permute-start.20 = (bf16[1,2,2,2,72,576]{5,4,3,2,1,0:T(8,128)(2,1)}, bf16[1,2,2,2,72,576]{5,4,3,2,1,0:T(8,128)(2,1)S(1)}, u32[]{:S(2)}, u32[]{:S(2)}) collective-permute-start(bf16[1,2,2,2,72,576]{5,4,3,2,1,0:T(8,128)(2,1)} %get-tuple-element.152), channel_id=1, source_target_pairs={{0,8},{4,12},{8,0},{12,4},{16,24},{20,28},{24,16},{28,20},{1,9},{5... | collective-permute-start | bytes 1990664 | tf_op jit(solution)/shard_map/ppermute | solution.py:748
  243.0 45.2 %collective-permute-start.17 = (bf16[1,2,2,2,72,576]{5,4,3,2,1,0:T(8,128)(2,1)}, bf16[1,2,2,2,72,576]{5,4,3,2,1,0:T(8,128)(2,1)S(1)}, u32[]{:S(2)}, u32[]{:S(2)}) collective-permute-start(bf16[1,2,2,2,72,576]{5,4,3,2,1,0:T(8,128)(2,1)} %get-tuple-element.163), channel_id=1, source_target_pairs={{0,4},{4,0},{8,12},{12,8},{16,20},{20,16},{24,28},{28,24},{1,5},{5... | collective-permute-start | bytes 1990664 | tf_op jit(solution)/shard_map/ppermute | solution.py:748
  244.3 44.7 %collective-permute-start.18 = (bf16[1,2,2,2,72,576]{5,4,3,2,1,0:T(8,128)(2,1)}, bf16[1,2,2,2,72,576]{5,4,3,2,1,0:T(8,128)(2,1)S(1)}, u32[]{:S(2)}, u32[]{:S(2)}) collective-permute-start(bf16[1,2,2,2,72,576]{5,4,3,2,1,0:T(8,128)(2,1)} %get-tuple-element.164), channel_id=1, source_target_pairs={{0,2},{1,3},{2,0},{3,1},{4,6},{5,7},{6,4},{7,5},{8,10},{9,11},{10,... | collective-permute-start | bytes 1990664 | tf_op jit(solution)/shard_map/ppermute | solution.py:844
  250.3 38.7 %collective-permute-start.19 = (bf16[1,2,2,2,72,576]{5,4,3,2,1,0:T(8,128)(2,1)}, bf16[1,2,2,2,72,576]{5,4,3,2,1,0:T(8,128)(2,1)S(1)}, u32[]{:S(2)}, u32[]{:S(2)}) collective-permute-start(bf16[1,2,2,2,72,576]{5,4,3,2,1,0:T(8,128)(2,1)} %get-tuple-element.165), channel_id=1, source_target_pairs={{0,8},{4,12},{8,0},{12,4},{16,24},{20,28},{24,16},{28,20},{1,9},{5... | collective-permute-start | bytes 1990664 | tf_op jit(solution)/shard_map/ppermute | solution.py:748
  285.5 13.2 %collective-permute-start.16 = (bf16[512,1152]{1,0:T(8,128)(2,1)}, bf16[512,1152]{1,0:T(8,128)(2,1)}, u32[]{:S(2)}, u32[]{:S(2)}) collective-permute-start(bf16[512,1152]{1,0:T(8,128)(2,1)} %get-tuple-element.173), channel_id=1, source_target_pairs={{0,1},{1,0},{2,3},{3,2},{4,5},{5,4},{6,7},{7,6},{8,9},{9,8},{10,11... | collective-permute-start | bytes 3538952 | tf_op jit(solution)/shard_map/ppermute | solution.py:847
  287.6 10.2 %collective-permute-start.24 = (bf16[1,1,8,576]{3,2,1,0:T(8,128)(2,1)S(1)}, bf16[1,1,8,576]{3,2,1,0:T(8,128)(2,1)S(1)}, u32[]{:S(2)}, u32[]{:S(2)}) collective-permute-start(bf16[1,1,8,576]{3,2,1,0:T(8,128)(2,1)S(1)} %convert_element_type.61), channel_id=1, source_target_pairs={{0,1},{1,0},{2,3},{3,2},{4,5},{5,4},{6,7},{7,6},{8,9},{9,8},{10,11... | collective-permute-start | bytes 27656 | tf_op jit(solution)/shard_map/ppermute | solution.py:847
  288.2 31.6 %collective-permute-start.25 = (bf16[2,2,72,1152]{3,2,1,0:T(8,128)(2,1)}, bf16[2,2,72,1152]{3,2,1,0:T(8,128)(2,1)}, u32[]{:S(2)}, u32[]{:S(2)}) collective-permute-start(bf16[2,2,72,1152]{3,2,1,0:T(8,128)(2,1)} %sum_pieces.13), channel_id=1, source_target_pairs={{0,8},{4,12},{8,0},{12,4},{16,24},{20,28},{24,16},{28,20},{1,9},{5... | collective-permute-start | bytes 1990664 | tf_op jit(solution)/shard_map/ppermute | solution.py:748
  294.4 18.8 %collective-permute-start.23 = (bf16[2,2,2,72,576]{4,3,2,1,0:T(8,128)(2,1)}, bf16[2,2,2,72,576]{4,3,2,1,0:T(8,128)(2,1)S(1)}, u32[]{:S(2)}, u32[]{:S(2)}) collective-permute-start(bf16[2,2,2,72,576]{4,3,2,1,0:T(8,128)(2,1)} %get-tuple-element.178), channel_id=1, source_target_pairs={{0,4},{4,0},{8,12},{12,8},{16,20},{20,16},{24,28},{28,24},{1,5},{5... | collective-permute-start | bytes 1990664 | tf_op jit(solution)/shard_map/ppermute | solution.py:748
  296.4 10.3 %collective-permute-start.21 = (bf16[1,2,2,72,576]{4,3,2,1,0:T(8,128)(2,1)}, bf16[1,2,2,72,576]{4,3,2,1,0:T(8,128)(2,1)S(1)}, u32[]{:S(2)}, u32[]{:S(2)}) collective-permute-start(bf16[1,2,2,72,576]{4,3,2,1,0:T(8,128)(2,1)} %get-tuple-element.176), channel_id=1, source_target_pairs={{0,2},{1,3},{2,0},{3,1},{4,6},{5,7},{6,4},{7,5},{8,10},{9,11},{10,... | collective-permute-start | bytes 995336 | tf_op jit(solution)/shard_map/ppermute | solution.py:844
  297.8 15.4 %collective-permute-start.22 = (bf16[1,2,2,72,576]{4,3,2,1,0:T(8,128)(2,1)}, bf16[1,2,2,72,576]{4,3,2,1,0:T(8,128)(2,1)S(1)}, u32[]{:S(2)}, u32[]{:S(2)}) collective-permute-start(bf16[1,2,2,72,576]{4,3,2,1,0:T(8,128)(2,1)} %get-tuple-element.177), channel_id=1, source_target_pairs={{0,8},{4,12},{8,0},{12,4},{16,24},{20,28},{24,16},{28,20},{1,9},{5... | collective-permute-start | bytes 995336 | tf_op jit(solution)/shard_map/ppermute | solution.py:748
  318.2 5.6 %collective-permute-start.26 = (bf16[1,1,8,1152]{3,2,1,0:T(8,128)(2,1)S(1)}, bf16[1,1,8,1152]{3,2,1,0:T(8,128)(2,1)S(1)}, u32[]{:S(2)}, u32[]{:S(2)}) collective-permute-start(bf16[1,1,8,1152]{3,2,1,0:T(8,128)(2,1)S(1)} %pad_maximum_fusion.16), channel_id=1, source_target_pairs={{0,2},{1,3},{2,0},{3,1},{4,6},{5,7},{6,4},{7,5},{8,10},{9,11},{10,... | collective-permute-start | bytes 55304 | tf_op jit(solution)/shard_map/ppermute | solution.py:844
  323.7 5.2 %collective-permute-start.31 = (f32[4324]{0:T(1024)S(1)}, f32[4324]{0:T(1024)S(1)}, u32[]{:S(2)}, u32[]{:S(2)}) collective-permute-start(f32[4324]{0:T(1024)S(1)} %concatenate.97), channel_id=1, source_target_pairs={{0,1},{1,0},{2,3},{3,2},{4,5},{5,4},{6,7},{7,6},{8,9},{9,8},{10,11... | collective-permute-start | bytes 51896 | tf_op jit(solution)/shard_map/ppermute | solution.py:847
  323.8 6.3 %collective-permute-start.33 = (bf16[1,2,8,1152]{3,2,1,0:T(8,128)(2,1)S(1)}, bf16[1,2,8,1152]{3,2,1,0:T(8,128)(2,1)S(1)}, u32[]{:S(2)}, u32[]{:S(2)}) collective-permute-start(bf16[1,2,8,1152]{3,2,1,0:T(8,128)(2,1)S(1)} %pad_maximum_fusion.13), channel_id=1, source_target_pairs={{0,4},{4,0},{8,12},{12,8},{16,20},{20,16},{24,28},{28,24},{1,5},{5... | collective-permute-start | bytes 110600 | tf_op jit(solution)/shard_map/ppermute | solution.py:783
  325.6 9.6 %collective-permute-start.27 = (bf16[1,2,72,576]{3,2,1,0:T(8,128)(2,1)S(1)}, bf16[1,2,72,576]{3,2,1,0:T(8,128)(2,1)S(1)}, u32[]{:S(2)}, u32[]{:S(2)}) collective-permute-start(bf16[1,2,72,576]{3,2,1,0:T(8,128)(2,1)S(1)} %copy-done.43), channel_id=1, source_target_pairs={{0,8},{4,12},{8,0},{12,4},{16,24},{20,28},{24,16},{28,20},{1,9},{5... | collective-permute-start | bytes 497672 | tf_op jit(solution)/shard_map/ppermute | solution.py:748
  326.9 8.4 %collective-permute-start.28 = (bf16[1,2,72,576]{3,2,1,0:T(8,128)(2,1)S(1)}, bf16[1,2,72,576]{3,2,1,0:T(8,128)(2,1)S(1)}, u32[]{:S(2)}, u32[]{:S(2)}) collective-permute-start(bf16[1,2,72,576]{3,2,1,0:T(8,128)(2,1)S(1)} %copy-done.42), channel_id=1, source_target_pairs={{0,4},{4,0},{8,12},{12,8},{16,20},{20,16},{24,28},{28,24},{1,5},{5... | collective-permute-start | bytes 497672 | tf_op jit(solution)/shard_map/ppermute | solution.py:748
  327.5 17.6 %collective-permute-start.34 = (bf16[2,72,1152]{2,1,0:T(8,128)(2,1)}, bf16[2,72,1152]{2,1,0:T(8,128)(2,1)S(1)}, u32[]{:S(2)}, u32[]{:S(2)}) collective-permute-start(bf16[2,72,1152]{2,1,0:T(8,128)(2,1)} %sum_pieces.16), channel_id=1, source_target_pairs={{0,16},{4,20},{8,24},{12,28},{16,0},{20,4},{24,8},{28,12},{1,17},{... | collective-permute-start | bytes 995336 | tf_op jit(solution)/shard_map/ppermute | solution.py:748
  328.9 11.5 %collective-permute-start.29 = (bf16[2,2,72,576]{3,2,1,0:T(8,128)(2,1)S(1)}, bf16[2,2,72,576]{3,2,1,0:T(8,128)(2,1)S(1)}, u32[]{:S(2)}, u32[]{:S(2)}) collective-permute-start(bf16[2,2,72,576]{3,2,1,0:T(8,128)(2,1)S(1)} %copy-done.41), channel_id=1, source_target_pairs={{0,2},{1,3},{2,0},{3,1},{4,6},{5,7},{6,4},{7,5},{8,10},{9,11},{10,... | collective-permute-start | bytes 995336 | tf_op jit(solution)/shard_map/ppermute | solution.py:844
  330.1 41.5 %collective-permute-start.38 = (bf16[144,1152]{1,0:T(8,128)(2,1)S(1)}, bf16[144,1152]{1,0:T(8,128)(2,1)S(1)}, u32[]{:S(2)}, u32[]{:S(2)}) collective-permute-start(bf16[144,1152]{1,0:T(8,128)(2,1)S(1)} %copy-done.26), channel_id=1, source_target_pairs={{0,2},{1,3},{2,0},{3,1},{4,6},{5,7},{6,4},{7,5},{8,10},{9,11},{10,... | collective-permute-start | bytes 995336 | tf_op jit(solution)/shard_map/ppermute | solution.py:844
  350.2 17.5 %collective-permute-start.35 = (bf16[4,72,576]{2,1,0:T(8,128)(2,1)S(1)}, bf16[4,72,576]{2,1,0:T(8,128)(2,1)S(1)}, u32[]{:S(2)}, u32[]{:S(2)}) collective-permute-start(bf16[4,72,576]{2,1,0:T(8,128)(2,1)S(1)} %copy-done.32), channel_id=1, source_target_pairs={{0,16},{4,20},{8,24},{12,28},{16,0},{20,4},{24,8},{28,12},{1,17},{... | collective-permute-start | bytes 995336 | tf_op jit(solution)/shard_map/ppermute | solution.py:748
  350.9 4.1 collective-permute-start.32
  351.6 7.4 %collective-permute-start.37 = (bf16[2,2,8,1152]{3,2,1,0:T(8,128)(2,1)S(1)}, bf16[2,2,8,1152]{3,2,1,0:T(8,128)(2,1)S(1)}, u32[]{:S(2)}, u32[]{:S(2)}) collective-permute-start(bf16[2,2,8,1152]{3,2,1,0:T(8,128)(2,1)S(1)} %pad_maximum_fusion.11), channel_id=1, source_target_pairs={{0,8},{4,12},{8,0},{12,4},{16,24},{20,28},{24,16},{28,20},{1,9},{5... | collective-permute-start | bytes 221192 | tf_op jit(solution)/shard_map/ppermute | solution.py:783
  353.5 19.2 %collective-permute-start.45 = (bf16[72,2304]{1,0:T(8,128)(2,1)S(1)}, bf16[72,2304]{1,0:T(8,128)(2,1)S(1)}, u32[]{:S(2)}, u32[]{:S(2)}) collective-permute-start(bf16[72,2304]{1,0:T(8,128)(2,1)S(1)} %constant_dynamic-update-slice_fusion.4), channel_id=1, source_target_pairs={{0,2},{1,3},{2,0},{3,1},{4,6},{5,7},{6,4},{7,5},{8,10},{9,11},{10,... | collective-permute-start | bytes 995336 | tf_op jit(solution)/shard_map/ppermute | solution.py:844
  355.0 30.6 %collective-permute-start.30 = (bf16[256,1152]{1,0:T(8,128)(2,1)S(1)}, bf16[256,1152]{1,0:T(8,128)(2,1)}, u32[]{:S(2)}, u32[]{:S(2)}) collective-permute-start(bf16[256,1152]{1,0:T(8,128)(2,1)S(1)} %slice.161), channel_id=1, source_target_pairs={{0,2},{1,3},{2,0},{3,1},{4,6},{5,7},{6,4},{7,5},{8,10},{9,11},{10,... | collective-permute-start | bytes 1769480 | tf_op jit(solution)/shard_map/ppermute | solution.py:844
  372.7 4.5 %collective-permute-start.36 = (f32[4324]{0:T(1024)S(1)}, f32[4324]{0:T(1024)S(1)}, u32[]{:S(2)}, u32[]{:S(2)}) collective-permute-start(f32[4324]{0:T(1024)S(1)} %add.127), channel_id=1, source_target_pairs={{0,4},{4,0},{8,12},{12,8},{16,20},{20,16},{24,28},{28,24},{1,5},{5... | collective-permute-start | bytes 51896 | tf_op jit(solution)/shard_map/ppermute | solution.py:801
  374.4 8.8 %collective-permute-start.43 = (bf16[4,2,8,1152]{3,2,1,0:T(8,128)(2,1)}, bf16[4,2,8,1152]{3,2,1,0:T(8,128)(2,1)S(1)}, u32[]{:S(2)}, u32[]{:S(2)}) collective-permute-start(bf16[4,2,8,1152]{3,2,1,0:T(8,128)(2,1)} %pad_maximum_fusion.9), channel_id=1, source_target_pairs={{0,16},{4,20},{8,24},{12,28},{16,0},{20,4},{24,8},{28,12},{1,17},{... | collective-permute-start | bytes 442376 | tf_op jit(solution)/shard_map/ppermute | solution.py:783
  374.5 16.8 %collective-permute-start.42 = (bf16[72,2304]{1,0:T(8,128)(2,1)S(1)}, bf16[72,2304]{1,0:T(8,128)(2,1)S(1)}, u32[]{:S(2)}, u32[]{:S(2)}) collective-permute-start(bf16[72,2304]{1,0:T(8,128)(2,1)S(1)} %concatenate.101), channel_id=1, source_target_pairs={{0,2},{1,3},{2,0},{3,1},{4,6},{5,7},{6,4},{7,5},{8,10},{9,11},{10,... | collective-permute-start | bytes 995336 | tf_op jit(solution)/shard_map/ppermute | solution.py:844
  376.3 11.8 %collective-permute-start.39 = (bf16[2,144,1152]{2,1,0:T(8,128)(2,1)}, bf16[2,144,1152]{2,1,0:T(8,128)(2,1)}, u32[]{:S(2)}, u32[]{:S(2)}) collective-permute-start(bf16[2,144,1152]{2,1,0:T(8,128)(2,1)} %maximum_select_fusion), channel_id=1, source_target_pairs={{0,1},{1,0},{2,3},{3,2},{4,5},{5,4},{6,7},{7,6},{8,9},{9,8},{10,11... | collective-permute-start | bytes 1990664 | tf_op jit(solution)/shard_map/ppermute | solution.py:847
  377.2 14.1 %collective-permute-start.46 = (bf16[144,2304]{1,0:T(8,128)(2,1)}, bf16[144,2304]{1,0:T(8,128)(2,1)}, u32[]{:S(2)}, u32[]{:S(2)}) collective-permute-start(bf16[144,2304]{1,0:T(8,128)(2,1)} %pad_maximum_fusion.5), channel_id=1, source_target_pairs={{0,1},{1,0},{2,3},{3,2},{4,5},{5,4},{6,7},{7,6},{8,9},{9,8},{10,11... | collective-permute-start | bytes 1990664 | tf_op jit(solution)/shard_map/ppermute | solution.py:847
  391.4 3.8 collective-permute-start.40
  392.4 11.5 %collective-permute-start.44 = (bf16[144,2304]{1,0:T(8,128)(2,1)}, bf16[144,2304]{1,0:T(8,128)(2,1)S(1)}, u32[]{:S(2)}, u32[]{:S(2)}) collective-permute-start(bf16[144,2304]{1,0:T(8,128)(2,1)} %pad_maximum_fusion.3), channel_id=1, source_target_pairs={{0,1},{1,0},{2,3},{3,2},{4,5},{5,4},{6,7},{7,6},{8,9},{9,8},{10,11... | collective-permute-start | bytes 1990664 | tf_op jit(solution)/shard_map/ppermute | solution.py:847
  395.2 4.7 %collective-permute-start.41 = (f32[4324]{0:T(1024)S(1)}, f32[4324]{0:T(1024)S(1)}, u32[]{:S(2)}, u32[]{:S(2)}) collective-permute-start(f32[4324]{0:T(1024)S(1)} %add.129), channel_id=1, source_target_pairs={{0,16},{4,20},{8,24},{12,28},{16,0},{20,4},{24,8},{28,12},{1,17},{... | collective-permute-start | bytes 51896 | tf_op jit(solution)/shard_map/ppermute | solution.py:801
  (44 other events, 322.8 us)
Sparse Core Ops, SparseCore 0:
  105.3 180.1 reduce-scatter.1
where the time goes:
time: 423 us; the launch traced here: 418 us
  Pallas kernels  195 us (46%)
  waiting for transfers between devices  80.3 us (19%)
  local copies, waits for them, and re-layouts  44.7 us (11%)
  starting transfers between devices  43.3 us (10%)
  other arithmetic  20.3 us (5%)
  matrix products  19.1 us (5%)
  between operations  15.7 us (4%)
    pallas_call x10, Pallas kernels, advance(): pl.pallas_call(functools.partial(sum_kernel, counts=counts, places=places...  37.7 us
    pallas_call x1, Pallas kernels, mlp_fall(): pl.pallas_call(fall_kernel, grid_spec=pltpu.PrefetchScalarGridSpec(num_sc...  29.7 us
    pallas_call x1, Pallas kernels, mlp_rise(): pl.pallas_call(rise_kernel, grid=(ff // tile,), in_specs=[pl.BlockSpec((r...  27.5 us
    pallas_call x1, Pallas kernels, attend_backward(): pl.pallas_call(functools.partial(backward_kernel, scale=scale), grid_spec...  27.2 us
    ppermute x12, waiting for transfers between devices, advance(): total = swaps[key[0]](total)  19.6 us
    ppermute x14, waiting for transfers between devices, swap_y(): return lax.ppermute(a, 'seq', over_y)  18.6 us
    pallas_call x2, Pallas kernels, attend_forward(): pl.pallas_call(forward_kernel, grid_spec=pltpu.PrefetchScalarGridSpec(num...  18.5 us
    ppermute x6, waiting for transfers between devices, tick(): self.far = swap(self.clock.tie(self.part))  17.5 us
  transfers between devices with their start and end apart: 48, of which 17 were waited for; matrix products, arithmetic and copies ran while one was open for 13% of the time, Pallas kernels for 40%

commit v1 on v0

--- a/solution.py
+++ b/solution.py
@@ -770,13 +770,16 @@
     def __init__(self, clock, part, swaps):
         self.clock, self.part, self.swaps, self.far = clock, part, list(swaps), None
 
-    def tick(self):
+    def land(self):
         if self.far is not None:
             bit, axis = self.put
             low, high = jnp.where(bit, self.far, self.part), jnp.where(bit, self.part, self.far)
             self.part = jnp.concatenate([low, high], axis=axis)
             self.clock.passed(self.part)
             self.far = None
+
+    def tick(self):
+        self.land()
         if self.swaps:
             swap, bit, axis = self.swaps.pop(0)
             self.put = (bit, axis)
@@ -905,11 +908,6 @@
 
     img_bits = [((me_img >> k) & 1) == 1 for k in range(bits)]
     clock = Clock(coords)
-    times_all = Gather(
-        clock,
-        lax.optimization_barrier((time_embed, feats))[0][None],
-        [(swaps[k], img_bits[k], 0) for k in range(bits)],
-    ).finish()
     clock.passed(feats, times, tables, core, pair, grad_out, grad_own, ln1_row, ln2_row)
     tok_rx = clock.tie(tok_rx)
     grad_rx = swap_y(lax.optimization_barrier((grad_out, tok_rx))[0])
@@ -918,9 +916,14 @@
         scale, own_heads,
     )
     clock.passed(qkv)
+    times_all = Gather(
+        clock, time_embed[None], [(swaps[k], img_bits[k], 0) for k in range(bits)]
+    )
+    times_all.tick()
     half_heads = own_heads // 2
     o_a, lse_a = attend_forward(clock.now, qkv, tables, feats, 0, half_heads)
     clock.passed(o_a, grad_rx)
+    times_all.tick()
     far_a = swap_core(o_a)
     o_b, lse_b = attend_forward(clock.now, qkv, tables, feats, half_heads, half_heads)
     far_b = swap_core(o_b)
@@ -940,7 +943,8 @@
     )
     branch_one = dot(attn_all[:, :mine], output_projection_weight, 0, 0)
     hidden_one = x.astype(F32) + branch_one
-    mlp_in = (moments(hidden_one)[0] * ln2_gain).astype(BF)
+    times_all.tick()
+    mlp_in = clock.tie((moments(hidden_one)[0] * ln2_gain).astype(BF))
 
     tile = ff // 6
     two, slope, down, mlp_in_t, grad_branch = mlp_rise(
@@ -964,8 +968,9 @@
         clock.now, gm, two, branch_one, hidden_one, grad_branch, valid, ln2_row
     )
     clock.passed(output)
-    far_up = swap_core(clock.tie(send))
-    gb_all = jnp.concatenate([gb_mine, swap_core(gb_mine)], axis=0)
+    gb_far = swap_core(gb_mine)
+    far_up = swap_core(lax.optimization_barrier((send, gb_far))[0])
+    gb_all = jnp.concatenate([gb_mine, gb_far], axis=0)
     out_far = swap_y(output[span:])
     w_proj_rows = lax.dynamic_slice_in_dim(output_projection_weight, c * cols, cols, 0)
     do = dot(w_proj_rows, gb_all, 1, 1).astype(BF).reshape(own_heads, width, 2 * mine)
@@ -988,9 +993,10 @@
     up_half = ff // 4
     jobs_up = [
         by_row(dims, (own, far_up), up_half, k)
-        for k, dims in enumerate([order(0, on_y, 1), order(on_y, 0, 1)])
+        for k, dims in enumerate([order(0, 1, on_y), order(on_y, 0, 1)])
     ]
     job_proj = by_row(orders[2], (proj_part,), cols)
+    clock.passed(out_far)
     step(jobs_up + [job_proj])
     grads = attend_backward(
         clock.now, qkv, o_own, do, lse, tables, feats, scale, 0, own_heads, ()
@@ -1007,16 +1013,19 @@
     )
     gather.tick()
     w_part = project_weights(clock.now, attn_in, d)
-    clock.passed(w_part, out_far)
+    clock.passed(w_part, job_proj.arrived[0][0])
+    gather.land()
+    times_all = times_all.finish()
     jobs_qkv = [by_row(dims, (w_part,), cols, prefix=(p,)) for p, dims in enumerate(orders)]
     step(jobs_qkv)
     jobs_qkv.append(job_proj)
     back, back_far = project_back(clock.now, core, d, w_qkv, mine)
     clock.passed(back)
     step(jobs_up)
-    clock.passed(down)
     back_far = swap_core(clock.tie(back_far))
     step(jobs_qkv)
+    clock.passed(down)
+    down_far = swap_y(clock.tie(down))
     input_grad, sums_one = last(back, back_far, x, grad_one, ln1_row)
     clock.passed(input_grad)
     reach = jnp.arange(2 * SIDE - 1, dtype=jnp.int32)
@@ -1036,43 +1045,43 @@
 
     small = Total(clock, small, [swap_core, swap_y] + [swaps[k] for k in range(bits)])
 
+    small.tick()
     step(jobs_qkv)
     gather.tick()
+    down = jnp.where(y == 0, jnp.stack([down, down_far]), jnp.stack([down_far, down]))
     output = returned(output[:span], out_far)
+    in_far = swap_y(clock.tie(input_grad)[span:])
     clock.passed(output)
     step(jobs_up)
     small.tick()
     gather.tick()
-    down = clock.tie(down)
+    down_far = swap_core(down)
     step(jobs_qkv)
-    in_far = swap_y(clock.tie(input_grad)[span:])
-    down_far = swap_y(down)
     small.tick()
     gather.tick()
+    h0, h1 = both_cores(down, down_far)
+    w_down_grad = jnp.concatenate([h0[0], h1[0], h0[1], h1[1]], axis=0)
+    clock.passed(w_down_grad)
     finish(jobs_up)
     up_parts, up_far = across_y([clock.tie(job.result) for job in jobs_up])
     finish(jobs_qkv)
     qkv_parts, qkv_far = across_y([job.result for job in jobs_qkv])
-    down, down_far = clock.tie(down), clock.tie(down_far)
-    down = jnp.where(y == 0, jnp.stack([down, down_far]), jnp.stack([down_far, down]))
-    down_far = swap_core(down)
     small.tick()
     gather.tick()
+    clock.passed(qkv_far, up_far)
+    qkv_part, qkv_far = across_core(qkv_parts, clock.tie(qkv_far))
     up_part, up_far = across_core(up_parts, clock.tie(up_far))
-    h0, h1 = both_cores(down, down_far)
-    w_down_grad = jnp.concatenate([h0[0], h1[0], h0[1], h1[1]], axis=0)
-    clock.passed(w_down_grad)
+    clock.passed(in_far)
+    in_far = clock.tie(in_far)
     small.tick()
     gather.tick()
-    qkv_part, qkv_far = across_core(qkv_parts, clock.tie(qkv_far))
-    u0, u1 = both_cores(up_part, clock.tie(up_far))
+    u0, u1 = both_cores(up_part, up_far)
     w_up_grad = jnp.concatenate(
         [u[:, k * tile : (k + 1) * tile] for k in range(3) for u in (u0, u1)], axis=1
     )
     clock.passed(w_up_grad)
     small = small.finish()
     factors = gather.finish().reshape(n_img * slots, 8, dm)
-    in_far = clock.tie(in_far)
 
     te_rows = lax.dynamic_slice_in_dim(times_all, me_img * rows, rows, 3)
     w_time_q_grad, w_time_v_grad = (

time: 423 us -> 384 us (0.908)
  waiting for transfers between devices: 80.3 us -> 48.5 us
    reduce_scatter x1, waiting for transfers between devices: 14.3 us -> 0.01 us  [per_device(): lax.psum_scatter(down, ('img', 'seq'), scatter_dimension=0, tiled=True)]
    ppermute x6, waiting for transfers between devices: 17.5 us -> 10.1 us  [tick(): self.far = swap(self.clock.tie(self.part))]
    ppermute x12 -> x13, waiting for transfers between devices: 19.6 us -> 12.3 us  [advance(): total = swaps[key[0]](total)]
    ppermute x14, starting transfers between devices: 13.6 us -> 18.1 us  [swap_y(): return lax.ppermute(a, 'seq', over_y)]
    unnamed x96 -> x118, local copies, waits for them, and re-layouts: 13.8 us -> 12.6 us
    ppermute x12 -> x13, starting transfers between devices: 14 us -> 15.2 us  [advance(): total = swaps[key[0]](total)]
  transfers between devices with their start and end apart: 48 -> 49, of which waited for: 17 -> 15; matrix products, arithmetic and copies ran while one was open for 13% -> 13% of each run, Pallas kernels for 40% -> 43%
where the time goes in v1:
time: 384 us; the launch traced here: 380 us
  Pallas kernels  194 us (51%)
  waiting for transfers between devices  48.5 us (13%)
  starting transfers between devices  43.8 us (11%)
  local copies, waits for them, and re-layouts  41.7 us (11%)
  matrix products  18.9 us (5%)
  other arithmetic  16.3 us (4%)
  between operations  15.9 us (4%)
    pallas_call x10, Pallas kernels, advance(): pl.pallas_call(functools.partial(sum_kernel, counts=counts, places=places...  37.3 us
    pallas_call x1, Pallas kernels, mlp_fall(): pl.pallas_call(fall_kernel, grid_spec=pltpu.PrefetchScalarGridSpec(num_sc...  29.7 us
    pallas_call x1, Pallas kernels, mlp_rise(): pl.pallas_call(rise_kernel, grid=(ff // tile,), in_specs=[pl.BlockSpec((r...  27.4 us
    pallas_call x1, Pallas kernels, attend_backward(): pl.pallas_call(functools.partial(backward_kernel, scale=scale), grid_spec...  27.2 us
    pallas_call x2, Pallas kernels, attend_forward(): pl.pallas_call(forward_kernel, grid_spec=pltpu.PrefetchScalarGridSpec(num...  18.5 us
    ppermute x14, starting transfers between devices, swap_y(): return lax.ppermute(a, 'seq', over_y)  18.1 us
    ppermute x14, waiting for transfers between devices, swap_y(): return lax.ppermute(a, 'seq', over_y)  16.9 us
    ppermute x13, starting transfers between devices, advance(): total = swaps[key[0]](total)  15.2 us
  transfers between devices with their start and end apart: 49, of which 15 were waited for; matrix products, arithmetic and copies ran while one was open for 13% of the time, Pallas kernels for 43%

profile of v1, /device:TPU:0, one launch (start us, length us, event | category | flops | bytes accessed | tf_op | source)
XLA Modules:
  0.0 379.6 jit_solution(996058553147919941)
XLA Ops:
  7.3 2.3 dynamic-slice_bitcast_fusion
  9.6 3.0 collective-permute-start
  13.8 2.2 fusion.25
  24.0 2.3 dynamic-slice_bitcast_fusion.2
  29.2 14.0 %project.1 = (bf16[1024,1152]{1,0:T(8,128)(2,1)}, bf16[512,1152]{1,0:T(8,128)(2,1)}, bf16[3,8,72,1024]{3,2,1,0:T(8,128)(2,1)}) custom-call(s32[1]{0:T(128)} %bitcast.4.core_ref, bf16[256,1152]{1,0:T(8,128)(2,1)} %copy-done.21, bf16[256,1152]{1,0:T(8,128)(2,1)} %collective-permute-done.b_ref, bf16[256,1152]{1,0:T(8,128)(2,1)} %collective-permute-done.1.c_ref, ...), custom_call_target="tpu_custom_call" | custom-call | flops 1000000 | bytes 100000 | tf_op jit(solution)/shard_map/project/pallas_call | solution.py:164
  44.8 9.2 %attention_forward.2 = (bf16[4,72,1024]{2,1,0:T(8,128)(2,1)}, f32[4,1,1024]{2,1,0:T(1,128)}) custom-call(s32[5]{0:T(128)} %stack.95.clock_ref.coord_ref, bf16[3,8,72,1024]{3,2,1,0:T(8,128)(2,1)} %get-tuple-element.120.p_ref.qkv_ref, bf16[8,64,64]{2,1,0:T(8,128)(2,1)} %fusion.20.table_ref, bf16[112,1024]{1,0:T(8,128)(2,1)} %get-tuple-element.117.feat_ref), custom_call_target="tpu_custom_call" | custom-call | flops 1000000 | bytes 100000 | tf_op jit(solution)/shard_map/attention_forward/pallas_call | solution.py:323
  55.2 9.3 %attention_forward.3 = (bf16[4,72,1024]{2,1,0:T(8,128)(2,1)}, f32[4,1,1024]{2,1,0:T(1,128)}) custom-call(s32[5]{0:T(128)} %stack.95.clock_ref.coord_ref, bf16[3,8,72,1024]{3,2,1,0:T(8,128)(2,1)} %get-tuple-element.120.p_ref.qkv_ref, bf16[8,64,64]{2,1,0:T(8,128)(2,1)} %fusion.20.table_ref, bf16[112,1024]{1,0:T(8,128)(2,1)} %get-tuple-element.117.feat_ref), custom_call_target="tpu_custom_call" | custom-call | flops 1000000 | bytes 100000 | tf_op jit(solution)/shard_map/attention_forward/pallas_call | solution.py:323
  69.9 3.4 fusion.42
  75.1 27.4 %feed_forward_rise.1 = (f32[512,1152]{1,0:T(8,128)}, bf16[512,4608]{1,0:T(8,128)(2,1)}, bf16[4608,1152]{1,0:T(8,128)(2,1)}, bf16[1152,512]{1,0:T(8,128)(2,1)}, bf16[512,1152]{1,0:T(8,128)(2,1)}) custom-call(bf16[512,1152]{1,0:T(8,128)(2,1)} %multiply_convert_fusion.m_ref, bf16[256,1152]{1,0:T(8,128)(2,1)} %get-tuple-element.249.near_ref, ...), custom_call_target="tpu_custom_call" | custom-call | flops 1000000 | bytes 100000 | tf_op jit(solution)/shard_map/feed_forward_rise/pallas_call | solution.py:468
  102.6 29.7 %feed_forward_fall.1 = (f32[512,1152]{1,0:T(8,128)}, bf16[1152,2304]{1,0:T(8,128)(2,1)}, bf16[1152,2304]{1,0:T(8,128)(2,1)}) custom-call(s32[5]{0:T(128)} %stack.95.clock_ref.coord_ref, s32[2]{0:T(128)} %pad_add_fusion.1.tile_ref, bf16[1152,512]{1,0:T(8,128)(2,1)} %get-tuple-element.136.mt_ref, bf16[512,1152]{1,0:T(8,128)(2,1)} %get-tuple-element.137.g_ref, ...), custom_call_target="tpu_custom_call" | custom-call | flops 1000000 | bytes 100000 | tf_op jit(solution)/shard_map/feed_forward_fall/pallas_call | solution.py:526
  132.3 9.2 %middle.1 = (bf16[512,1152]{1,0:T(8,128)(2,1)}, f32[512,1152]{1,0:T(8,128)}, bf16[512,1152]{1,0:T(8,128)(2,1)}, f32[8,1152]{1,0:T(8,128)}) custom-call(s32[5]{0:T(128)} %stack.95.clock_ref.coord_ref, f32[512,1152]{1,0:T(8,128)} %get-tuple-element.139.gm_ref, f32[512,1152]{1,0:T(8,128)} %get-tuple-element.134.two_ref, ...), custom_call_target="tpu_custom_call" | custom-call | flops 1000000 | bytes 100000 | tf_op jit(solution)/shard_map/middle/pallas_call | solution.py:600
  141.6 3.0 collective-permute-done.9
  149.6 3.3 convolution_convert_fusion
  152.8 2.6 copy.44
  155.4 4.4 %convolution_convert_fusion.1 = bf16[576,1024]{1,0:T(8,128)(2,1)} fusion(bf16[1024,1152]{1,0:T(8,128)(2,1)} %copy-done.35, bf16[1152,1152]{1,0:T(8,128)(2,1)S(1)} %copy-done, s32[]{:T(128)S(6)} %select_n.235), kind=kOutput, calls=%fused_computation.8 | convolution fusion | flops 1359544320 | bytes 4866052 | tf_op jit(solution)/shard_map/dot_general | solution.py:30
  159.8 2.7 collective-permute-done.8
  162.5 5.7 %sum_pieces.10 = (bf16[1,2,2,2,72,1152]{5,4,3,2,1,0:T(8,128)(2,1)}, bf16[1,2,2,2,72,1152]{5,4,3,2,1,0:T(8,128)(2,1)}, bf16[1,2,2,2,72,576]{5,4,3,2,1,0:T(8,128)(2,1)}) custom-call(s32[5]{0:T(128)} %stack.95.clock_ref.coord_ref, bf16[2,2,2,2,72,2304]{5,4,3,2,1,0:T(8,128)(2,1)} %bitcast.127, ...), custom_call_target="tpu_custom_call" | custom-call | flops 1000000 | bytes 100000 | tf_op jit(solution)/shard_map/sum_pieces/pallas_call | solution.py:733
  171.4 2.6 collective-permute-start.15
  176.3 5.2 %collective-permute-done.15 = bf16[4,2,4,1152]{3,2,1,0:T(4,128)(2,1)S(1)} collective-permute-done((bf16[4,2,4,1152]{3,2,1,0:T(4,128)(2,1)S(1)}, bf16[4,2,4,1152]{3,2,1,0:T(4,128)(2,1)S(1)}, u32[]{:S(2)}, u32[]{:S(2)}) %collective-permute-start.15) | collective-permute-done | bytes 73760 | tf_op jit(solution)/shard_map/ppermute | solution.py:786
  182.3 27.2 %attention_backward.1 = (bf16[3,8,72,1024]{3,2,1,0:T(8,128)(2,1)}, f32[8,64,64]{2,1,0:T(8,128)}, f32[2,8,16,72]{3,2,1,0:T(8,128)}) custom-call(s32[5]{0:T(128)} %stack.95.clock_ref.coord_ref, bf16[3,8,72,1024]{3,2,1,0:T(8,128)(2,1)} %get-tuple-element.120.p_ref.qkv_ref, bf16[8,72,1024]{2,1,0:T(8,128)(2,1)} %copy-done.10, bf16[8,72,1024]{2,1,0:T(8,128)(2,1)} %bitcast.146, ...), custom_call_target="tpu_custom_call" | custom-call | flops 1000000 | bytes 100000 | tf_op jit(solution)/shard_map/attention_backward/pallas_call | solution.py:400
  211.6 3.9 %sum_pieces.11 = (bf16[1,2,2,72,1152]{4,3,2,1,0:T(8,128)(2,1)}, bf16[1,2,2,72,1152]{4,3,2,1,0:T(8,128)(2,1)}) custom-call(s32[5]{0:T(128)} %stack.95.clock_ref.coord_ref, bf16[2,2,2,2,72,2304]{5,4,3,2,1,0:T(8,128)(2,1)} %bitcast.129, bf16[2,2,2,2,72,2304]{5,4,3,2,1,0:T(8,128)(2,1)} %bitcast.31.refs_1_.refs_3_.refs_4_.refs_5_.refs_6_.refs_7_, ...), custom_call_target="tpu_custom_call" | custom-call | flops 1000000 | bytes 100000 | tf_op jit(solution)/shard_map/sum_pieces/pallas_call | solution.py:733
  218.6 10.0 %project_weights.1 = bf16[3,1152,576]{2,1,0:T(8,128)(2,1)} custom-call(s32[5]{0:T(128)} %stack.95.clock_ref.coord_ref, bf16[1024,1152]{1,0:T(8,128)(2,1)} %get-tuple-element.160.in_ref, bf16[3,8,72,1024]{3,2,1,0:T(8,128)(2,1)} %get-tuple-element.155.d_ref), custom_call_target="tpu_custom_call" | custom-call | flops 1000000 | bytes 100000 | tf_op jit(solution)/shard_map/project_weights/pallas_call | solution.py:206
  229.5 4.6 %sum_pieces.12 = (bf16[1,2,2,2,72,576]{5,4,3,2,1,0:T(8,128)(2,1)}, bf16[1,2,2,2,72,576]{5,4,3,2,1,0:T(8,128)(2,1)}, bf16[1,2,2,2,72,576]{5,4,3,2,1,0:T(8,128)(2,1)}) custom-call(s32[5]{0:T(128)} %stack.95.clock_ref.coord_ref, bf16[3,2,2,2,2,72,576]{6,5,4,3,2,1,0:T(8,128)(2,1)} %bitcast.112, bf16[3,2,2,2,2,72,576]{6,5,4,3,2,1,0:T(8,128)(2,1)} %bitcast.113, ...), custom_call_target="tpu_custom_call" | custom-call | flops 1000000 | bytes 100000 | tf_op jit(solution)/shard_map/sum_pieces/pallas_call | solution.py:733
  235.5 2.0 collective-permute-start.21
  237.5 13.7 %project_back.1 = (f32[512,1152]{1,0:T(8,128)}, bf16[512,1152]{1,0:T(8,128)(2,1)}) custom-call(s32[5]{0:T(128)} %stack.95.clock_ref.coord_ref, s32[1]{0:T(128)} %bitcast.4.core_ref, bf16[3,8,72,1024]{3,2,1,0:T(8,128)(2,1)} %get-tuple-element.155.d_ref, bf16[1152,3456]{1,0:T(8,128)(2,1)} %w_ref.3), custom_call_target="tpu_custom_call" | custom-call | flops 1000000 | bytes 100000 | tf_op jit(solution)/shard_map/project_back/pallas_call | solution.py:266
  251.2 3.6 sum_pieces.13
  256.4 8.4 %collective-permute-done.21.refs_5_.refs_7_.refs_9_.refs_11_ = bf16[1,2,2,2,72,576]{5,4,3,2,1,0:T(8,128)(2,1)S(1)} collective-permute-done((bf16[1,2,2,2,72,576]{5,4,3,2,1,0:T(8,128)(2,1)}, bf16[1,2,2,2,72,576]{5,4,3,2,1,0:T(8,128)(2,1)S(1)}, u32[]{:S(2)}, u32[]{:S(2)}) %collective-permute-start.21) | collective-permute-done | bytes 663584 | tf_op jit(solution)/shard_map/ppermute | solution.py:748
  265.6 3.6 sum_pieces.14
  271.3 2.0 collective-permute-start.27
  273.3 2.0 collective-permute-start.28
  275.3 5.8 %last.1 = (bf16[512,1152]{1,0:T(8,128)(2,1)}, f32[8,1152]{1,0:T(8,128)}) custom-call(f32[512,1152]{1,0:T(8,128)} %get-tuple-element.171.back_ref, bf16[512,1152]{1,0:T(8,128)(2,1)} %collective-permute-done.18.far_ref, bf16[512,1152]{1,0:T(8,128)(2,1)} %get-tuple-element.131.x_ref, f32[512,1152]{1,0:T(8,128)} %get-tuple-element.178.grad_ref, ...), custom_call_target="tpu_custom_call" | custom-call | flops 1000000 | bytes 100000 | tf_op jit(solution)/shard_map/last/pallas_call | solution.py:639
  282.8 3.8 %collective-permute-done.24.refs_8_.refs_11_.refs_10_.refs_14_.refs_12_.refs_17_ = bf16[2,2,2,72,576]{4,3,2,1,0:T(8,128)(2,1)S(1)} collective-permute-done((bf16[2,2,2,72,576]{4,3,2,1,0:T(8,128)(2,1)}, bf16[2,2,2,72,576]{4,3,2,1,0:T(8,128)(2,1)S(1)}, u32[]{:S(2)}, u32[]{:S(2)}) %collective-permute-start.24) | collective-permute-done | bytes 663584 | tf_op jit(solution)/shard_map/ppermute | solution.py:748
  287.5 3.3 sum_pieces.15
  293.6 3.1 sum_pieces.16
  296.7 2.1 collective-permute-start.29
  301.4 3.4 collective-permute-start.38
  304.8 2.1 collective-permute-start.33
  307.1 2.1 collective-permute-start.25
  309.1 7.3 %collective-permute-done.33.refs_11_.refs_15_.refs_13_.refs_18_ = bf16[2,2,72,576]{3,2,1,0:T(8,128)(2,1)S(1)} collective-permute-done((bf16[2,2,72,576]{3,2,1,0:T(8,128)(2,1)S(1)}, bf16[2,2,72,576]{3,2,1,0:T(8,128)(2,1)S(1)}, u32[]{:S(2)}, u32[]{:S(2)}) %collective-permute-start.33) | collective-permute-done | bytes 331808 | tf_op jit(solution)/shard_map/ppermute | solution.py:847
  317.2 3.0 sum_pieces.17
  321.1 2.4 collective-permute-done.36
  324.0 3.8 %collective-permute-done.43 = bf16[2,2,8,1152]{3,2,1,0:T(8,128)(2,1)S(1)} collective-permute-done((bf16[2,2,8,1152]{3,2,1,0:T(8,128)(2,1)S(1)}, bf16[2,2,8,1152]{3,2,1,0:T(8,128)(2,1)S(1)}, u32[]{:S(2)}, u32[]{:S(2)}) %collective-permute-start.43) | collective-permute-done | bytes 73760 | tf_op jit(solution)/shard_map/ppermute | solution.py:786
  327.9 3.9 %collective-permute-done.25 = bf16[256,1152]{1,0:T(8,128)(2,1)S(1)} collective-permute-done((bf16[256,1152]{1,0:T(8,128)(2,1)S(1)}, bf16[256,1152]{1,0:T(8,128)(2,1)S(1)}, u32[]{:S(2)}, u32[]{:S(2)}) %collective-permute-start.25) | collective-permute-done | bytes 589856 | tf_op jit(solution)/shard_map/ppermute | solution.py:847
  335.9 3.3 sum_pieces.18
  341.0 3.2 sum_pieces.19
  346.7 2.4 collective-permute-done.40
  351.7 2.1 collective-permute-done.41
  368.5 4.0 %concatenate.104 = f32[144,3456]{1,0:T(8,128)} concatenate(f32[144,576]{1,0:T(8,128)} %get-tuple-element.234, f32[144,576]{1,0:T(8,128)} %get-tuple-element.238, f32[144,576]{1,0:T(8,128)} %get-tuple-element.233, f32[144,576]{1,0:T(8,128)S(1)} %get-tuple-element.237, f32[144,576]{1,0:T(8,128)} %get-tuple-element.232, f32[144,576]{1,0:T(8,128)S(1)} %get-tuple-element.236), dimensions={1} | concatenate | bytes 3981312 | tf_op jit(solution)/shard_map/concatenate | solution.py:1102
  (297 shorter events, 80.3 us)
Async XLA Ops:
  7.2 275.5 %reduce-scatter.2.cloned.1.call-start = ((), (), s32[]{:S(2)}) async-start(), calls=%async_computation.1 | async-start | bytes 10948608 | tf_op jit(solution)/shard_map/reduce_scatter | solution.py:954
  9.6 16.7 %collective-permute-start = (bf16[256,1152]{1,0:T(8,128)(2,1)}, bf16[256,1152]{1,0:T(8,128)(2,1)}, u32[]{:S(2)}, u32[]{:S(2)}) collective-permute-start(bf16[256,1152]{1,0:T(8,128)(2,1)} %get-tuple-element.247), channel_id=1, source_target_pairs={{0,2},{1,3},{2,0},{3,1},{4,6},{5,7},{6,4},{7,5},{8,10},{9,11},{10,... | collective-permute-start | bytes 1769480 | tf_op jit(solution)/shard_map/ppermute | solution.py:847
  12.6 16.6 %collective-permute-start.1 = (bf16[256,1152]{1,0:T(8,128)(2,1)S(1)}, bf16[256,1152]{1,0:T(8,128)(2,1)}, u32[]{:S(2)}, u32[]{:S(2)}) collective-permute-start(bf16[256,1152]{1,0:T(8,128)(2,1)S(1)} %get-tuple-element.248.a_ref), channel_id=1, source_target_pairs={{0,1},{1,0},{2,3},{3,2},{4,5},{5,4},{6,7},{7,6},{8,9},{9,8},{10,11... | collective-permute-start | bytes 1769480 | tf_op jit(solution)/shard_map/ppermute | solution.py:850
  26.3 2.9 collective-permute-start.2
  26.8 28.3 %collective-permute-start.3 = (bf16[256,1152]{1,0:T(8,128)(2,1)}, bf16[256,1152]{1,0:T(8,128)(2,1)}, u32[]{:S(2)}, u32[]{:S(2)}) collective-permute-start(bf16[256,1152]{1,0:T(8,128)(2,1)} %get-tuple-element.123), channel_id=1, source_target_pairs={{0,2},{1,3},{2,0},{3,1},{4,6},{5,7},{6,4},{7,5},{8,10},{9,11},{10,... | collective-permute-start | bytes 1769480 | tf_op jit(solution)/shard_map/ppermute | solution.py:847
  43.2 11.9 %collective-permute-start.4 = (bf16[1,2,4,1152]{3,2,1,0:T(4,128)(2,1)S(1)}, bf16[1,2,4,1152]{3,2,1,0:T(4,128)(2,1)S(1)}, u32[]{:S(2)}, u32[]{:S(2)}) collective-permute-start(bf16[1,2,4,1152]{3,2,1,0:T(4,128)(2,1)S(1)} %bitcast.150), channel_id=1, source_target_pairs={{0,4},{4,0},{8,12},{12,8},{16,20},{20,16},{24,28},{28,24},{1,5},{5... | collective-permute-start | bytes 55304 | tf_op jit(solution)/shard_map/ppermute | solution.py:786
  54.0 14.5 %collective-permute-start.6 = (bf16[4,72,1024]{2,1,0:T(8,128)(2,1)}, bf16[4,72,1024]{2,1,0:T(8,128)(2,1)S(1)}, u32[]{:S(2)}, u32[]{:S(2)}) collective-permute-start(bf16[4,72,1024]{2,1,0:T(8,128)(2,1)} %get-tuple-element.122), channel_id=1, source_target_pairs={{0,1},{1,0},{2,3},{3,2},{4,5},{5,4},{6,7},{7,6},{8,9},{9,8},{10,11... | collective-permute-start | bytes 1769480 | tf_op jit(solution)/shard_map/ppermute | solution.py:850
  64.4 4.0 %collective-permute-start.5 = (bf16[2,2,4,1152]{3,2,1,0:T(4,128)(2,1)S(1)}, bf16[2,2,4,1152]{3,2,1,0:T(4,128)(2,1)S(1)}, u32[]{:S(2)}, u32[]{:S(2)}) collective-permute-start(bf16[2,2,4,1152]{3,2,1,0:T(4,128)(2,1)S(1)} %pad_maximum_fusion.12), channel_id=1, source_target_pairs={{0,8},{4,12},{8,0},{12,4},{16,24},{20,28},{24,16},{28,20},{1,9},{5... | collective-permute-start | bytes 110600 | tf_op jit(solution)/shard_map/ppermute | solution.py:786
  66.0 2.6 collective-permute-start.7
  141.5 3.1 collective-permute-start.9
  144.6 17.9 %collective-permute-start.10 = (bf16[1152,2304]{1,0:T(8,128)(2,1)}, bf16[1152,2304]{1,0:T(8,128)(2,1)}, u32[]{:S(2)}, u32[]{:S(2)}) collective-permute-start(bf16[1152,2304]{1,0:T(8,128)(2,1)} %get-tuple-element.148), channel_id=1, source_target_pairs={{0,1},{1,0},{2,3},{3,2},{4,5},{5,4},{6,7},{7,6},{8,9},{9,8},{10,11... | collective-permute-start | bytes 15925256 | tf_op jit(solution)/shard_map/ppermute | solution.py:850
  146.7 15.8 %collective-permute-start.8 = (bf16[256,1152]{1,0:T(8,128)(2,1)}, bf16[256,1152]{1,0:T(8,128)(2,1)S(1)}, u32[]{:S(2)}, u32[]{:S(2)}) collective-permute-start(bf16[256,1152]{1,0:T(8,128)(2,1)} %slice.158), channel_id=1, source_target_pairs={{0,2},{1,3},{2,0},{3,1},{4,6},{5,7},{6,4},{7,5},{8,10},{9,11},{10,... | collective-permute-start | bytes 1769480 | tf_op jit(solution)/shard_map/ppermute | solution.py:847
  168.3 41.2 %collective-permute-start.11 = (bf16[1,2,2,2,72,1152]{5,4,3,2,1,0:T(8,128)(2,1)}, bf16[1,2,2,2,72,1152]{5,4,3,2,1,0:T(8,128)(2,1)S(1)}, u32[]{:S(2)}, u32[]{:S(2)}) collective-permute-start(bf16[1,2,2,2,72,1152]{5,4,3,2,1,0:T(8,128)(2,1)} %get-tuple-element.149), channel_id=1, source_target_pairs={{0,4},{4,0},{8,12},{12,8},{16,20},{20,16},{24,28},{28,24},{1,5},{5... | collective-permute-start | bytes 3981320 | tf_op jit(solution)/shard_map/ppermute | solution.py:748
  168.9 40.6 %collective-permute-start.12 = (bf16[1,2,2,2,72,1152]{5,4,3,2,1,0:T(8,128)(2,1)}, bf16[1,2,2,2,72,1152]{5,4,3,2,1,0:T(8,128)(2,1)S(1)}, u32[]{:S(2)}, u32[]{:S(2)}) collective-permute-start(bf16[1,2,2,2,72,1152]{5,4,3,2,1,0:T(8,128)(2,1)} %get-tuple-element.150), channel_id=1, source_target_pairs={{0,2},{1,3},{2,0},{3,1},{4,6},{5,7},{6,4},{7,5},{8,10},{9,11},{10,... | collective-permute-start | bytes 3981320 | tf_op jit(solution)/shard_map/ppermute | solution.py:847
  171.4 10.1 %collective-permute-start.15 = (bf16[4,2,4,1152]{3,2,1,0:T(4,128)(2,1)S(1)}, bf16[4,2,4,1152]{3,2,1,0:T(4,128)(2,1)S(1)}, u32[]{:S(2)}, u32[]{:S(2)}) collective-permute-start(bf16[4,2,4,1152]{3,2,1,0:T(4,128)(2,1)S(1)} %pad_maximum_fusion.10), channel_id=1, source_target_pairs={{0,16},{4,20},{8,24},{12,28},{16,0},{20,4},{24,8},{28,12},{1,17},{... | collective-permute-start | bytes 221192 | tf_op jit(solution)/shard_map/ppermute | solution.py:786
  174.6 54.0 %collective-permute-start.13 = (bf16[1,2,2,2,72,576]{5,4,3,2,1,0:T(8,128)(2,1)}, bf16[1,2,2,2,72,576]{5,4,3,2,1,0:T(8,128)(2,1)S(1)}, u32[]{:S(2)}, u32[]{:S(2)}) collective-permute-start(bf16[1,2,2,2,72,576]{5,4,3,2,1,0:T(8,128)(2,1)} %get-tuple-element.151), channel_id=1, source_target_pairs={{0,8},{4,12},{8,0},{12,4},{16,24},{20,28},{24,16},{28,20},{1,9},{5... | collective-permute-start | bytes 1990664 | tf_op jit(solution)/shard_map/ppermute | solution.py:748
  215.6 35.6 %collective-permute-start.16 = (bf16[1,2,2,72,1152]{4,3,2,1,0:T(8,128)(2,1)}, bf16[1,2,2,72,1152]{4,3,2,1,0:T(8,128)(2,1)}, u32[]{:S(2)}, u32[]{:S(2)}) collective-permute-start(bf16[1,2,2,72,1152]{4,3,2,1,0:T(8,128)(2,1)} %get-tuple-element.157), channel_id=1, source_target_pairs={{0,8},{4,12},{8,0},{12,4},{16,24},{20,28},{24,16},{28,20},{1,9},{5... | collective-permute-start | bytes 1990664 | tf_op jit(solution)/shard_map/ppermute | solution.py:748
  215.8 35.4 %collective-permute-start.17 = (bf16[1,2,2,72,1152]{4,3,2,1,0:T(8,128)(2,1)}, bf16[1,2,2,72,1152]{4,3,2,1,0:T(8,128)(2,1)}, u32[]{:S(2)}, u32[]{:S(2)}) collective-permute-start(bf16[1,2,2,72,1152]{4,3,2,1,0:T(8,128)(2,1)} %get-tuple-element.158), channel_id=1, source_target_pairs={{0,4},{4,0},{8,12},{12,8},{16,20},{20,16},{24,28},{28,24},{1,5},{5... | collective-permute-start | bytes 1990664 | tf_op jit(solution)/shard_map/ppermute | solution.py:748
  218.4 10.2 %collective-permute-start.14 = (bf16[1,1,8,576]{3,2,1,0:T(8,128)(2,1)S(1)}, bf16[1,1,8,576]{3,2,1,0:T(8,128)(2,1)S(1)}, u32[]{:S(2)}, u32[]{:S(2)}) collective-permute-start(bf16[1,1,8,576]{3,2,1,0:T(8,128)(2,1)S(1)} %convert_element_type.61), channel_id=1, source_target_pairs={{0,1},{1,0},{2,3},{3,2},{4,5},{5,4},{6,7},{7,6},{8,9},{9,8},{10,11... | collective-permute-start | bytes 27656 | tf_op jit(solution)/shard_map/ppermute | solution.py:850
  234.1 22.3 %collective-permute-start.19 = (bf16[1,2,2,2,72,576]{5,4,3,2,1,0:T(8,128)(2,1)}, bf16[1,2,2,2,72,576]{5,4,3,2,1,0:T(8,128)(2,1)S(1)}, u32[]{:S(2)}, u32[]{:S(2)}) collective-permute-start(bf16[1,2,2,2,72,576]{5,4,3,2,1,0:T(8,128)(2,1)} %get-tuple-element.167), channel_id=1, source_target_pairs={{0,4},{4,0},{8,12},{12,8},{16,20},{20,16},{24,28},{28,24},{1,5},{5... | collective-permute-start | bytes 1990664 | tf_op jit(solution)/shard_map/ppermute | solution.py:748
  234.5 21.9 %collective-permute-start.20 = (bf16[1,2,2,2,72,576]{5,4,3,2,1,0:T(8,128)(2,1)}, bf16[1,2,2,2,72,576]{5,4,3,2,1,0:T(8,128)(2,1)S(1)}, u32[]{:S(2)}, u32[]{:S(2)}) collective-permute-start(bf16[1,2,2,2,72,576]{5,4,3,2,1,0:T(8,128)(2,1)} %get-tuple-element.168), channel_id=1, source_target_pairs={{0,2},{1,3},{2,0},{3,1},{4,6},{5,7},{6,4},{7,5},{8,10},{9,11},{10,... | collective-permute-start | bytes 1990664 | tf_op jit(solution)/shard_map/ppermute | solution.py:847
  235.5 29.3 %collective-permute-start.21 = (bf16[1,2,2,2,72,576]{5,4,3,2,1,0:T(8,128)(2,1)}, bf16[1,2,2,2,72,576]{5,4,3,2,1,0:T(8,128)(2,1)S(1)}, u32[]{:S(2)}, u32[]{:S(2)}) collective-permute-start(bf16[1,2,2,2,72,576]{5,4,3,2,1,0:T(8,128)(2,1)} %get-tuple-element.169), channel_id=1, source_target_pairs={{0,8},{4,12},{8,0},{12,4},{16,24},{20,28},{24,16},{28,20},{1,9},{5... | collective-permute-start | bytes 1990664 | tf_op jit(solution)/shard_map/ppermute | solution.py:748
  254.8 18.5 %collective-permute-start.18 = (bf16[512,1152]{1,0:T(8,128)(2,1)}, bf16[512,1152]{1,0:T(8,128)(2,1)}, u32[]{:S(2)}, u32[]{:S(2)}) collective-permute-start(bf16[512,1152]{1,0:T(8,128)(2,1)} %get-tuple-element.177), channel_id=1, source_target_pairs={{0,1},{1,0},{2,3},{3,2},{4,5},{5,4},{6,7},{7,6},{8,9},{9,8},{10,11... | collective-permute-start | bytes 3538952 | tf_op jit(solution)/shard_map/ppermute | solution.py:850
  269.2 17.4 %collective-permute-start.24 = (bf16[2,2,2,72,576]{4,3,2,1,0:T(8,128)(2,1)}, bf16[2,2,2,72,576]{4,3,2,1,0:T(8,128)(2,1)S(1)}, u32[]{:S(2)}, u32[]{:S(2)}) collective-permute-start(bf16[2,2,2,72,576]{4,3,2,1,0:T(8,128)(2,1)} %get-tuple-element.182), channel_id=1, source_target_pairs={{0,4},{4,0},{8,12},{12,8},{16,20},{20,16},{24,28},{28,24},{1,5},{5... | collective-permute-start | bytes 1990664 | tf_op jit(solution)/shard_map/ppermute | solution.py:748
  270.5 12.2 %collective-permute-start.22 = (bf16[1,2,2,72,576]{4,3,2,1,0:T(8,128)(2,1)}, bf16[1,2,2,72,576]{4,3,2,1,0:T(8,128)(2,1)S(1)}, u32[]{:S(2)}, u32[]{:S(2)}) collective-permute-start(bf16[1,2,2,72,576]{4,3,2,1,0:T(8,128)(2,1)} %get-tuple-element.180), channel_id=1, source_target_pairs={{0,2},{1,3},{2,0},{3,1},{4,6},{5,7},{6,4},{7,5},{8,10},{9,11},{10,... | collective-permute-start | bytes 995336 | tf_op jit(solution)/shard_map/ppermute | solution.py:847
  270.5 12.3 %collective-permute-start.23 = (bf16[1,2,2,72,576]{4,3,2,1,0:T(8,128)(2,1)}, bf16[1,2,2,72,576]{4,3,2,1,0:T(8,128)(2,1)S(1)}, u32[]{:S(2)}, u32[]{:S(2)}) collective-permute-start(bf16[1,2,2,72,576]{4,3,2,1,0:T(8,128)(2,1)} %get-tuple-element.181), channel_id=1, source_target_pairs={{0,8},{4,12},{8,0},{12,4},{16,24},{20,28},{24,16},{28,20},{1,9},{5... | collective-permute-start | bytes 995336 | tf_op jit(solution)/shard_map/ppermute | solution.py:748
  271.3 20.8 %collective-permute-start.27 = (bf16[1,2,72,1152]{3,2,1,0:T(8,128)(2,1)}, bf16[1,2,72,1152]{3,2,1,0:T(8,128)(2,1)S(1)}, u32[]{:S(2)}, u32[]{:S(2)}) collective-permute-start(bf16[1,2,72,1152]{3,2,1,0:T(8,128)(2,1)} %get-tuple-element.174), channel_id=1, source_target_pairs={{0,2},{1,3},{2,0},{3,1},{4,6},{5,7},{6,4},{7,5},{8,10},{9,11},{10,... | collective-permute-start | bytes 995336 | tf_op jit(solution)/shard_map/ppermute | solution.py:847
  273.3 18.8 %collective-permute-start.28 = (bf16[1,2,72,1152]{3,2,1,0:T(8,128)(2,1)}, bf16[1,2,72,1152]{3,2,1,0:T(8,128)(2,1)S(1)}, u32[]{:S(2)}, u32[]{:S(2)}) collective-permute-start(bf16[1,2,72,1152]{3,2,1,0:T(8,128)(2,1)} %get-tuple-element.175), channel_id=1, source_target_pairs={{0,8},{4,12},{8,0},{12,4},{16,24},{20,28},{24,16},{28,20},{1,9},{5... | collective-permute-start | bytes 995336 | tf_op jit(solution)/shard_map/ppermute | solution.py:748
  282.7 14.0 %collective-permute-start.26 = (f32[4324]{0:T(1024)S(1)}, f32[4324]{0:T(1024)S(1)}, u32[]{:S(2)}, u32[]{:S(2)}) collective-permute-start(f32[4324]{0:T(1024)S(1)} %concatenate.96), channel_id=1, source_target_pairs={{0,1},{1,0},{2,3},{3,2},{4,5},{5,4},{6,7},{7,6},{8,9},{9,8},{10,11... | collective-permute-start | bytes 51896 | tf_op jit(solution)/shard_map/ppermute | solution.py:850
  290.9 7.9 %collective-permute-start.30 = (bf16[1,1,8,1152]{3,2,1,0:T(8,128)(2,1)S(1)}, bf16[1,1,8,1152]{3,2,1,0:T(8,128)(2,1)S(1)}, u32[]{:S(2)}, u32[]{:S(2)}) collective-permute-start(bf16[1,1,8,1152]{3,2,1,0:T(8,128)(2,1)S(1)} %copy-done.45), channel_id=1, source_target_pairs={{0,2},{1,3},{2,0},{3,1},{4,6},{5,7},{6,4},{7,5},{8,10},{9,11},{10,... | collective-permute-start | bytes 55304 | tf_op jit(solution)/shard_map/ppermute | solution.py:847
  296.7 8.1 %collective-permute-start.29 = (f32[4324]{0:T(1024)S(1)}, f32[4324]{0:T(1024)S(1)}, u32[]{:S(2)}, u32[]{:S(2)}) collective-permute-start(f32[4324]{0:T(1024)S(1)} %add.126), channel_id=1, source_target_pairs={{0,2},{1,3},{2,0},{3,1},{4,6},{5,7},{6,4},{7,5},{8,10},{9,11},{10,... | collective-permute-start | bytes 51896 | tf_op jit(solution)/shard_map/ppermute | solution.py:847
  298.8 8.1 %collective-permute-start.35 = (bf16[1,2,8,1152]{3,2,1,0:T(8,128)(2,1)S(1)}, bf16[1,2,8,1152]{3,2,1,0:T(8,128)(2,1)S(1)}, u32[]{:S(2)}, u32[]{:S(2)}) collective-permute-start(bf16[1,2,8,1152]{3,2,1,0:T(8,128)(2,1)S(1)} %pad_maximum_fusion.13), channel_id=1, source_target_pairs={{0,4},{4,0},{8,12},{12,8},{16,20},{20,16},{24,28},{28,24},{1,5},{5... | collective-permute-start | bytes 110600 | tf_op jit(solution)/shard_map/ppermute | solution.py:786
  299.4 7.7 %collective-permute-start.31 = (bf16[1,2,72,576]{3,2,1,0:T(8,128)(2,1)}, bf16[1,2,72,576]{3,2,1,0:T(8,128)(2,1)S(1)}, u32[]{:S(2)}, u32[]{:S(2)}) collective-permute-start(bf16[1,2,72,576]{3,2,1,0:T(8,128)(2,1)} %get-tuple-element.187), channel_id=1, source_target_pairs={{0,8},{4,12},{8,0},{12,4},{16,24},{20,28},{24,16},{28,20},{1,9},{5... | collective-permute-start | bytes 497672 | tf_op jit(solution)/shard_map/ppermute | solution.py:748
  299.7 9.5 %collective-permute-start.32 = (bf16[1,2,72,576]{3,2,1,0:T(8,128)(2,1)S(1)}, bf16[1,2,72,576]{3,2,1,0:T(8,128)(2,1)S(1)}, u32[]{:S(2)}, u32[]{:S(2)}) collective-permute-start(bf16[1,2,72,576]{3,2,1,0:T(8,128)(2,1)S(1)} %copy-done.54), channel_id=1, source_target_pairs={{0,4},{4,0},{8,12},{12,8},{16,20},{20,16},{24,28},{28,24},{1,5},{5... | collective-permute-start | bytes 497672 | tf_op jit(solution)/shard_map/ppermute | solution.py:748
  301.4 33.8 %collective-permute-start.38 = (bf16[2,72,1152]{2,1,0:T(8,128)(2,1)}, bf16[2,72,1152]{2,1,0:T(8,128)(2,1)S(1)}, u32[]{:S(2)}, u32[]{:S(2)}) collective-permute-start(bf16[2,72,1152]{2,1,0:T(8,128)(2,1)} %sum_pieces.16), channel_id=1, source_target_pairs={{0,16},{4,20},{8,24},{12,28},{16,0},{20,4},{24,8},{28,12},{1,17},{... | collective-permute-start | bytes 995336 | tf_op jit(solution)/shard_map/ppermute | solution.py:748
  304.8 11.6 %collective-permute-start.33 = (bf16[2,2,72,576]{3,2,1,0:T(8,128)(2,1)S(1)}, bf16[2,2,72,576]{3,2,1,0:T(8,128)(2,1)S(1)}, u32[]{:S(2)}, u32[]{:S(2)}) collective-permute-start(bf16[2,2,72,576]{3,2,1,0:T(8,128)(2,1)S(1)} %copy-done.53), channel_id=1, source_target_pairs={{0,2},{1,3},{2,0},{3,1},{4,6},{5,7},{6,4},{7,5},{8,10},{9,11},{10,... | collective-permute-start | bytes 995336 | tf_op jit(solution)/shard_map/ppermute | solution.py:847
  306.9 16.6 %collective-permute-start.36 = (bf16[144,1152]{1,0:T(8,128)(2,1)S(1)}, bf16[144,1152]{1,0:T(8,128)(2,1)S(1)}, u32[]{:S(2)}, u32[]{:S(2)}) collective-permute-start(bf16[144,1152]{1,0:T(8,128)(2,1)S(1)} %copy-done.27), channel_id=1, source_target_pairs={{0,2},{1,3},{2,0},{3,1},{4,6},{5,7},{6,4},{7,5},{8,10},{9,11},{10,... | collective-permute-start | bytes 995336 | tf_op jit(solution)/shard_map/ppermute | solution.py:847
  307.1 24.8 %collective-permute-start.25 = (bf16[256,1152]{1,0:T(8,128)(2,1)S(1)}, bf16[256,1152]{1,0:T(8,128)(2,1)S(1)}, u32[]{:S(2)}, u32[]{:S(2)}) collective-permute-start(bf16[256,1152]{1,0:T(8,128)(2,1)S(1)} %slice.161), channel_id=1, source_target_pairs={{0,2},{1,3},{2,0},{3,1},{4,6},{5,7},{6,4},{7,5},{8,10},{9,11},{10,... | collective-permute-start | bytes 1769480 | tf_op jit(solution)/shard_map/ppermute | solution.py:847
  320.2 20.0 %collective-permute-start.39 = (bf16[4,72,576]{2,1,0:T(8,128)(2,1)}, bf16[4,72,576]{2,1,0:T(8,128)(2,1)S(1)}, u32[]{:S(2)}, u32[]{:S(2)}) collective-permute-start(bf16[4,72,576]{2,1,0:T(8,128)(2,1)} %sum_pieces.17), channel_id=1, source_target_pairs={{0,16},{4,20},{8,24},{12,28},{16,0},{20,4},{24,8},{28,12},{1,17},{... | collective-permute-start | bytes 995336 | tf_op jit(solution)/shard_map/ppermute | solution.py:748
  320.2 3.8 %collective-permute-start.34 = (f32[4324]{0:T(1024)S(1)}, f32[4324]{0:T(1024)S(1)}, u32[]{:S(2)}, u32[]{:S(2)}) collective-permute-start(f32[4324]{0:T(1024)S(1)} %add.127), channel_id=1, source_target_pairs={{0,4},{4,0},{8,12},{12,8},{16,20},{20,16},{24,28},{28,24},{1,5},{5... | collective-permute-start | bytes 51896 | tf_op jit(solution)/shard_map/ppermute | solution.py:804
  323.5 4.4 %collective-permute-start.43 = (bf16[2,2,8,1152]{3,2,1,0:T(8,128)(2,1)S(1)}, bf16[2,2,8,1152]{3,2,1,0:T(8,128)(2,1)S(1)}, u32[]{:S(2)}, u32[]{:S(2)}) collective-permute-start(bf16[2,2,8,1152]{3,2,1,0:T(8,128)(2,1)S(1)} %pad_maximum_fusion.11), channel_id=1, source_target_pairs={{0,8},{4,12},{8,0},{12,4},{16,24},{20,28},{24,16},{28,20},{1,9},{5... | collective-permute-start | bytes 221192 | tf_op jit(solution)/shard_map/ppermute | solution.py:786
  324.0 9.0 %collective-permute-start.37 = (bf16[2,144,1152]{2,1,0:T(8,128)(2,1)S(1)}, bf16[2,144,1152]{2,1,0:T(8,128)(2,1)S(1)}, u32[]{:S(2)}, u32[]{:S(2)}) collective-permute-start(bf16[2,144,1152]{2,1,0:T(8,128)(2,1)S(1)} %maximum_select_fusion), channel_id=1, source_target_pairs={{0,1},{1,0},{2,3},{3,2},{4,5},{5,4},{6,7},{7,6},{8,9},{9,8},{10,11... | collective-permute-start | bytes 1990664 | tf_op jit(solution)/shard_map/ppermute | solution.py:850
  345.2 3.8 %collective-permute-start.40 = (f32[4324]{0:T(1024)S(1)}, f32[4324]{0:T(1024)S(1)}, u32[]{:S(2)}, u32[]{:S(2)}) collective-permute-start(f32[4324]{0:T(1024)S(1)} %add.128), channel_id=1, source_target_pairs={{0,8},{4,12},{8,0},{12,4},{16,24},{20,28},{24,16},{28,20},{1,9},{5... | collective-permute-start | bytes 51896 | tf_op jit(solution)/shard_map/ppermute | solution.py:804
  345.6 12.0 %collective-permute-start.46 = (bf16[4,2,8,1152]{3,2,1,0:T(8,128)(2,1)S(1)}, bf16[4,2,8,1152]{3,2,1,0:T(8,128)(2,1)S(1)}, u32[]{:S(2)}, u32[]{:S(2)}) collective-permute-start(bf16[4,2,8,1152]{3,2,1,0:T(8,128)(2,1)S(1)} %pad_maximum_fusion.9), channel_id=1, source_target_pairs={{0,16},{4,20},{8,24},{12,28},{16,0},{20,4},{24,8},{28,12},{1,17},{... | collective-permute-start | bytes 442376 | tf_op jit(solution)/shard_map/ppermute | solution.py:786
  349.1 4.7 %collective-permute-start.41 = (f32[4324]{0:T(1024)S(1)}, f32[4324]{0:T(1024)S(1)}, u32[]{:S(2)}, u32[]{:S(2)}) collective-permute-start(f32[4324]{0:T(1024)S(1)} %add.129), channel_id=1, source_target_pairs={{0,16},{4,20},{8,24},{12,28},{16,0},{20,4},{24,8},{28,12},{1,17},{... | collective-permute-start | bytes 51896 | tf_op jit(solution)/shard_map/ppermute | solution.py:804
  349.4 10.8 %collective-permute-start.44 = (bf16[72,2304]{1,0:T(8,128)(2,1)S(1)}, bf16[72,2304]{1,0:T(8,128)(2,1)S(1)}, u32[]{:S(2)}, u32[]{:S(2)}) collective-permute-start(bf16[72,2304]{1,0:T(8,128)(2,1)S(1)} %constant_dynamic-update-slice_fusion.4), channel_id=1, source_target_pairs={{0,2},{1,3},{2,0},{3,1},{4,6},{5,7},{6,4},{7,5},{8,10},{9,11},{10,... | collective-permute-start | bytes 995336 | tf_op jit(solution)/shard_map/ppermute | solution.py:847
  351.3 9.5 %collective-permute-start.42 = (bf16[72,2304]{1,0:T(8,128)(2,1)S(1)}, bf16[72,2304]{1,0:T(8,128)(2,1)S(1)}, u32[]{:S(2)}, u32[]{:S(2)}) collective-permute-start(bf16[72,2304]{1,0:T(8,128)(2,1)S(1)} %concatenate.100), channel_id=1, source_target_pairs={{0,2},{1,3},{2,0},{3,1},{4,6},{5,7},{6,4},{7,5},{8,10},{9,11},{10,... | collective-permute-start | bytes 995336 | tf_op jit(solution)/shard_map/ppermute | solution.py:847
  361.2 4.3 %collective-permute-start.47 = (bf16[144,2304]{1,0:T(8,128)(2,1)S(1)}, bf16[144,2304]{1,0:T(8,128)(2,1)S(1)}, u32[]{:S(2)}, u32[]{:S(2)}) collective-permute-start(bf16[144,2304]{1,0:T(8,128)(2,1)S(1)} %pad_maximum_fusion.5), channel_id=1, source_target_pairs={{0,1},{1,0},{2,3},{3,2},{4,5},{5,4},{6,7},{7,6},{8,9},{9,8},{10,11... | collective-permute-start | bytes 1990664 | tf_op jit(solution)/shard_map/ppermute | solution.py:850
  (56 other events, 365.1 us)
Sparse Core Ops, SparseCore 0:
  102.7 170.7 reduce-scatter.1

commit v2 on v1

--- a/solution.py
+++ b/solution.py
@@ -916,14 +916,9 @@
         scale, own_heads,
     )
     clock.passed(qkv)
-    times_all = Gather(
-        clock, time_embed[None], [(swaps[k], img_bits[k], 0) for k in range(bits)]
-    )
-    times_all.tick()
     half_heads = own_heads // 2
     o_a, lse_a = attend_forward(clock.now, qkv, tables, feats, 0, half_heads)
     clock.passed(o_a, grad_rx)
-    times_all.tick()
     far_a = swap_core(o_a)
     o_b, lse_b = attend_forward(clock.now, qkv, tables, feats, half_heads, half_heads)
     far_b = swap_core(o_b)
@@ -943,7 +938,6 @@
     )
     branch_one = dot(attn_all[:, :mine], output_projection_weight, 0, 0)
     hidden_one = x.astype(F32) + branch_one
-    times_all.tick()
     mlp_in = clock.tie((moments(hidden_one)[0] * ln2_gain).astype(BF))
 
     tile = ff // 6
@@ -1009,13 +1003,13 @@
         clock,
         part[None, None],
         [(swap_core, c == 1, 3), (swap_y, y == 1, 1)]
-        + [(swaps[k], img_bits[k], 0) for k in range(bits)],
+        + [(swaps[k], img_bits[k], 0) for k in [*range(1, bits), 0]],
     )
     gather.tick()
     w_part = project_weights(clock.now, attn_in, d)
     clock.passed(w_part, job_proj.arrived[0][0])
     gather.land()
-    times_all = times_all.finish()
+    gather.part = jnp.concatenate([gather.part, te[None, None]], axis=2)
     jobs_qkv = [by_row(dims, (w_part,), cols, prefix=(p,)) for p, dims in enumerate(orders)]
     step(jobs_qkv)
     jobs_qkv.append(job_proj)
@@ -1081,9 +1075,9 @@
     )
     clock.passed(w_up_grad)
     small = small.finish()
-    factors = gather.finish().reshape(n_img * slots, 8, dm)
-
-    te_rows = lax.dynamic_slice_in_dim(times_all, me_img * rows, rows, 3)
+    factors = gather.finish().reshape(n_img * slots, 12, dm)
+
+    te_rows = lax.dynamic_slice_in_dim(factors[:, 8:], me_img * rows, rows, 2)
     w_time_q_grad, w_time_v_grad = (
         lax.dot_general(
             te_rows.reshape(-1, rows),

time: 384 us -> 389 us (1.013)
  waiting for transfers between devices: 48.5 us -> 55.4 us
    ppermute x13, waiting for transfers between devices: 12.3 us -> 18.4 us  [advance(): total = swaps[key[0]](total)]
    ppermute x6 -> x3, waiting for transfers between devices: 10.1 us -> 14.8 us  [tick(): self.far = swap(self.clock.tie(self.part))]
    unnamed x118 -> x112, local copies, waits for them, and re-layouts: 12.6 us -> 12.7 us
  transfers between devices with their start and end apart: 49 -> 46, of which waited for: 15 -> 17; matrix products, arithmetic and copies ran while one was open for 13% -> 13% of each run, Pallas kernels for 43% -> 43%
where the time goes in v2:
time: 389 us; the launch traced here: 385 us
  Pallas kernels  194 us (50%)
  waiting for transfers between devices  55.4 us (14%)
  local copies, waits for them, and re-layouts  43.3 us (11%)
  starting transfers between devices  41 us (11%)
  matrix products  19 us (5%)
  other arithmetic  16.1 us (4%)
  between operations  15.8 us (4%)
    pallas_call x10, Pallas kernels, advance(): pl.pallas_call(functools.partial(sum_kernel, counts=counts, places=places...  37.4 us
    pallas_call x1, Pallas kernels, mlp_fall(): pl.pallas_call(fall_kernel, grid_spec=pltpu.PrefetchScalarGridSpec(num_sc...  29.7 us
    pallas_call x1, Pallas kernels, mlp_rise(): pl.pallas_call(rise_kernel, grid=(ff // tile,), in_specs=[pl.BlockSpec((r...  27.4 us
    pallas_call x1, Pallas kernels, attend_backward(): pl.pallas_call(functools.partial(backward_kernel, scale=scale), grid_spec...  27.3 us
    pallas_call x2, Pallas kernels, attend_forward(): pl.pallas_call(forward_kernel, grid_spec=pltpu.PrefetchScalarGridSpec(num...  18.5 us
    ppermute x13, waiting for transfers between devices, advance(): total = swaps[key[0]](total)  18.4 us
    ppermute x13, starting transfers between devices, advance(): total = swaps[key[0]](total)  16.5 us
    ppermute x14, starting transfers between devices, swap_y(): return lax.ppermute(a, 'seq', over_y)  15.6 us
  transfers between devices with their start and end apart: 46, of which 17 were waited for; matrix products, arithmetic and copies ran while one was open for 13% of the time, Pallas kernels for 43%

profile of v2, /device:TPU:0, one launch (start us, length us, event | category | flops | bytes accessed | tf_op | source)
XLA Modules:
  0.0 385.1 jit_solution(16061687419283990135)
XLA Ops:
  7.3 2.3 dynamic-slice_bitcast_fusion
  9.6 3.0 collective-permute-start
  13.8 2.2 fusion.28
  21.0 1.6 token_features.1
  23.9 2.3 dynamic-slice_bitcast_fusion.2
  29.2 14.0 %project.1 = (bf16[1024,1152]{1,0:T(8,128)(2,1)}, bf16[512,1152]{1,0:T(8,128)(2,1)}, bf16[3,8,72,1024]{3,2,1,0:T(8,128)(2,1)}) custom-call(s32[1]{0:T(128)} %bitcast.4.core_ref, bf16[256,1152]{1,0:T(8,128)(2,1)} %copy-done.21, bf16[256,1152]{1,0:T(8,128)(2,1)} %collective-permute-done.b_ref, bf16[256,1152]{1,0:T(8,128)(2,1)} %collective-permute-done.1.c_ref, ...), custom_call_target="tpu_custom_call" | custom-call | flops 1000000 | bytes 100000 | tf_op jit(solution)/shard_map/project/pallas_call | solution.py:164
  43.2 9.2 %attention_forward.2 = (bf16[4,72,1024]{2,1,0:T(8,128)(2,1)}, f32[4,1,1024]{2,1,0:T(1,128)}) custom-call(s32[5]{0:T(128)} %stack.95.clock_ref.coord_ref, bf16[3,8,72,1024]{3,2,1,0:T(8,128)(2,1)} %get-tuple-element.114.p_ref.qkv_ref, bf16[8,64,64]{2,1,0:T(8,128)(2,1)} %fusion.22.table_ref, bf16[112,1024]{1,0:T(8,128)(2,1)} %get-tuple-element.111.feat_ref), custom_call_target="tpu_custom_call" | custom-call | flops 1000000 | bytes 100000 | tf_op jit(solution)/shard_map/attention_forward/pallas_call | solution.py:323
  52.7 9.3 %attention_forward.3 = (bf16[4,72,1024]{2,1,0:T(8,128)(2,1)}, f32[4,1,1024]{2,1,0:T(1,128)}) custom-call(s32[5]{0:T(128)} %stack.95.clock_ref.coord_ref, bf16[3,8,72,1024]{3,2,1,0:T(8,128)(2,1)} %get-tuple-element.114.p_ref.qkv_ref, bf16[8,64,64]{2,1,0:T(8,128)(2,1)} %fusion.22.table_ref, bf16[112,1024]{1,0:T(8,128)(2,1)} %get-tuple-element.111.feat_ref), custom_call_target="tpu_custom_call" | custom-call | flops 1000000 | bytes 100000 | tf_op jit(solution)/shard_map/attention_forward/pallas_call | solution.py:323
  67.2 3.4 fusion.45
  72.5 27.4 %feed_forward_rise.1 = (f32[512,1152]{1,0:T(8,128)}, bf16[512,4608]{1,0:T(8,128)(2,1)}, bf16[4608,1152]{1,0:T(8,128)(2,1)}, bf16[1152,512]{1,0:T(8,128)(2,1)}, bf16[512,1152]{1,0:T(8,128)(2,1)}) custom-call(bf16[512,1152]{1,0:T(8,128)(2,1)} %multiply_convert_fusion.m_ref, bf16[256,1152]{1,0:T(8,128)(2,1)} %get-tuple-element.237.near_ref, ...), custom_call_target="tpu_custom_call" | custom-call | flops 1000000 | bytes 100000 | tf_op jit(solution)/shard_map/feed_forward_rise/pallas_call | solution.py:468
  99.9 29.7 %feed_forward_fall.1 = (f32[512,1152]{1,0:T(8,128)}, bf16[1152,2304]{1,0:T(8,128)(2,1)}, bf16[1152,2304]{1,0:T(8,128)(2,1)}) custom-call(s32[5]{0:T(128)} %stack.95.clock_ref.coord_ref, s32[2]{0:T(128)} %pad_add_fusion.1.tile_ref, bf16[1152,512]{1,0:T(8,128)(2,1)} %get-tuple-element.126.mt_ref, bf16[512,1152]{1,0:T(8,128)(2,1)} %get-tuple-element.127.g_ref, ...), custom_call_target="tpu_custom_call" | custom-call | flops 1000000 | bytes 100000 | tf_op jit(solution)/shard_map/feed_forward_fall/pallas_call | solution.py:526
  129.6 9.2 %middle.1 = (bf16[512,1152]{1,0:T(8,128)(2,1)}, f32[512,1152]{1,0:T(8,128)}, bf16[512,1152]{1,0:T(8,128)(2,1)}, f32[8,1152]{1,0:T(8,128)}) custom-call(s32[5]{0:T(128)} %stack.95.clock_ref.coord_ref, f32[512,1152]{1,0:T(8,128)} %get-tuple-element.129.gm_ref, f32[512,1152]{1,0:T(8,128)} %get-tuple-element.124.two_ref, ...), custom_call_target="tpu_custom_call" | custom-call | flops 1000000 | bytes 100000 | tf_op jit(solution)/shard_map/middle/pallas_call | solution.py:600
  139.2 3.1 collective-permute-done.7
  142.6 1.9 slice.161
  146.8 3.3 convolution_convert_fusion
  150.1 2.6 copy.45
  152.7 4.4 %convolution_convert_fusion.1 = bf16[576,1024]{1,0:T(8,128)(2,1)} fusion(bf16[1024,1152]{1,0:T(8,128)(2,1)} %copy-done.35, bf16[1152,1152]{1,0:T(8,128)(2,1)S(1)} %copy-done, s32[]{:T(128)S(6)} %select_n.199), kind=kOutput, calls=%fused_computation.10 | convolution fusion | flops 1359544320 | bytes 4866052 | tf_op jit(solution)/shard_map/dot_general | solution.py:30
  157.1 3.0 collective-permute-done.6
  160.2 5.7 %sum_pieces.10 = (bf16[1,2,2,2,72,1152]{5,4,3,2,1,0:T(8,128)(2,1)}, bf16[1,2,2,2,72,1152]{5,4,3,2,1,0:T(8,128)(2,1)}, bf16[1,2,2,2,72,576]{5,4,3,2,1,0:T(8,128)(2,1)}) custom-call(s32[5]{0:T(128)} %stack.95.clock_ref.coord_ref, bf16[2,2,2,2,72,2304]{5,4,3,2,1,0:T(8,128)(2,1)} %bitcast.126, ...), custom_call_target="tpu_custom_call" | custom-call | flops 1000000 | bytes 100000 | tf_op jit(solution)/shard_map/sum_pieces/pallas_call | solution.py:733
  169.0 1.8 collective-permute-start.11
  172.2 27.3 %attention_backward.1 = (bf16[3,8,72,1024]{3,2,1,0:T(8,128)(2,1)}, f32[8,64,64]{2,1,0:T(8,128)}, f32[2,8,16,72]{3,2,1,0:T(8,128)}) custom-call(s32[5]{0:T(128)} %stack.95.clock_ref.coord_ref, bf16[3,8,72,1024]{3,2,1,0:T(8,128)(2,1)} %get-tuple-element.114.p_ref.qkv_ref, bf16[8,72,1024]{2,1,0:T(8,128)(2,1)} %copy-done.10, bf16[8,72,1024]{2,1,0:T(8,128)(2,1)} %bitcast.146, ...), custom_call_target="tpu_custom_call" | custom-call | flops 1000000 | bytes 100000 | tf_op jit(solution)/shard_map/attention_backward/pallas_call | solution.py:400
  199.5 4.3 %collective-permute-done.9.refs_2_ = bf16[1,2,2,2,72,1152]{5,4,3,2,1,0:T(8,128)(2,1)S(1)} collective-permute-done((bf16[1,2,2,2,72,1152]{5,4,3,2,1,0:T(8,128)(2,1)}, bf16[1,2,2,2,72,1152]{5,4,3,2,1,0:T(8,128)(2,1)S(1)}, u32[]{:S(2)}, u32[]{:S(2)}) %collective-permute-start.9) | collective-permute-done | bytes 1327136 | tf_op jit(solution)/shard_map/ppermute | solution.py:748
  206.0 3.8 sum_pieces.11
  212.8 10.0 %project_weights.1 = bf16[3,1152,576]{2,1,0:T(8,128)(2,1)} custom-call(s32[5]{0:T(128)} %stack.95.clock_ref.coord_ref, bf16[1024,1152]{1,0:T(8,128)(2,1)} %get-tuple-element.150.in_ref, bf16[3,8,72,1024]{3,2,1,0:T(8,128)(2,1)} %get-tuple-element.145.d_ref), custom_call_target="tpu_custom_call" | custom-call | flops 1000000 | bytes 100000 | tf_op jit(solution)/shard_map/project_weights/pallas_call | solution.py:206
  223.7 4.6 %sum_pieces.12 = (bf16[1,2,2,2,72,576]{5,4,3,2,1,0:T(8,128)(2,1)}, bf16[1,2,2,2,72,576]{5,4,3,2,1,0:T(8,128)(2,1)}, bf16[1,2,2,2,72,576]{5,4,3,2,1,0:T(8,128)(2,1)}) custom-call(s32[5]{0:T(128)} %stack.95.clock_ref.coord_ref, bf16[3,2,2,2,2,72,576]{6,5,4,3,2,1,0:T(8,128)(2,1)} %bitcast.111, bf16[3,2,2,2,2,72,576]{6,5,4,3,2,1,0:T(8,128)(2,1)} %bitcast.112, ...), custom_call_target="tpu_custom_call" | custom-call | flops 1000000 | bytes 100000 | tf_op jit(solution)/shard_map/sum_pieces/pallas_call | solution.py:733
  230.0 1.7 collective-permute-start.18
  231.7 13.6 %project_back.1 = (f32[512,1152]{1,0:T(8,128)}, bf16[512,1152]{1,0:T(8,128)(2,1)}) custom-call(s32[5]{0:T(128)} %stack.95.clock_ref.coord_ref, s32[1]{0:T(128)} %bitcast.4.core_ref, bf16[3,8,72,1024]{3,2,1,0:T(8,128)(2,1)} %get-tuple-element.145.d_ref, bf16[1152,3456]{1,0:T(8,128)(2,1)} %w_ref.3), custom_call_target="tpu_custom_call" | custom-call | flops 1000000 | bytes 100000 | tf_op jit(solution)/shard_map/project_back/pallas_call | solution.py:266
  245.4 3.6 sum_pieces.13
  250.5 6.4 %collective-permute-done.18.refs_5_.refs_7_.refs_9_.refs_11_ = bf16[1,2,2,2,72,576]{5,4,3,2,1,0:T(8,128)(2,1)S(1)} collective-permute-done((bf16[1,2,2,2,72,576]{5,4,3,2,1,0:T(8,128)(2,1)}, bf16[1,2,2,2,72,576]{5,4,3,2,1,0:T(8,128)(2,1)S(1)}, u32[]{:S(2)}, u32[]{:S(2)}) %collective-permute-start.18) | collective-permute-done | bytes 663584 | tf_op jit(solution)/shard_map/ppermute | solution.py:748
  257.8 3.8 sum_pieces.14
  268.6 5.9 %last.1 = (bf16[512,1152]{1,0:T(8,128)(2,1)}, f32[8,1152]{1,0:T(8,128)}) custom-call(f32[512,1152]{1,0:T(8,128)} %get-tuple-element.159.back_ref, bf16[512,1152]{1,0:T(8,128)(2,1)} %collective-permute-done.15.far_ref, bf16[512,1152]{1,0:T(8,128)(2,1)} %get-tuple-element.121.x_ref, f32[512,1152]{1,0:T(8,128)} %get-tuple-element.166.grad_ref, ...), custom_call_target="tpu_custom_call" | custom-call | flops 1000000 | bytes 100000 | tf_op jit(solution)/shard_map/last/pallas_call | solution.py:639
  276.1 2.9 collective-permute-done.20.refs_5_.refs_6_.refs_7_
  280.6 3.3 sum_pieces.15
  288.0 3.1 sum_pieces.16
  295.2 2.4 collective-permute-start.35
  299.9 4.1 %collective-permute-done.28.refs_3_ = bf16[1,2,72,576]{3,2,1,0:T(8,128)(2,1)S(1)} collective-permute-done((bf16[1,2,72,576]{3,2,1,0:T(8,128)(2,1)S(1)}, bf16[1,2,72,576]{3,2,1,0:T(8,128)(2,1)S(1)}, u32[]{:S(2)}, u32[]{:S(2)}) %collective-permute-start.28) | collective-permute-done | bytes 165920 | tf_op jit(solution)/shard_map/ppermute | solution.py:748
  304.7 4.6 %collective-permute-done.30.refs_11_.refs_15_.refs_13_.refs_18_ = bf16[2,2,72,576]{3,2,1,0:T(8,128)(2,1)S(1)} collective-permute-done((bf16[2,2,72,576]{3,2,1,0:T(8,128)(2,1)S(1)}, bf16[2,2,72,576]{3,2,1,0:T(8,128)(2,1)S(1)}, u32[]{:S(2)}, u32[]{:S(2)}) %collective-permute-start.30) | collective-permute-done | bytes 331808 | tf_op jit(solution)/shard_map/ppermute | solution.py:847
  310.0 3.0 sum_pieces.17
  314.7 1.7 collective-permute-done.33
  317.9 14.8 %collective-permute-done.40 = bf16[2,2,12,1152]{3,2,1,0:T(8,128)(2,1)S(1)} collective-permute-done((bf16[2,2,12,1152]{3,2,1,0:T(8,128)(2,1)S(1)}, bf16[2,2,12,1152]{3,2,1,0:T(8,128)(2,1)S(1)}, u32[]{:S(2)}, u32[]{:S(2)}) %collective-permute-start.40) | collective-permute-done | bytes 110624 | tf_op jit(solution)/shard_map/ppermute | solution.py:786
  334.5 1.7 pad_maximum_fusion
  336.9 3.3 sum_pieces.18
  342.0 3.2 sum_pieces.19
  346.5 1.6 collective-permute-start.43
  348.1 2.0 collective-permute-done.37
  351.7 1.7 collective-permute-start.41
  362.5 3.9 %collective-permute-done.39 = bf16[72,2304]{1,0:T(8,128)(2,1)S(1)} collective-permute-done((bf16[72,2304]{1,0:T(8,128)(2,1)S(1)}, bf16[72,2304]{1,0:T(8,128)(2,1)S(1)}, u32[]{:S(2)}, u32[]{:S(2)}) %collective-permute-start.39) | collective-permute-done | bytes 331808 | tf_op jit(solution)/shard_map/ppermute | solution.py:847
  374.0 4.0 %concatenate.96 = f32[144,3456]{1,0:T(8,128)} concatenate(f32[144,576]{1,0:T(8,128)} %get-tuple-element.222, f32[144,576]{1,0:T(8,128)} %get-tuple-element.226, f32[144,576]{1,0:T(8,128)} %get-tuple-element.221, f32[144,576]{1,0:T(8,128)S(1)} %get-tuple-element.225, f32[144,576]{1,0:T(8,128)} %get-tuple-element.220, f32[144,576]{1,0:T(8,128)S(1)} %get-tuple-element.224), dimensions={1} | concatenate | bytes 3981312 | tf_op jit(solution)/shard_map/concatenate | solution.py:1096
  (279 shorter events, 83.7 us)
Async XLA Ops:
  7.2 59.5 %copy-start = (bf16[1152,1152]{1,0:T(8,128)(2,1)S(1)}, bf16[1152,1152]{1,0:T(8,128)(2,1)}, u32[]{:S(2)}) copy-start(bf16[1152,1152]{1,0:T(8,128)(2,1)} %param.25) | copy-start | bytes 7962628
  7.2 268.8 %reduce-scatter.2.cloned.1.call-start = ((), (), s32[]{:S(2)}) async-start(), calls=%async_computation.1 | async-start | bytes 10948608 | tf_op jit(solution)/shard_map/reduce_scatter | solution.py:948
  9.6 16.6 %collective-permute-start = (bf16[256,1152]{1,0:T(8,128)(2,1)}, bf16[256,1152]{1,0:T(8,128)(2,1)}, u32[]{:S(2)}, u32[]{:S(2)}) collective-permute-start(bf16[256,1152]{1,0:T(8,128)(2,1)} %get-tuple-element.235), channel_id=1, source_target_pairs={{0,2},{1,3},{2,0},{3,1},{4,6},{5,7},{6,4},{7,5},{8,10},{9,11},{10,... | collective-permute-start | bytes 1769480 | tf_op jit(solution)/shard_map/ppermute | solution.py:847
  12.6 16.6 %collective-permute-start.1 = (bf16[256,1152]{1,0:T(8,128)(2,1)S(1)}, bf16[256,1152]{1,0:T(8,128)(2,1)}, u32[]{:S(2)}, u32[]{:S(2)}) collective-permute-start(bf16[256,1152]{1,0:T(8,128)(2,1)S(1)} %get-tuple-element.236.a_ref), channel_id=1, source_target_pairs={{0,1},{1,0},{2,3},{3,2},{4,5},{5,4},{6,7},{7,6},{8,9},{9,8},{10,11... | collective-permute-start | bytes 1769480 | tf_op jit(solution)/shard_map/ppermute | solution.py:850
  26.2 3.0 collective-permute-start.2
  26.7 25.9 %collective-permute-start.3 = (bf16[256,1152]{1,0:T(8,128)(2,1)}, bf16[256,1152]{1,0:T(8,128)(2,1)}, u32[]{:S(2)}, u32[]{:S(2)}) collective-permute-start(bf16[256,1152]{1,0:T(8,128)(2,1)} %get-tuple-element.117), channel_id=1, source_target_pairs={{0,2},{1,3},{2,0},{3,1},{4,6},{5,7},{6,4},{7,5},{8,10},{9,11},{10,... | collective-permute-start | bytes 1769480 | tf_op jit(solution)/shard_map/ppermute | solution.py:847
  52.4 12.0 %collective-permute-start.4 = (bf16[4,72,1024]{2,1,0:T(8,128)(2,1)}, bf16[4,72,1024]{2,1,0:T(8,128)(2,1)S(1)}, u32[]{:S(2)}, u32[]{:S(2)}) collective-permute-start(bf16[4,72,1024]{2,1,0:T(8,128)(2,1)} %get-tuple-element.116), channel_id=1, source_target_pairs={{0,1},{1,0},{2,3},{3,2},{4,5},{5,4},{6,7},{7,6},{8,9},{9,8},{10,11... | collective-permute-start | bytes 1769480 | tf_op jit(solution)/shard_map/ppermute | solution.py:850
  61.9 2.6 collective-permute-start.5
  138.8 3.4 collective-permute-start.7
  142.2 17.9 %collective-permute-start.8 = (bf16[1152,2304]{1,0:T(8,128)(2,1)}, bf16[1152,2304]{1,0:T(8,128)(2,1)}, u32[]{:S(2)}, u32[]{:S(2)}) collective-permute-start(bf16[1152,2304]{1,0:T(8,128)(2,1)} %get-tuple-element.138), channel_id=1, source_target_pairs={{0,1},{1,0},{2,3},{3,2},{4,5},{5,4},{6,7},{7,6},{8,9},{9,8},{10,11... | collective-permute-start | bytes 15925256 | tf_op jit(solution)/shard_map/ppermute | solution.py:850
  144.5 15.6 %collective-permute-start.6 = (bf16[256,1152]{1,0:T(8,128)(2,1)}, bf16[256,1152]{1,0:T(8,128)(2,1)S(1)}, u32[]{:S(2)}, u32[]{:S(2)}) collective-permute-start(bf16[256,1152]{1,0:T(8,128)(2,1)} %slice.161), channel_id=1, source_target_pairs={{0,2},{1,3},{2,0},{3,1},{4,6},{5,7},{6,4},{7,5},{8,10},{9,11},{10,... | collective-permute-start | bytes 1769480 | tf_op jit(solution)/shard_map/ppermute | solution.py:847
  165.9 37.9 %collective-permute-start.9 = (bf16[1,2,2,2,72,1152]{5,4,3,2,1,0:T(8,128)(2,1)}, bf16[1,2,2,2,72,1152]{5,4,3,2,1,0:T(8,128)(2,1)S(1)}, u32[]{:S(2)}, u32[]{:S(2)}) collective-permute-start(bf16[1,2,2,2,72,1152]{5,4,3,2,1,0:T(8,128)(2,1)} %get-tuple-element.139), channel_id=1, source_target_pairs={{0,4},{4,0},{8,12},{12,8},{16,20},{20,16},{24,28},{28,24},{1,5},{5... | collective-permute-start | bytes 3981320 | tf_op jit(solution)/shard_map/ppermute | solution.py:748
  167.2 36.7 %collective-permute-start.10 = (bf16[1,2,2,2,72,1152]{5,4,3,2,1,0:T(8,128)(2,1)}, bf16[1,2,2,2,72,1152]{5,4,3,2,1,0:T(8,128)(2,1)S(1)}, u32[]{:S(2)}, u32[]{:S(2)}) collective-permute-start(bf16[1,2,2,2,72,1152]{5,4,3,2,1,0:T(8,128)(2,1)} %get-tuple-element.140), channel_id=1, source_target_pairs={{0,2},{1,3},{2,0},{3,1},{4,6},{5,7},{6,4},{7,5},{8,10},{9,11},{10,... | collective-permute-start | bytes 3981320 | tf_op jit(solution)/shard_map/ppermute | solution.py:847
  169.0 53.8 %collective-permute-start.11 = (bf16[1,2,2,2,72,576]{5,4,3,2,1,0:T(8,128)(2,1)}, bf16[1,2,2,2,72,576]{5,4,3,2,1,0:T(8,128)(2,1)S(1)}, u32[]{:S(2)}, u32[]{:S(2)}) collective-permute-start(bf16[1,2,2,2,72,576]{5,4,3,2,1,0:T(8,128)(2,1)} %get-tuple-element.141), channel_id=1, source_target_pairs={{0,8},{4,12},{8,0},{12,4},{16,24},{20,28},{24,16},{28,20},{1,9},{5... | collective-permute-start | bytes 1990664 | tf_op jit(solution)/shard_map/ppermute | solution.py:748
  209.7 35.6 %collective-permute-start.13 = (bf16[1,2,2,72,1152]{4,3,2,1,0:T(8,128)(2,1)}, bf16[1,2,2,72,1152]{4,3,2,1,0:T(8,128)(2,1)}, u32[]{:S(2)}, u32[]{:S(2)}) collective-permute-start(bf16[1,2,2,72,1152]{4,3,2,1,0:T(8,128)(2,1)} %get-tuple-element.147), channel_id=1, source_target_pairs={{0,8},{4,12},{8,0},{12,4},{16,24},{20,28},{24,16},{28,20},{1,9},{5... | collective-permute-start | bytes 1990664 | tf_op jit(solution)/shard_map/ppermute | solution.py:748
  209.7 35.6 %collective-permute-start.14 = (bf16[1,2,2,72,1152]{4,3,2,1,0:T(8,128)(2,1)}, bf16[1,2,2,72,1152]{4,3,2,1,0:T(8,128)(2,1)}, u32[]{:S(2)}, u32[]{:S(2)}) collective-permute-start(bf16[1,2,2,72,1152]{4,3,2,1,0:T(8,128)(2,1)} %get-tuple-element.148), channel_id=1, source_target_pairs={{0,4},{4,0},{8,12},{12,8},{16,20},{20,16},{24,28},{28,24},{1,5},{5... | collective-permute-start | bytes 1990664 | tf_op jit(solution)/shard_map/ppermute | solution.py:748
  212.1 10.7 %collective-permute-start.12 = (bf16[1,1,8,576]{3,2,1,0:T(8,128)(2,1)S(1)}, bf16[1,1,8,576]{3,2,1,0:T(8,128)(2,1)S(1)}, u32[]{:S(2)}, u32[]{:S(2)}) collective-permute-start(bf16[1,1,8,576]{3,2,1,0:T(8,128)(2,1)S(1)} %convert_element_type.61), channel_id=1, source_target_pairs={{0,1},{1,0},{2,3},{3,2},{4,5},{5,4},{6,7},{7,6},{8,9},{9,8},{10,11... | collective-permute-start | bytes 27656 | tf_op jit(solution)/shard_map/ppermute | solution.py:850
  228.3 21.8 %collective-permute-start.16 = (bf16[1,2,2,2,72,576]{5,4,3,2,1,0:T(8,128)(2,1)}, bf16[1,2,2,2,72,576]{5,4,3,2,1,0:T(8,128)(2,1)S(1)}, u32[]{:S(2)}, u32[]{:S(2)}) collective-permute-start(bf16[1,2,2,2,72,576]{5,4,3,2,1,0:T(8,128)(2,1)} %get-tuple-element.155), channel_id=1, source_target_pairs={{0,4},{4,0},{8,12},{12,8},{16,20},{20,16},{24,28},{28,24},{1,5},{5... | collective-permute-start | bytes 1990664 | tf_op jit(solution)/shard_map/ppermute | solution.py:748
  229.0 21.5 %collective-permute-start.17 = (bf16[1,2,2,2,72,576]{5,4,3,2,1,0:T(8,128)(2,1)}, bf16[1,2,2,2,72,576]{5,4,3,2,1,0:T(8,128)(2,1)S(1)}, u32[]{:S(2)}, u32[]{:S(2)}) collective-permute-start(bf16[1,2,2,2,72,576]{5,4,3,2,1,0:T(8,128)(2,1)} %get-tuple-element.156), channel_id=1, source_target_pairs={{0,2},{1,3},{2,0},{3,1},{4,6},{5,7},{6,4},{7,5},{8,10},{9,11},{10,... | collective-permute-start | bytes 1990664 | tf_op jit(solution)/shard_map/ppermute | solution.py:847
  230.0 26.9 %collective-permute-start.18 = (bf16[1,2,2,2,72,576]{5,4,3,2,1,0:T(8,128)(2,1)}, bf16[1,2,2,2,72,576]{5,4,3,2,1,0:T(8,128)(2,1)S(1)}, u32[]{:S(2)}, u32[]{:S(2)}) collective-permute-start(bf16[1,2,2,2,72,576]{5,4,3,2,1,0:T(8,128)(2,1)} %get-tuple-element.157), channel_id=1, source_target_pairs={{0,8},{4,12},{8,0},{12,4},{16,24},{20,28},{24,16},{28,20},{1,9},{5... | collective-permute-start | bytes 1990664 | tf_op jit(solution)/shard_map/ppermute | solution.py:748
  249.0 18.2 %collective-permute-start.15 = (bf16[512,1152]{1,0:T(8,128)(2,1)}, bf16[512,1152]{1,0:T(8,128)(2,1)}, u32[]{:S(2)}, u32[]{:S(2)}) collective-permute-start(bf16[512,1152]{1,0:T(8,128)(2,1)} %get-tuple-element.165), channel_id=1, source_target_pairs={{0,1},{1,0},{2,3},{3,2},{4,5},{5,4},{6,7},{7,6},{8,9},{9,8},{10,11... | collective-permute-start | bytes 3538952 | tf_op jit(solution)/shard_map/ppermute | solution.py:850
  250.0 13.1 %copy-start.42 = (s32[32,32]{1,0:T(8,128)S(1)}, s32[32,32]{1,0:T(8,128)}, u32[]{:S(2)}) copy-start(s32[32,32]{1,0:T(8,128)} %subtract_add_fusion) | copy-start | bytes 12292
  261.6 18.0 %collective-permute-start.21 = (bf16[2,2,2,72,576]{4,3,2,1,0:T(8,128)(2,1)}, bf16[2,2,2,72,576]{4,3,2,1,0:T(8,128)(2,1)S(1)}, u32[]{:S(2)}, u32[]{:S(2)}) collective-permute-start(bf16[2,2,2,72,576]{4,3,2,1,0:T(8,128)(2,1)} %get-tuple-element.170), channel_id=1, source_target_pairs={{0,4},{4,0},{8,12},{12,8},{16,20},{20,16},{24,28},{28,24},{1,5},{5... | collective-permute-start | bytes 1990664 | tf_op jit(solution)/shard_map/ppermute | solution.py:748
  263.8 12.3 %collective-permute-start.19 = (bf16[1,2,2,72,576]{4,3,2,1,0:T(8,128)(2,1)}, bf16[1,2,2,72,576]{4,3,2,1,0:T(8,128)(2,1)S(1)}, u32[]{:S(2)}, u32[]{:S(2)}) collective-permute-start(bf16[1,2,2,72,576]{4,3,2,1,0:T(8,128)(2,1)} %get-tuple-element.168), channel_id=1, source_target_pairs={{0,2},{1,3},{2,0},{3,1},{4,6},{5,7},{6,4},{7,5},{8,10},{9,11},{10,... | collective-permute-start | bytes 995336 | tf_op jit(solution)/shard_map/ppermute | solution.py:847
  264.2 14.8 %collective-permute-start.20 = (bf16[1,2,2,72,576]{4,3,2,1,0:T(8,128)(2,1)}, bf16[1,2,2,72,576]{4,3,2,1,0:T(8,128)(2,1)S(1)}, u32[]{:S(2)}, u32[]{:S(2)}) collective-permute-start(bf16[1,2,2,72,576]{4,3,2,1,0:T(8,128)(2,1)} %get-tuple-element.169), channel_id=1, source_target_pairs={{0,8},{4,12},{8,0},{12,4},{16,24},{20,28},{24,16},{28,20},{1,9},{5... | collective-permute-start | bytes 995336 | tf_op jit(solution)/shard_map/ppermute | solution.py:748
  265.9 20.7 %collective-permute-start.24 = (bf16[1,2,72,1152]{3,2,1,0:T(8,128)(2,1)}, bf16[1,2,72,1152]{3,2,1,0:T(8,128)(2,1)S(1)}, u32[]{:S(2)}, u32[]{:S(2)}) collective-permute-start(bf16[1,2,72,1152]{3,2,1,0:T(8,128)(2,1)} %get-tuple-element.162), channel_id=1, source_target_pairs={{0,2},{1,3},{2,0},{3,1},{4,6},{5,7},{6,4},{7,5},{8,10},{9,11},{10,... | collective-permute-start | bytes 995336 | tf_op jit(solution)/shard_map/ppermute | solution.py:847
  267.1 19.5 %collective-permute-start.25 = (bf16[1,2,72,1152]{3,2,1,0:T(8,128)(2,1)}, bf16[1,2,72,1152]{3,2,1,0:T(8,128)(2,1)S(1)}, u32[]{:S(2)}, u32[]{:S(2)}) collective-permute-start(bf16[1,2,72,1152]{3,2,1,0:T(8,128)(2,1)} %get-tuple-element.163), channel_id=1, source_target_pairs={{0,8},{4,12},{8,0},{12,4},{16,24},{20,28},{24,16},{28,20},{1,9},{5... | collective-permute-start | bytes 995336 | tf_op jit(solution)/shard_map/ppermute | solution.py:748
  276.0 15.1 %collective-permute-start.23 = (f32[4324]{0:T(1024)S(1)}, f32[4324]{0:T(1024)S(1)}, u32[]{:S(2)}, u32[]{:S(2)}) collective-permute-start(f32[4324]{0:T(1024)S(1)} %concatenate.87), channel_id=1, source_target_pairs={{0,1},{1,0},{2,3},{3,2},{4,5},{5,4},{6,7},{7,6},{8,9},{9,8},{10,11... | collective-permute-start | bytes 51896 | tf_op jit(solution)/shard_map/ppermute | solution.py:850
  283.9 7.3 %collective-permute-start.27 = (bf16[1,1,12,1152]{3,2,1,0:T(8,128)(2,1)S(1)}, bf16[1,1,12,1152]{3,2,1,0:T(8,128)(2,1)S(1)}, u32[]{:S(2)}, u32[]{:S(2)}) collective-permute-start(bf16[1,1,12,1152]{3,2,1,0:T(8,128)(2,1)S(1)} %pad_maximum_fusion.11), channel_id=1, source_target_pairs={{0,2},{1,3},{2,0},{3,1},{4,6},{5,7},{6,4},{7,5},{8,10},{9,11},{10,... | collective-permute-start | bytes 82952 | tf_op jit(solution)/shard_map/ppermute | solution.py:847
  291.2 7.1 %collective-permute-start.32 = (bf16[1,2,12,1152]{3,2,1,0:T(8,128)(2,1)S(1)}, bf16[1,2,12,1152]{3,2,1,0:T(8,128)(2,1)S(1)}, u32[]{:S(2)}, u32[]{:S(2)}) collective-permute-start(bf16[1,2,12,1152]{3,2,1,0:T(8,128)(2,1)S(1)} %pad_maximum_fusion.10), channel_id=1, source_target_pairs={{0,8},{4,12},{8,0},{12,4},{16,24},{20,28},{24,16},{28,20},{1,9},{5... | collective-permute-start | bytes 165896 | tf_op jit(solution)/shard_map/ppermute | solution.py:786
  292.7 5.0 %collective-permute-start.26 = (f32[4324]{0:T(1024)S(1)}, f32[4324]{0:T(1024)S(1)}, u32[]{:S(2)}, u32[]{:S(2)}) collective-permute-start(f32[4324]{0:T(1024)S(1)} %add.126), channel_id=1, source_target_pairs={{0,2},{1,3},{2,0},{3,1},{4,6},{5,7},{6,4},{7,5},{8,10},{9,11},{10,... | collective-permute-start | bytes 51896 | tf_op jit(solution)/shard_map/ppermute | solution.py:847
  293.2 10.8 %collective-permute-start.28 = (bf16[1,2,72,576]{3,2,1,0:T(8,128)(2,1)S(1)}, bf16[1,2,72,576]{3,2,1,0:T(8,128)(2,1)S(1)}, u32[]{:S(2)}, u32[]{:S(2)}) collective-permute-start(bf16[1,2,72,576]{3,2,1,0:T(8,128)(2,1)S(1)} %copy-done.51), channel_id=1, source_target_pairs={{0,8},{4,12},{8,0},{12,4},{16,24},{20,28},{24,16},{28,20},{1,9},{5... | collective-permute-start | bytes 497672 | tf_op jit(solution)/shard_map/ppermute | solution.py:748
  293.9 10.8 %collective-permute-start.29 = (bf16[1,2,72,576]{3,2,1,0:T(8,128)(2,1)S(1)}, bf16[1,2,72,576]{3,2,1,0:T(8,128)(2,1)S(1)}, u32[]{:S(2)}, u32[]{:S(2)}) collective-permute-start(bf16[1,2,72,576]{3,2,1,0:T(8,128)(2,1)S(1)} %copy-done.50), channel_id=1, source_target_pairs={{0,4},{4,0},{8,12},{12,8},{16,20},{20,16},{24,28},{28,24},{1,5},{5... | collective-permute-start | bytes 497672 | tf_op jit(solution)/shard_map/ppermute | solution.py:748
  295.2 41.0 %collective-permute-start.35 = (bf16[2,72,1152]{2,1,0:T(8,128)(2,1)}, bf16[2,72,1152]{2,1,0:T(8,128)(2,1)S(1)}, u32[]{:S(2)}, u32[]{:S(2)}) collective-permute-start(bf16[2,72,1152]{2,1,0:T(8,128)(2,1)} %sum_pieces.16), channel_id=1, source_target_pairs={{0,16},{4,20},{8,24},{12,28},{16,0},{20,4},{24,8},{28,12},{1,17},{... | collective-permute-start | bytes 995336 | tf_op jit(solution)/shard_map/ppermute | solution.py:748
  297.7 11.6 %collective-permute-start.30 = (bf16[2,2,72,576]{3,2,1,0:T(8,128)(2,1)S(1)}, bf16[2,2,72,576]{3,2,1,0:T(8,128)(2,1)S(1)}, u32[]{:S(2)}, u32[]{:S(2)}) collective-permute-start(bf16[2,2,72,576]{3,2,1,0:T(8,128)(2,1)S(1)} %copy-done.49), channel_id=1, source_target_pairs={{0,2},{1,3},{2,0},{3,1},{4,6},{5,7},{6,4},{7,5},{8,10},{9,11},{10,... | collective-permute-start | bytes 995336 | tf_op jit(solution)/shard_map/ppermute | solution.py:847
  298.4 18.0 %collective-permute-start.33 = (bf16[144,1152]{1,0:T(8,128)(2,1)S(1)}, bf16[144,1152]{1,0:T(8,128)(2,1)S(1)}, u32[]{:S(2)}, u32[]{:S(2)}) collective-permute-start(bf16[144,1152]{1,0:T(8,128)(2,1)S(1)} %copy-done.27), channel_id=1, source_target_pairs={{0,2},{1,3},{2,0},{3,1},{4,6},{5,7},{6,4},{7,5},{8,10},{9,11},{10,... | collective-permute-start | bytes 995336 | tf_op jit(solution)/shard_map/ppermute | solution.py:847
  304.0 28.8 %collective-permute-start.22 = (bf16[256,1152]{1,0:T(8,128)(2,1)S(1)}, bf16[256,1152]{1,0:T(8,128)(2,1)S(1)}, u32[]{:S(2)}, u32[]{:S(2)}) collective-permute-start(bf16[256,1152]{1,0:T(8,128)(2,1)S(1)} %slice.164), channel_id=1, source_target_pairs={{0,2},{1,3},{2,0},{3,1},{4,6},{5,7},{6,4},{7,5},{8,10},{9,11},{10,... | collective-permute-start | bytes 1769480 | tf_op jit(solution)/shard_map/ppermute | solution.py:847
  313.0 28.2 %collective-permute-start.36 = (bf16[4,72,576]{2,1,0:T(8,128)(2,1)}, bf16[4,72,576]{2,1,0:T(8,128)(2,1)S(1)}, u32[]{:S(2)}, u32[]{:S(2)}) collective-permute-start(bf16[4,72,576]{2,1,0:T(8,128)(2,1)} %sum_pieces.17), channel_id=1, source_target_pairs={{0,16},{4,20},{8,24},{12,28},{16,0},{20,4},{24,8},{28,12},{1,17},{... | collective-permute-start | bytes 995336 | tf_op jit(solution)/shard_map/ppermute | solution.py:748
  314.1 3.8 collective-permute-start.31
  316.4 16.3 %collective-permute-start.40 = (bf16[2,2,12,1152]{3,2,1,0:T(8,128)(2,1)S(1)}, bf16[2,2,12,1152]{3,2,1,0:T(8,128)(2,1)S(1)}, u32[]{:S(2)}, u32[]{:S(2)}) collective-permute-start(bf16[2,2,12,1152]{3,2,1,0:T(8,128)(2,1)S(1)} %pad_maximum_fusion.9), channel_id=1, source_target_pairs={{0,16},{4,20},{8,24},{12,28},{16,0},{20,4},{24,8},{28,12},{1,17},{... | collective-permute-start | bytes 331784 | tf_op jit(solution)/shard_map/ppermute | solution.py:786
  317.9 16.2 %collective-permute-start.34 = (bf16[2,144,1152]{2,1,0:T(8,128)(2,1)S(1)}, bf16[2,144,1152]{2,1,0:T(8,128)(2,1)S(1)}, u32[]{:S(2)}, u32[]{:S(2)}) collective-permute-start(bf16[2,144,1152]{2,1,0:T(8,128)(2,1)S(1)} %maximum_select_fusion), channel_id=1, source_target_pairs={{0,1},{1,0},{2,3},{3,2},{4,5},{5,4},{6,7},{7,6},{8,9},{9,8},{10,11... | collective-permute-start | bytes 1990664 | tf_op jit(solution)/shard_map/ppermute | solution.py:850
  346.2 3.8 collective-permute-start.37
  346.5 12.4 %collective-permute-start.43 = (bf16[4,2,12,1152]{3,2,1,0:T(8,128)(2,1)S(1)}, bf16[4,2,12,1152]{3,2,1,0:T(8,128)(2,1)S(1)}, u32[]{:S(2)}, u32[]{:S(2)}) collective-permute-start(bf16[4,2,12,1152]{3,2,1,0:T(8,128)(2,1)S(1)} %pad_maximum_fusion.7), channel_id=1, source_target_pairs={{0,4},{4,0},{8,12},{12,8},{16,20},{20,16},{24,28},{28,24},{1,5},{5... | collective-permute-start | bytes 663560 | tf_op jit(solution)/shard_map/ppermute | solution.py:786
  350.1 4.9 %collective-permute-start.38 = (f32[4324]{0:T(1024)S(1)}, f32[4324]{0:T(1024)S(1)}, u32[]{:S(2)}, u32[]{:S(2)}) collective-permute-start(f32[4324]{0:T(1024)S(1)} %add.129), channel_id=1, source_target_pairs={{0,16},{4,20},{8,24},{12,28},{16,0},{20,4},{24,8},{28,12},{1,17},{... | collective-permute-start | bytes 51896 | tf_op jit(solution)/shard_map/ppermute | solution.py:804
  351.7 10.8 %collective-permute-start.41 = (bf16[72,2304]{1,0:T(8,128)(2,1)S(1)}, bf16[72,2304]{1,0:T(8,128)(2,1)S(1)}, u32[]{:S(2)}, u32[]{:S(2)}) collective-permute-start(bf16[72,2304]{1,0:T(8,128)(2,1)S(1)} %constant_dynamic-update-slice_fusion.4), channel_id=1, source_target_pairs={{0,2},{1,3},{2,0},{3,1},{4,6},{5,7},{6,4},{7,5},{8,10},{9,11},{10,... | collective-permute-start | bytes 995336 | tf_op jit(solution)/shard_map/ppermute | solution.py:847
  353.6 12.8 %collective-permute-start.39 = (bf16[72,2304]{1,0:T(8,128)(2,1)S(1)}, bf16[72,2304]{1,0:T(8,128)(2,1)S(1)}, u32[]{:S(2)}, u32[]{:S(2)}) collective-permute-start(bf16[72,2304]{1,0:T(8,128)(2,1)S(1)} %concatenate.92), channel_id=1, source_target_pairs={{0,2},{1,3},{2,0},{3,1},{4,6},{5,7},{6,4},{7,5},{8,10},{9,11},{10,... | collective-permute-start | bytes 995336 | tf_op jit(solution)/shard_map/ppermute | solution.py:847
  366.4 2.2 collective-permute-start.42
  366.7 4.3 %collective-permute-start.44 = (bf16[144,2304]{1,0:T(8,128)(2,1)S(1)}, bf16[144,2304]{1,0:T(8,128)(2,1)S(1)}, u32[]{:S(2)}, u32[]{:S(2)}) collective-permute-start(bf16[144,2304]{1,0:T(8,128)(2,1)S(1)} %pad_maximum_fusion.5), channel_id=1, source_target_pairs={{0,1},{1,0},{2,3},{3,2},{4,5},{5,4},{6,7},{7,6},{8,9},{9,8},{10,11... | collective-permute-start | bytes 1990664 | tf_op jit(solution)/shard_map/ppermute | solution.py:850
  (50 other events, 231.2 us)
Sparse Core Ops, SparseCore 0:
  100.0 175.1 reduce-scatter.1

commit v3 on v2

--- a/solution.py
+++ b/solution.py
@@ -1003,7 +1003,7 @@
         clock,
         part[None, None],
         [(swap_core, c == 1, 3), (swap_y, y == 1, 1)]
-        + [(swaps[k], img_bits[k], 0) for k in [*range(1, bits), 0]],
+        + [(swaps[k], img_bits[k], 0) for k in range(bits)],
     )
     gather.tick()
     w_part = project_weights(clock.now, attn_in, d)
@@ -1013,6 +1013,7 @@
     jobs_qkv = [by_row(dims, (w_part,), cols, prefix=(p,)) for p, dims in enumerate(orders)]
     step(jobs_qkv)
     jobs_qkv.append(job_proj)
+    gather.tick()
     back, back_far = project_back(clock.now, core, d, w_qkv, mine)
     clock.passed(back)
     step(jobs_up)

time: 389 us -> 399 us (1.026)
  waiting for transfers between devices: 55.4 us -> 64.6 us
    ppermute x3, waiting for transfers between devices: 14.8 us -> 24.6 us  [tick(): self.far = swap(self.clock.tie(self.part))]
    unnamed x112 -> x122, local copies, waits for them, and re-layouts: 12.7 us -> 14.8 us
  transfers between devices with their start and end apart: 46 -> 46, of which waited for: 17 -> 18; matrix products, arithmetic and copies ran while one was open for 13% -> 13% of each run, Pallas kernels for 43% -> 41%
where the time goes in v3:
time: 399 us; the launch traced here: 395 us
  Pallas kernels  194 us (49%)
  waiting for transfers between devices  64.6 us (16%)
  local copies, waits for them, and re-layouts  46.6 us (12%)
  starting transfers between devices  38.5 us (10%)
  matrix products  19 us (5%)
  other arithmetic  16.7 us (4%)
  between operations  15.7 us (4%)
    pallas_call x10, Pallas kernels, advance(): pl.pallas_call(functools.partial(sum_kernel, counts=counts, places=places...  37.1 us
    pallas_call x1, Pallas kernels, mlp_fall(): pl.pallas_call(fall_kernel, grid_spec=pltpu.PrefetchScalarGridSpec(num_sc...  29.7 us
    pallas_call x1, Pallas kernels, mlp_rise(): pl.pallas_call(rise_kernel, grid=(ff // tile,), in_specs=[pl.BlockSpec((r...  27.4 us
    pallas_call x1, Pallas kernels, attend_backward(): pl.pallas_call(functools.partial(backward_kernel, scale=scale), grid_spec...  27.2 us
    ppermute x3, waiting for transfers between devices, tick(): self.far = swap(self.clock.tie(self.part))  24.6 us
    pallas_call x2, Pallas kernels, attend_forward(): pl.pallas_call(forward_kernel, grid_spec=pltpu.PrefetchScalarGridSpec(num...  18.5 us
    ppermute x13, waiting for transfers between devices, advance(): total = swaps[key[0]](total)  16.9 us
    ppermute x14, starting transfers between devices, swap_y(): return lax.ppermute(a, 'seq', over_y)  15.6 us
  transfers between devices with their start and end apart: 46, of which 18 were waited for; matrix products, arithmetic and copies ran while one was open for 13% of the time, Pallas kernels for 41%

profile of v3, /device:TPU:0, one launch (start us, length us, event | category | flops | bytes accessed | tf_op | source)
XLA Modules:
  0.0 395.1 jit_solution(13918958365238779453)
XLA Ops:
  7.3 2.3 dynamic-slice_bitcast_fusion
  9.6 3.0 collective-permute-start
  13.8 2.2 fusion.28
  23.9 2.3 dynamic-slice_bitcast_fusion.2
  29.2 14.0 %project.1 = (bf16[1024,1152]{1,0:T(8,128)(2,1)}, bf16[512,1152]{1,0:T(8,128)(2,1)}, bf16[3,8,72,1024]{3,2,1,0:T(8,128)(2,1)}) custom-call(s32[1]{0:T(128)} %bitcast.4.core_ref, bf16[256,1152]{1,0:T(8,128)(2,1)} %copy-done.23, bf16[256,1152]{1,0:T(8,128)(2,1)} %collective-permute-done.b_ref, bf16[256,1152]{1,0:T(8,128)(2,1)} %collective-permute-done.1.c_ref, ...), custom_call_target="tpu_custom_call" | custom-call | flops 1000000 | bytes 100000 | tf_op jit(solution)/shard_map/project/pallas_call | solution.py:164
  43.2 9.2 %attention_forward.2 = (bf16[4,72,1024]{2,1,0:T(8,128)(2,1)}, f32[4,1,1024]{2,1,0:T(1,128)}) custom-call(s32[5]{0:T(128)} %stack.95.clock_ref.coord_ref, bf16[3,8,72,1024]{3,2,1,0:T(8,128)(2,1)} %get-tuple-element.115.p_ref.qkv_ref, bf16[8,64,64]{2,1,0:T(8,128)(2,1)} %fusion.22.table_ref, bf16[112,1024]{1,0:T(8,128)(2,1)} %get-tuple-element.112.feat_ref), custom_call_target="tpu_custom_call" | custom-call | flops 1000000 | bytes 100000 | tf_op jit(solution)/shard_map/attention_forward/pallas_call | solution.py:323
  52.7 9.3 %attention_forward.3 = (bf16[4,72,1024]{2,1,0:T(8,128)(2,1)}, f32[4,1,1024]{2,1,0:T(1,128)}) custom-call(s32[5]{0:T(128)} %stack.95.clock_ref.coord_ref, bf16[3,8,72,1024]{3,2,1,0:T(8,128)(2,1)} %get-tuple-element.115.p_ref.qkv_ref, bf16[8,64,64]{2,1,0:T(8,128)(2,1)} %fusion.22.table_ref, bf16[112,1024]{1,0:T(8,128)(2,1)} %get-tuple-element.112.feat_ref), custom_call_target="tpu_custom_call" | custom-call | flops 1000000 | bytes 100000 | tf_op jit(solution)/shard_map/attention_forward/pallas_call | solution.py:323
  67.2 3.4 fusion.45
  72.4 27.4 %feed_forward_rise.1 = (f32[512,1152]{1,0:T(8,128)}, bf16[512,4608]{1,0:T(8,128)(2,1)}, bf16[4608,1152]{1,0:T(8,128)(2,1)}, bf16[1152,512]{1,0:T(8,128)(2,1)}, bf16[512,1152]{1,0:T(8,128)(2,1)}) custom-call(bf16[512,1152]{1,0:T(8,128)(2,1)} %multiply_convert_fusion.m_ref, bf16[256,1152]{1,0:T(8,128)(2,1)} %get-tuple-element.239.near_ref, ...), custom_call_target="tpu_custom_call" | custom-call | flops 1000000 | bytes 100000 | tf_op jit(solution)/shard_map/feed_forward_rise/pallas_call | solution.py:468
  99.9 29.7 %feed_forward_fall.1 = (f32[512,1152]{1,0:T(8,128)}, bf16[1152,2304]{1,0:T(8,128)(2,1)}, bf16[1152,2304]{1,0:T(8,128)(2,1)}) custom-call(s32[5]{0:T(128)} %stack.95.clock_ref.coord_ref, s32[2]{0:T(128)} %pad_add_fusion.1.tile_ref, bf16[1152,512]{1,0:T(8,128)(2,1)} %get-tuple-element.127.mt_ref, bf16[512,1152]{1,0:T(8,128)(2,1)} %get-tuple-element.128.g_ref, ...), custom_call_target="tpu_custom_call" | custom-call | flops 1000000 | bytes 100000 | tf_op jit(solution)/shard_map/feed_forward_fall/pallas_call | solution.py:526
  129.5 9.2 %middle.1 = (bf16[512,1152]{1,0:T(8,128)(2,1)}, f32[512,1152]{1,0:T(8,128)}, bf16[512,1152]{1,0:T(8,128)(2,1)}, f32[8,1152]{1,0:T(8,128)}) custom-call(s32[5]{0:T(128)} %stack.95.clock_ref.coord_ref, f32[512,1152]{1,0:T(8,128)} %get-tuple-element.130.gm_ref, f32[512,1152]{1,0:T(8,128)} %get-tuple-element.125.two_ref, ...), custom_call_target="tpu_custom_call" | custom-call | flops 1000000 | bytes 100000 | tf_op jit(solution)/shard_map/middle/pallas_call | solution.py:600
  139.1 3.1 collective-permute-done.7
  142.5 1.9 slice.161
  146.8 3.2 convolution_convert_fusion
  150.0 2.6 copy.45
  152.6 4.4 %convolution_convert_fusion.1 = bf16[576,1024]{1,0:T(8,128)(2,1)} fusion(bf16[1024,1152]{1,0:T(8,128)(2,1)} %copy-done.37, bf16[1152,1152]{1,0:T(8,128)(2,1)S(1)} %copy-done, s32[]{:T(128)S(6)} %select_n.199), kind=kOutput, calls=%fused_computation.10 | convolution fusion | flops 1359544320 | bytes 4866052 | tf_op jit(solution)/shard_map/dot_general | solution.py:30
  157.0 3.0 collective-permute-done.6
  160.1 5.7 %sum_pieces.10 = (bf16[1,2,2,2,72,1152]{5,4,3,2,1,0:T(8,128)(2,1)}, bf16[1,2,2,2,72,1152]{5,4,3,2,1,0:T(8,128)(2,1)}, bf16[1,2,2,2,72,576]{5,4,3,2,1,0:T(8,128)(2,1)}) custom-call(s32[5]{0:T(128)} %stack.95.clock_ref.coord_ref, bf16[2,2,2,2,72,2304]{5,4,3,2,1,0:T(8,128)(2,1)} %bitcast.126, ...), custom_call_target="tpu_custom_call" | custom-call | flops 1000000 | bytes 100000 | tf_op jit(solution)/shard_map/sum_pieces/pallas_call | solution.py:733
  171.0 2.0 collective-permute-start.11
  172.9 27.2 %attention_backward.1 = (bf16[3,8,72,1024]{3,2,1,0:T(8,128)(2,1)}, f32[8,64,64]{2,1,0:T(8,128)}, f32[2,8,16,72]{3,2,1,0:T(8,128)}) custom-call(s32[5]{0:T(128)} %stack.95.clock_ref.coord_ref, bf16[3,8,72,1024]{3,2,1,0:T(8,128)(2,1)} %get-tuple-element.115.p_ref.qkv_ref, bf16[8,72,1024]{2,1,0:T(8,128)(2,1)} %copy-done.10, bf16[8,72,1024]{2,1,0:T(8,128)(2,1)} %bitcast.146, ...), custom_call_target="tpu_custom_call" | custom-call | flops 1000000 | bytes 100000 | tf_op jit(solution)/shard_map/attention_backward/pallas_call | solution.py:400
  201.7 4.2 %collective-permute-done.9.refs_2_ = bf16[1,2,2,2,72,1152]{5,4,3,2,1,0:T(8,128)(2,1)S(1)} collective-permute-done((bf16[1,2,2,2,72,1152]{5,4,3,2,1,0:T(8,128)(2,1)}, bf16[1,2,2,2,72,1152]{5,4,3,2,1,0:T(8,128)(2,1)S(1)}, u32[]{:S(2)}, u32[]{:S(2)}) %collective-permute-start.9) | collective-permute-done | bytes 1327136 | tf_op jit(solution)/shard_map/ppermute | solution.py:748
  208.1 3.8 sum_pieces.11
  214.5 10.0 %project_weights.1 = bf16[3,1152,576]{2,1,0:T(8,128)(2,1)} custom-call(s32[5]{0:T(128)} %stack.95.clock_ref.coord_ref, bf16[1024,1152]{1,0:T(8,128)(2,1)} %get-tuple-element.151.in_ref, bf16[3,8,72,1024]{3,2,1,0:T(8,128)(2,1)} %get-tuple-element.146.d_ref), custom_call_target="tpu_custom_call" | custom-call | flops 1000000 | bytes 100000 | tf_op jit(solution)/shard_map/project_weights/pallas_call | solution.py:206
  225.3 4.7 %sum_pieces.12 = (bf16[1,2,2,2,72,576]{5,4,3,2,1,0:T(8,128)(2,1)}, bf16[1,2,2,2,72,576]{5,4,3,2,1,0:T(8,128)(2,1)}, bf16[1,2,2,2,72,576]{5,4,3,2,1,0:T(8,128)(2,1)}) custom-call(s32[5]{0:T(128)} %stack.95.clock_ref.coord_ref, bf16[3,2,2,2,2,72,576]{6,5,4,3,2,1,0:T(8,128)(2,1)} %bitcast.111, bf16[3,2,2,2,2,72,576]{6,5,4,3,2,1,0:T(8,128)(2,1)} %bitcast.112, ...), custom_call_target="tpu_custom_call" | custom-call | flops 1000000 | bytes 100000 | tf_op jit(solution)/shard_map/sum_pieces/pallas_call | solution.py:733
  233.0 13.6 %project_back.1 = (f32[512,1152]{1,0:T(8,128)}, bf16[512,1152]{1,0:T(8,128)(2,1)}) custom-call(s32[5]{0:T(128)} %stack.95.clock_ref.coord_ref, s32[1]{0:T(128)} %bitcast.4.core_ref, bf16[3,8,72,1024]{3,2,1,0:T(8,128)(2,1)} %get-tuple-element.146.d_ref, bf16[1152,3456]{1,0:T(8,128)(2,1)} %w_ref.3), custom_call_target="tpu_custom_call" | custom-call | flops 1000000 | bytes 100000 | tf_op jit(solution)/shard_map/project_back/pallas_call | solution.py:266
  248.2 3.4 sum_pieces.13
  252.4 1.8 collective-permute-start.22
  255.4 4.8 %collective-permute-done.18.refs_5_.refs_7_.refs_9_.refs_11_ = bf16[1,2,2,2,72,576]{5,4,3,2,1,0:T(8,128)(2,1)S(1)} collective-permute-done((bf16[1,2,2,2,72,576]{5,4,3,2,1,0:T(8,128)(2,1)}, bf16[1,2,2,2,72,576]{5,4,3,2,1,0:T(8,128)(2,1)S(1)}, u32[]{:S(2)}, u32[]{:S(2)}) %collective-permute-start.18) | collective-permute-done | bytes 663584 | tf_op jit(solution)/shard_map/ppermute | solution.py:748
  261.1 3.6 sum_pieces.14
  270.2 5.7 %last.1 = (bf16[512,1152]{1,0:T(8,128)(2,1)}, f32[8,1152]{1,0:T(8,128)}) custom-call(f32[512,1152]{1,0:T(8,128)} %get-tuple-element.160.back_ref, bf16[512,1152]{1,0:T(8,128)(2,1)} %collective-permute-done.15.far_ref, bf16[512,1152]{1,0:T(8,128)(2,1)} %get-tuple-element.122.x_ref, f32[512,1152]{1,0:T(8,128)} %get-tuple-element.167.grad_ref, ...), custom_call_target="tpu_custom_call" | custom-call | flops 1000000 | bytes 100000 | tf_op jit(solution)/shard_map/last/pallas_call | solution.py:639
  279.3 3.6 collective-permute-done.21.refs_8_.refs_11_.refs_10_.refs_14_.refs_12_.refs_17_
  283.8 3.3 sum_pieces.15
  290.3 3.1 sum_pieces.16
  295.3 1.6 collective-permute-start.29
  300.0 3.9 collective-permute-done.33
  304.1 2.7 collective-permute-done.29.refs_3_
  307.3 3.1 collective-permute-done.31.refs_11_.refs_15_.refs_13_.refs_18_
  311.1 3.0 sum_pieces.17
  314.2 2.6 collective-permute-start.37
  317.5 2.6 collective-permute-start.41
  320.5 20.7 %collective-permute-done.41 = bf16[4,2,12,1152]{3,2,1,0:T(8,128)(2,1)S(1)} collective-permute-done((bf16[4,2,12,1152]{3,2,1,0:T(8,128)(2,1)S(1)}, bf16[4,2,12,1152]{3,2,1,0:T(8,128)(2,1)S(1)}, u32[]{:S(2)}, u32[]{:S(2)}) %collective-permute-start.41) | collective-permute-done | bytes 221216 | tf_op jit(solution)/shard_map/ppermute | solution.py:786
  345.6 1.7 pad_maximum_fusion
  348.0 3.2 sum_pieces.18
  353.0 3.2 sum_pieces.19
  357.3 3.7 collective-permute-done.38
  369.7 3.2 collective-permute-done.42
  372.8 3.6 collective-permute-done.40
  384.0 4.0 %concatenate.97 = f32[144,3456]{1,0:T(8,128)} concatenate(f32[144,576]{1,0:T(8,128)} %get-tuple-element.224, f32[144,576]{1,0:T(8,128)} %get-tuple-element.228, f32[144,576]{1,0:T(8,128)} %get-tuple-element.223, f32[144,576]{1,0:T(8,128)S(1)} %get-tuple-element.227, f32[144,576]{1,0:T(8,128)} %get-tuple-element.222, f32[144,576]{1,0:T(8,128)S(1)} %get-tuple-element.226), dimensions={1} | concatenate | bytes 3981312 | tf_op jit(solution)/shard_map/concatenate | solution.py:1097
  (289 shorter events, 85.9 us)
Async XLA Ops:
  7.2 59.5 %copy-start = (bf16[1152,1152]{1,0:T(8,128)(2,1)S(1)}, bf16[1152,1152]{1,0:T(8,128)(2,1)}, u32[]{:S(2)}) copy-start(bf16[1152,1152]{1,0:T(8,128)(2,1)} %param.25) | copy-start | bytes 7962628
  7.2 270.2 %reduce-scatter.2.cloned.1.call-start = ((), (), s32[]{:S(2)}) async-start(), calls=%async_computation.1 | async-start | bytes 10948608 | tf_op jit(solution)/shard_map/reduce_scatter | solution.py:948
  9.6 16.7 %collective-permute-start = (bf16[256,1152]{1,0:T(8,128)(2,1)}, bf16[256,1152]{1,0:T(8,128)(2,1)}, u32[]{:S(2)}, u32[]{:S(2)}) collective-permute-start(bf16[256,1152]{1,0:T(8,128)(2,1)} %get-tuple-element.237), channel_id=1, source_target_pairs={{0,2},{1,3},{2,0},{3,1},{4,6},{5,7},{6,4},{7,5},{8,10},{9,11},{10,... | collective-permute-start | bytes 1769480 | tf_op jit(solution)/shard_map/ppermute | solution.py:847
  12.6 16.6 %collective-permute-start.1 = (bf16[256,1152]{1,0:T(8,128)(2,1)S(1)}, bf16[256,1152]{1,0:T(8,128)(2,1)}, u32[]{:S(2)}, u32[]{:S(2)}) collective-permute-start(bf16[256,1152]{1,0:T(8,128)(2,1)S(1)} %get-tuple-element.238.a_ref), channel_id=1, source_target_pairs={{0,1},{1,0},{2,3},{3,2},{4,5},{5,4},{6,7},{7,6},{8,9},{9,8},{10,11... | collective-permute-start | bytes 1769480 | tf_op jit(solution)/shard_map/ppermute | solution.py:850
  26.3 2.9 collective-permute-start.2
  26.8 25.9 %collective-permute-start.3 = (bf16[256,1152]{1,0:T(8,128)(2,1)}, bf16[256,1152]{1,0:T(8,128)(2,1)}, u32[]{:S(2)}, u32[]{:S(2)}) collective-permute-start(bf16[256,1152]{1,0:T(8,128)(2,1)} %get-tuple-element.118), channel_id=1, source_target_pairs={{0,2},{1,3},{2,0},{3,1},{4,6},{5,7},{6,4},{7,5},{8,10},{9,11},{10,... | collective-permute-start | bytes 1769480 | tf_op jit(solution)/shard_map/ppermute | solution.py:847
  52.4 12.0 %collective-permute-start.4 = (bf16[4,72,1024]{2,1,0:T(8,128)(2,1)}, bf16[4,72,1024]{2,1,0:T(8,128)(2,1)S(1)}, u32[]{:S(2)}, u32[]{:S(2)}) collective-permute-start(bf16[4,72,1024]{2,1,0:T(8,128)(2,1)} %get-tuple-element.117), channel_id=1, source_target_pairs={{0,1},{1,0},{2,3},{3,2},{4,5},{5,4},{6,7},{7,6},{8,9},{9,8},{10,11... | collective-permute-start | bytes 1769480 | tf_op jit(solution)/shard_map/ppermute | solution.py:850
  61.9 2.6 collective-permute-start.5
  138.8 3.4 collective-permute-start.7
  142.1 17.9 %collective-permute-start.8 = (bf16[1152,2304]{1,0:T(8,128)(2,1)}, bf16[1152,2304]{1,0:T(8,128)(2,1)}, u32[]{:S(2)}, u32[]{:S(2)}) collective-permute-start(bf16[1152,2304]{1,0:T(8,128)(2,1)} %get-tuple-element.139), channel_id=1, source_target_pairs={{0,1},{1,0},{2,3},{3,2},{4,5},{5,4},{6,7},{7,6},{8,9},{9,8},{10,11... | collective-permute-start | bytes 15925256 | tf_op jit(solution)/shard_map/ppermute | solution.py:850
  144.4 15.6 %collective-permute-start.6 = (bf16[256,1152]{1,0:T(8,128)(2,1)}, bf16[256,1152]{1,0:T(8,128)(2,1)S(1)}, u32[]{:S(2)}, u32[]{:S(2)}) collective-permute-start(bf16[256,1152]{1,0:T(8,128)(2,1)} %slice.161), channel_id=1, source_target_pairs={{0,2},{1,3},{2,0},{3,1},{4,6},{5,7},{6,4},{7,5},{8,10},{9,11},{10,... | collective-permute-start | bytes 1769480 | tf_op jit(solution)/shard_map/ppermute | solution.py:847
  165.8 40.1 %collective-permute-start.9 = (bf16[1,2,2,2,72,1152]{5,4,3,2,1,0:T(8,128)(2,1)}, bf16[1,2,2,2,72,1152]{5,4,3,2,1,0:T(8,128)(2,1)S(1)}, u32[]{:S(2)}, u32[]{:S(2)}) collective-permute-start(bf16[1,2,2,2,72,1152]{5,4,3,2,1,0:T(8,128)(2,1)} %get-tuple-element.140), channel_id=1, source_target_pairs={{0,4},{4,0},{8,12},{12,8},{16,20},{20,16},{24,28},{28,24},{1,5},{5... | collective-permute-start | bytes 3981320 | tf_op jit(solution)/shard_map/ppermute | solution.py:748
  167.2 38.8 %collective-permute-start.10 = (bf16[1,2,2,2,72,1152]{5,4,3,2,1,0:T(8,128)(2,1)}, bf16[1,2,2,2,72,1152]{5,4,3,2,1,0:T(8,128)(2,1)S(1)}, u32[]{:S(2)}, u32[]{:S(2)}) collective-permute-start(bf16[1,2,2,2,72,1152]{5,4,3,2,1,0:T(8,128)(2,1)} %get-tuple-element.141), channel_id=1, source_target_pairs={{0,2},{1,3},{2,0},{3,1},{4,6},{5,7},{6,4},{7,5},{8,10},{9,11},{10,... | collective-permute-start | bytes 3981320 | tf_op jit(solution)/shard_map/ppermute | solution.py:847
  171.0 53.5 %collective-permute-start.11 = (bf16[1,2,2,2,72,576]{5,4,3,2,1,0:T(8,128)(2,1)}, bf16[1,2,2,2,72,576]{5,4,3,2,1,0:T(8,128)(2,1)S(1)}, u32[]{:S(2)}, u32[]{:S(2)}) collective-permute-start(bf16[1,2,2,2,72,576]{5,4,3,2,1,0:T(8,128)(2,1)} %get-tuple-element.142), channel_id=1, source_target_pairs={{0,8},{4,12},{8,0},{12,4},{16,24},{20,28},{24,16},{28,20},{1,9},{5... | collective-permute-start | bytes 1990664 | tf_op jit(solution)/shard_map/ppermute | solution.py:748
  211.9 12.7 %collective-permute-start.12 = (bf16[1,1,8,576]{3,2,1,0:T(8,128)(2,1)}, bf16[1,1,8,576]{3,2,1,0:T(8,128)(2,1)S(1)}, u32[]{:S(2)}, u32[]{:S(2)}) collective-permute-start(bf16[1,1,8,576]{3,2,1,0:T(8,128)(2,1)} %convert_element_type.61), channel_id=1, source_target_pairs={{0,1},{1,0},{2,3},{3,2},{4,5},{5,4},{6,7},{7,6},{8,9},{9,8},{10,11... | collective-permute-start | bytes 27656 | tf_op jit(solution)/shard_map/ppermute | solution.py:850
  213.0 33.6 %collective-permute-start.13 = (bf16[1,2,2,72,1152]{4,3,2,1,0:T(8,128)(2,1)S(1)}, bf16[1,2,2,72,1152]{4,3,2,1,0:T(8,128)(2,1)S(1)}, u32[]{:S(2)}, u32[]{:S(2)}) collective-permute-start(bf16[1,2,2,72,1152]{4,3,2,1,0:T(8,128)(2,1)S(1)} %copy-done.54), channel_id=1, source_target_pairs={{0,8},{4,12},{8,0},{12,4},{16,24},{20,28},{24,16},{28,20},{1,9},{5... | collective-permute-start | bytes 1990664 | tf_op jit(solution)/shard_map/ppermute | solution.py:748
  213.4 33.2 %collective-permute-start.14 = (bf16[1,2,2,72,1152]{4,3,2,1,0:T(8,128)(2,1)S(1)}, bf16[1,2,2,72,1152]{4,3,2,1,0:T(8,128)(2,1)S(1)}, u32[]{:S(2)}, u32[]{:S(2)}) collective-permute-start(bf16[1,2,2,72,1152]{4,3,2,1,0:T(8,128)(2,1)S(1)} %copy-done.53), channel_id=1, source_target_pairs={{0,4},{4,0},{8,12},{12,8},{16,20},{20,16},{24,28},{28,24},{1,5},{5... | collective-permute-start | bytes 1990664 | tf_op jit(solution)/shard_map/ppermute | solution.py:748
  225.3 26.4 %copy-start.39 = (bf16[1,1,8,1152]{3,2,1,0:T(8,128)(2,1)}, bf16[1,1,8,1152]{3,2,1,0:T(8,128)(2,1)S(1)}, u32[]{:S(2)}) copy-start(bf16[1,1,8,1152]{3,2,1,0:T(8,128)(2,1)S(1)} %pad_maximum_fusion.14) | copy-start | bytes 55300
  230.0 25.4 %collective-permute-start.16 = (bf16[1,2,2,2,72,576]{5,4,3,2,1,0:T(8,128)(2,1)}, bf16[1,2,2,2,72,576]{5,4,3,2,1,0:T(8,128)(2,1)S(1)}, u32[]{:S(2)}, u32[]{:S(2)}) collective-permute-start(bf16[1,2,2,2,72,576]{5,4,3,2,1,0:T(8,128)(2,1)} %get-tuple-element.156), channel_id=1, source_target_pairs={{0,4},{4,0},{8,12},{12,8},{16,20},{20,16},{24,28},{28,24},{1,5},{5... | collective-permute-start | bytes 1990664 | tf_op jit(solution)/shard_map/ppermute | solution.py:748
  231.0 24.4 %collective-permute-start.17 = (bf16[1,2,2,2,72,576]{5,4,3,2,1,0:T(8,128)(2,1)}, bf16[1,2,2,2,72,576]{5,4,3,2,1,0:T(8,128)(2,1)S(1)}, u32[]{:S(2)}, u32[]{:S(2)}) collective-permute-start(bf16[1,2,2,2,72,576]{5,4,3,2,1,0:T(8,128)(2,1)} %get-tuple-element.157), channel_id=1, source_target_pairs={{0,2},{1,3},{2,0},{3,1},{4,6},{5,7},{6,4},{7,5},{8,10},{9,11},{10,... | collective-permute-start | bytes 1990664 | tf_op jit(solution)/shard_map/ppermute | solution.py:847
  231.5 28.8 %collective-permute-start.18 = (bf16[1,2,2,2,72,576]{5,4,3,2,1,0:T(8,128)(2,1)}, bf16[1,2,2,2,72,576]{5,4,3,2,1,0:T(8,128)(2,1)S(1)}, u32[]{:S(2)}, u32[]{:S(2)}) collective-permute-start(bf16[1,2,2,2,72,576]{5,4,3,2,1,0:T(8,128)(2,1)} %get-tuple-element.158), channel_id=1, source_target_pairs={{0,8},{4,12},{8,0},{12,4},{16,24},{20,28},{24,16},{28,20},{1,9},{5... | collective-permute-start | bytes 1990664 | tf_op jit(solution)/shard_map/ppermute | solution.py:748
  251.7 17.5 %collective-permute-start.15 = (bf16[512,1152]{1,0:T(8,128)(2,1)}, bf16[512,1152]{1,0:T(8,128)(2,1)}, u32[]{:S(2)}, u32[]{:S(2)}) collective-permute-start(bf16[512,1152]{1,0:T(8,128)(2,1)} %get-tuple-element.166), channel_id=1, source_target_pairs={{0,1},{1,0},{2,3},{3,2},{4,5},{5,4},{6,7},{7,6},{8,9},{9,8},{10,11... | collective-permute-start | bytes 3538952 | tf_op jit(solution)/shard_map/ppermute | solution.py:850
  252.4 12.8 %collective-permute-start.22 = (bf16[1,1,12,1152]{3,2,1,0:T(8,128)(2,1)}, bf16[1,1,12,1152]{3,2,1,0:T(8,128)(2,1)}, u32[]{:S(2)}, u32[]{:S(2)}) collective-permute-start(bf16[1,1,12,1152]{3,2,1,0:T(8,128)(2,1)} %pad_maximum_fusion.11), channel_id=1, source_target_pairs={{0,2},{1,3},{2,0},{3,1},{4,6},{5,7},{6,4},{7,5},{8,10},{9,11},{10,... | collective-permute-start | bytes 82952 | tf_op jit(solution)/shard_map/ppermute | solution.py:847
  264.7 18.2 %collective-permute-start.21 = (bf16[2,2,2,72,576]{4,3,2,1,0:T(8,128)(2,1)}, bf16[2,2,2,72,576]{4,3,2,1,0:T(8,128)(2,1)S(1)}, u32[]{:S(2)}, u32[]{:S(2)}) collective-permute-start(bf16[2,2,2,72,576]{4,3,2,1,0:T(8,128)(2,1)} %get-tuple-element.171), channel_id=1, source_target_pairs={{0,4},{4,0},{8,12},{12,8},{16,20},{20,16},{24,28},{28,24},{1,5},{5... | collective-permute-start | bytes 1990664 | tf_op jit(solution)/shard_map/ppermute | solution.py:748
  266.0 11.8 %collective-permute-start.19 = (bf16[1,2,2,72,576]{4,3,2,1,0:T(8,128)(2,1)}, bf16[1,2,2,72,576]{4,3,2,1,0:T(8,128)(2,1)S(1)}, u32[]{:S(2)}, u32[]{:S(2)}) collective-permute-start(bf16[1,2,2,72,576]{4,3,2,1,0:T(8,128)(2,1)} %get-tuple-element.169), channel_id=1, source_target_pairs={{0,2},{1,3},{2,0},{3,1},{4,6},{5,7},{6,4},{7,5},{8,10},{9,11},{10,... | collective-permute-start | bytes 995336 | tf_op jit(solution)/shard_map/ppermute | solution.py:847
  267.4 12.0 %collective-permute-start.20 = (bf16[1,2,2,72,576]{4,3,2,1,0:T(8,128)(2,1)}, bf16[1,2,2,72,576]{4,3,2,1,0:T(8,128)(2,1)S(1)}, u32[]{:S(2)}, u32[]{:S(2)}) collective-permute-start(bf16[1,2,2,72,576]{4,3,2,1,0:T(8,128)(2,1)} %get-tuple-element.170), channel_id=1, source_target_pairs={{0,8},{4,12},{8,0},{12,4},{16,24},{20,28},{24,16},{28,20},{1,9},{5... | collective-permute-start | bytes 995336 | tf_op jit(solution)/shard_map/ppermute | solution.py:748
  267.9 20.9 %collective-permute-start.25 = (bf16[1,2,72,1152]{3,2,1,0:T(8,128)(2,1)}, bf16[1,2,72,1152]{3,2,1,0:T(8,128)(2,1)S(1)}, u32[]{:S(2)}, u32[]{:S(2)}) collective-permute-start(bf16[1,2,72,1152]{3,2,1,0:T(8,128)(2,1)} %get-tuple-element.163), channel_id=1, source_target_pairs={{0,2},{1,3},{2,0},{3,1},{4,6},{5,7},{6,4},{7,5},{8,10},{9,11},{10,... | collective-permute-start | bytes 995336 | tf_op jit(solution)/shard_map/ppermute | solution.py:847
  269.2 19.6 %collective-permute-start.26 = (bf16[1,2,72,1152]{3,2,1,0:T(8,128)(2,1)}, bf16[1,2,72,1152]{3,2,1,0:T(8,128)(2,1)S(1)}, u32[]{:S(2)}, u32[]{:S(2)}) collective-permute-start(bf16[1,2,72,1152]{3,2,1,0:T(8,128)(2,1)} %get-tuple-element.164), channel_id=1, source_target_pairs={{0,8},{4,12},{8,0},{12,4},{16,24},{20,28},{24,16},{28,20},{1,9},{5... | collective-permute-start | bytes 995336 | tf_op jit(solution)/shard_map/ppermute | solution.py:748
  277.8 15.6 %collective-permute-start.24 = (f32[4324]{0:T(1024)S(1)}, f32[4324]{0:T(1024)S(1)}, u32[]{:S(2)}, u32[]{:S(2)}) collective-permute-start(f32[4324]{0:T(1024)S(1)} %concatenate.89), channel_id=1, source_target_pairs={{0,1},{1,0},{2,3},{3,2},{4,5},{5,4},{6,7},{7,6},{8,9},{9,8},{10,11... | collective-permute-start | bytes 51896 | tf_op jit(solution)/shard_map/ppermute | solution.py:850
  287.2 6.2 %collective-permute-start.28 = (bf16[1,2,12,1152]{3,2,1,0:T(8,128)(2,1)S(1)}, bf16[1,2,12,1152]{3,2,1,0:T(8,128)(2,1)S(1)}, u32[]{:S(2)}, u32[]{:S(2)}) collective-permute-start(bf16[1,2,12,1152]{3,2,1,0:T(8,128)(2,1)S(1)} %pad_maximum_fusion.10), channel_id=1, source_target_pairs={{0,4},{4,0},{8,12},{12,8},{16,20},{20,16},{24,28},{28,24},{1,5},{5... | collective-permute-start | bytes 165896 | tf_op jit(solution)/shard_map/ppermute | solution.py:786
  293.5 10.5 %collective-permute-start.33 = (bf16[2,2,12,1152]{3,2,1,0:T(8,128)(2,1)S(1)}, bf16[2,2,12,1152]{3,2,1,0:T(8,128)(2,1)S(1)}, u32[]{:S(2)}, u32[]{:S(2)}) collective-permute-start(bf16[2,2,12,1152]{3,2,1,0:T(8,128)(2,1)S(1)} %pad_maximum_fusion.9), channel_id=1, source_target_pairs={{0,8},{4,12},{8,0},{12,4},{16,24},{20,28},{24,16},{28,20},{1,9},{5... | collective-permute-start | bytes 331784 | tf_op jit(solution)/shard_map/ppermute | solution.py:786
  294.5 4.3 %collective-permute-start.27 = (f32[4324]{0:T(1024)S(1)}, f32[4324]{0:T(1024)S(1)}, u32[]{:S(2)}, u32[]{:S(2)}) collective-permute-start(f32[4324]{0:T(1024)S(1)} %add.126), channel_id=1, source_target_pairs={{0,2},{1,3},{2,0},{3,1},{4,6},{5,7},{6,4},{7,5},{8,10},{9,11},{10,... | collective-permute-start | bytes 51896 | tf_op jit(solution)/shard_map/ppermute | solution.py:847
  295.3 11.5 %collective-permute-start.29 = (bf16[1,2,72,576]{3,2,1,0:T(8,128)(2,1)}, bf16[1,2,72,576]{3,2,1,0:T(8,128)(2,1)S(1)}, u32[]{:S(2)}, u32[]{:S(2)}) collective-permute-start(bf16[1,2,72,576]{3,2,1,0:T(8,128)(2,1)} %get-tuple-element.176), channel_id=1, source_target_pairs={{0,8},{4,12},{8,0},{12,4},{16,24},{20,28},{24,16},{28,20},{1,9},{5... | collective-permute-start | bytes 497672 | tf_op jit(solution)/shard_map/ppermute | solution.py:748
  296.9 10.4 %collective-permute-start.30 = (bf16[1,2,72,576]{3,2,1,0:T(8,128)(2,1)S(1)}, bf16[1,2,72,576]{3,2,1,0:T(8,128)(2,1)S(1)}, u32[]{:S(2)}, u32[]{:S(2)}) collective-permute-start(bf16[1,2,72,576]{3,2,1,0:T(8,128)(2,1)S(1)} %copy-done.56), channel_id=1, source_target_pairs={{0,4},{4,0},{8,12},{12,8},{16,20},{20,16},{24,28},{28,24},{1,5},{5... | collective-permute-start | bytes 497672 | tf_op jit(solution)/shard_map/ppermute | solution.py:748
  297.4 49.9 %collective-permute-start.36 = (bf16[2,72,1152]{2,1,0:T(8,128)(2,1)}, bf16[2,72,1152]{2,1,0:T(8,128)(2,1)S(1)}, u32[]{:S(2)}, u32[]{:S(2)}) collective-permute-start(bf16[2,72,1152]{2,1,0:T(8,128)(2,1)} %sum_pieces.16), channel_id=1, source_target_pairs={{0,16},{4,20},{8,24},{12,28},{16,0},{20,4},{24,8},{28,12},{1,17},{... | collective-permute-start | bytes 995336 | tf_op jit(solution)/shard_map/ppermute | solution.py:748
  298.8 11.6 %collective-permute-start.31 = (bf16[2,2,72,576]{3,2,1,0:T(8,128)(2,1)S(1)}, bf16[2,2,72,576]{3,2,1,0:T(8,128)(2,1)S(1)}, u32[]{:S(2)}, u32[]{:S(2)}) collective-permute-start(bf16[2,2,72,576]{3,2,1,0:T(8,128)(2,1)S(1)} %copy-done.55), channel_id=1, source_target_pairs={{0,2},{1,3},{2,0},{3,1},{4,6},{5,7},{6,4},{7,5},{8,10},{9,11},{10,... | collective-permute-start | bytes 995336 | tf_op jit(solution)/shard_map/ppermute | solution.py:847
  304.0 13.5 %collective-permute-start.34 = (bf16[144,1152]{1,0:T(8,128)(2,1)S(1)}, bf16[144,1152]{1,0:T(8,128)(2,1)S(1)}, u32[]{:S(2)}, u32[]{:S(2)}) collective-permute-start(bf16[144,1152]{1,0:T(8,128)(2,1)S(1)} %copy-done.29), channel_id=1, source_target_pairs={{0,2},{1,3},{2,0},{3,1},{4,6},{5,7},{6,4},{7,5},{8,10},{9,11},{10,... | collective-permute-start | bytes 995336 | tf_op jit(solution)/shard_map/ppermute | solution.py:847
  306.8 37.1 %collective-permute-start.23 = (bf16[256,1152]{1,0:T(8,128)(2,1)S(1)}, bf16[256,1152]{1,0:T(8,128)(2,1)S(1)}, u32[]{:S(2)}, u32[]{:S(2)}) collective-permute-start(bf16[256,1152]{1,0:T(8,128)(2,1)S(1)} %slice.164), channel_id=1, source_target_pairs={{0,2},{1,3},{2,0},{3,1},{4,6},{5,7},{6,4},{7,5},{8,10},{9,11},{10,... | collective-permute-start | bytes 1769480 | tf_op jit(solution)/shard_map/ppermute | solution.py:847
  314.2 38.1 %collective-permute-start.37 = (bf16[4,72,576]{2,1,0:T(8,128)(2,1)}, bf16[4,72,576]{2,1,0:T(8,128)(2,1)S(1)}, u32[]{:S(2)}, u32[]{:S(2)}) collective-permute-start(bf16[4,72,576]{2,1,0:T(8,128)(2,1)} %sum_pieces.17), channel_id=1, source_target_pairs={{0,16},{4,20},{8,24},{12,28},{16,0},{20,4},{24,8},{28,12},{1,17},{... | collective-permute-start | bytes 995336 | tf_op jit(solution)/shard_map/ppermute | solution.py:748
  316.7 3.8 collective-permute-start.32
  317.5 23.7 %collective-permute-start.41 = (bf16[4,2,12,1152]{3,2,1,0:T(8,128)(2,1)S(1)}, bf16[4,2,12,1152]{3,2,1,0:T(8,128)(2,1)S(1)}, u32[]{:S(2)}, u32[]{:S(2)}) collective-permute-start(bf16[4,2,12,1152]{3,2,1,0:T(8,128)(2,1)S(1)} %pad_maximum_fusion.7), channel_id=1, source_target_pairs={{0,16},{4,20},{8,24},{12,28},{16,0},{20,4},{24,8},{28,12},{1,17},{... | collective-permute-start | bytes 663560 | tf_op jit(solution)/shard_map/ppermute | solution.py:786
  320.5 24.7 %collective-permute-start.35 = (bf16[2,144,1152]{2,1,0:T(8,128)(2,1)S(1)}, bf16[2,144,1152]{2,1,0:T(8,128)(2,1)S(1)}, u32[]{:S(2)}, u32[]{:S(2)}) collective-permute-start(bf16[2,144,1152]{2,1,0:T(8,128)(2,1)S(1)} %maximum_select_fusion), channel_id=1, source_target_pairs={{0,1},{1,0},{2,3},{3,2},{4,5},{5,4},{6,7},{7,6},{8,9},{9,8},{10,11... | collective-permute-start | bytes 1990664 | tf_op jit(solution)/shard_map/ppermute | solution.py:850
  357.2 3.8 collective-permute-start.38
  361.1 4.7 %collective-permute-start.39 = (f32[4324]{0:T(1024)S(1)}, f32[4324]{0:T(1024)S(1)}, u32[]{:S(2)}, u32[]{:S(2)}) collective-permute-start(f32[4324]{0:T(1024)S(1)} %add.129), channel_id=1, source_target_pairs={{0,16},{4,20},{8,24},{12,28},{16,0},{20,4},{24,8},{28,12},{1,17},{... | collective-permute-start | bytes 51896 | tf_op jit(solution)/shard_map/ppermute | solution.py:804
  362.2 10.6 %collective-permute-start.42 = (bf16[72,2304]{1,0:T(8,128)(2,1)S(1)}, bf16[72,2304]{1,0:T(8,128)(2,1)S(1)}, u32[]{:S(2)}, u32[]{:S(2)}) collective-permute-start(bf16[72,2304]{1,0:T(8,128)(2,1)S(1)} %constant_dynamic-update-slice_fusion.4), channel_id=1, source_target_pairs={{0,2},{1,3},{2,0},{3,1},{4,6},{5,7},{6,4},{7,5},{8,10},{9,11},{10,... | collective-permute-start | bytes 995336 | tf_op jit(solution)/shard_map/ppermute | solution.py:847
  363.6 12.7 %collective-permute-start.40 = (bf16[72,2304]{1,0:T(8,128)(2,1)S(1)}, bf16[72,2304]{1,0:T(8,128)(2,1)S(1)}, u32[]{:S(2)}, u32[]{:S(2)}) collective-permute-start(bf16[72,2304]{1,0:T(8,128)(2,1)S(1)} %concatenate.93), channel_id=1, source_target_pairs={{0,2},{1,3},{2,0},{3,1},{4,6},{5,7},{6,4},{7,5},{8,10},{9,11},{10,... | collective-permute-start | bytes 995336 | tf_op jit(solution)/shard_map/ppermute | solution.py:847
  376.5 2.2 collective-permute-start.43
  376.7 4.3 %collective-permute-start.44 = (bf16[144,2304]{1,0:T(8,128)(2,1)S(1)}, bf16[144,2304]{1,0:T(8,128)(2,1)S(1)}, u32[]{:S(2)}, u32[]{:S(2)}) collective-permute-start(bf16[144,2304]{1,0:T(8,128)(2,1)S(1)} %pad_maximum_fusion.5), channel_id=1, source_target_pairs={{0,1},{1,0},{2,3},{3,2},{4,5},{5,4},{6,7},{7,6},{8,9},{9,8},{10,11... | collective-permute-start | bytes 1990664 | tf_op jit(solution)/shard_map/ppermute | solution.py:850
  (55 other events, 263.7 us)
Sparse Core Ops, SparseCore 0:
  100.0 172.7 reduce-scatter.1

commit v4 on v3

--- a/solution.py
+++ b/solution.py
@@ -1013,7 +1013,6 @@
     jobs_qkv = [by_row(dims, (w_part,), cols, prefix=(p,)) for p, dims in enumerate(orders)]
     step(jobs_qkv)
     jobs_qkv.append(job_proj)
-    gather.tick()
     back, back_far = project_back(clock.now, core, d, w_qkv, mine)
     clock.passed(back)
     step(jobs_up)

time: 399 us -> 383 us (0.960)
  waiting for transfers between devices: 64.6 us -> 50.2 us
    ppermute x3, waiting for transfers between devices: 24.6 us -> 4.2 us  [tick(): self.far = swap(self.clock.tie(self.part))]
    ppermute x3, waiting for transfers between devices: 5.28 us -> 10 us  [tick(): self.far = self.swaps.pop(0)(self.clock.tie(self.part))]
    unnamed x122 -> x112, local copies, waits for them, and re-layouts: 14.8 us -> 12.7 us
  transfers between devices with their start and end apart: 46 -> 46, of which waited for: 18 -> 15; matrix products, arithmetic and copies ran while one was open for 13% -> 13% of each run, Pallas kernels for 41% -> 43%
where the time goes in v4:
time: 383 us; the launch traced here: 379 us
  Pallas kernels  194 us (51%)
  waiting for transfers between devices  50.2 us (13%)
  local copies, waits for them, and re-layouts  43.3 us (11%)
  starting transfers between devices  40.2 us (10%)
  matrix products  19 us (5%)
  other arithmetic  16.1 us (4%)
  between operations  15.8 us (4%)
    pallas_call x10, Pallas kernels, advance(): pl.pallas_call(functools.partial(sum_kernel, counts=counts, places=places...  37.4 us
    pallas_call x1, Pallas kernels, mlp_fall(): pl.pallas_call(fall_kernel, grid_spec=pltpu.PrefetchScalarGridSpec(num_sc...  29.7 us
    pallas_call x1, Pallas kernels, mlp_rise(): pl.pallas_call(rise_kernel, grid=(ff // tile,), in_specs=[pl.BlockSpec((r...  27.4 us
    pallas_call x1, Pallas kernels, attend_backward(): pl.pallas_call(functools.partial(backward_kernel, scale=scale), grid_spec...  27.3 us
    pallas_call x2, Pallas kernels, attend_forward(): pl.pallas_call(forward_kernel, grid_spec=pltpu.PrefetchScalarGridSpec(num...  18.5 us
    ppermute x14, waiting for transfers between devices, swap_y(): return lax.ppermute(a, 'seq', over_y)  17.2 us
    ppermute x14, starting transfers between devices, swap_y(): return lax.ppermute(a, 'seq', over_y)  16.5 us
    ppermute x13, starting transfers between devices, advance(): total = swaps[key[0]](total)  16 us
  transfers between devices with their start and end apart: 46, of which 15 were waited for; matrix products, arithmetic and copies ran while one was open for 13% of the time, Pallas kernels for 43%

profile of v4, /device:TPU:0, one launch (start us, length us, event | category | flops | bytes accessed | tf_op | source)
XLA Modules:
  0.0 379.0 jit_solution(7324688511704258841)
XLA Ops:
  7.3 2.3 dynamic-slice_bitcast_fusion
  9.6 3.0 collective-permute-start
  13.8 2.2 fusion.28
  21.0 1.6 token_features.1
  23.9 2.3 dynamic-slice_bitcast_fusion.2
  29.2 14.0 %project.1 = (bf16[1024,1152]{1,0:T(8,128)(2,1)}, bf16[512,1152]{1,0:T(8,128)(2,1)}, bf16[3,8,72,1024]{3,2,1,0:T(8,128)(2,1)}) custom-call(s32[1]{0:T(128)} %bitcast.4.core_ref, bf16[256,1152]{1,0:T(8,128)(2,1)} %copy-done.21, bf16[256,1152]{1,0:T(8,128)(2,1)} %collective-permute-done.b_ref, bf16[256,1152]{1,0:T(8,128)(2,1)} %collective-permute-done.1.c_ref, ...), custom_call_target="tpu_custom_call" | custom-call | flops 1000000 | bytes 100000 | tf_op jit(solution)/shard_map/project/pallas_call | solution.py:164
  43.2 9.2 %attention_forward.2 = (bf16[4,72,1024]{2,1,0:T(8,128)(2,1)}, f32[4,1,1024]{2,1,0:T(1,128)}) custom-call(s32[5]{0:T(128)} %stack.95.clock_ref.coord_ref, bf16[3,8,72,1024]{3,2,1,0:T(8,128)(2,1)} %get-tuple-element.114.p_ref.qkv_ref, bf16[8,64,64]{2,1,0:T(8,128)(2,1)} %fusion.22.table_ref, bf16[112,1024]{1,0:T(8,128)(2,1)} %get-tuple-element.111.feat_ref), custom_call_target="tpu_custom_call" | custom-call | flops 1000000 | bytes 100000 | tf_op jit(solution)/shard_map/attention_forward/pallas_call | solution.py:323
  52.7 9.3 %attention_forward.3 = (bf16[4,72,1024]{2,1,0:T(8,128)(2,1)}, f32[4,1,1024]{2,1,0:T(1,128)}) custom-call(s32[5]{0:T(128)} %stack.95.clock_ref.coord_ref, bf16[3,8,72,1024]{3,2,1,0:T(8,128)(2,1)} %get-tuple-element.114.p_ref.qkv_ref, bf16[8,64,64]{2,1,0:T(8,128)(2,1)} %fusion.22.table_ref, bf16[112,1024]{1,0:T(8,128)(2,1)} %get-tuple-element.111.feat_ref), custom_call_target="tpu_custom_call" | custom-call | flops 1000000 | bytes 100000 | tf_op jit(solution)/shard_map/attention_forward/pallas_call | solution.py:323
  67.2 3.4 fusion.45
  72.5 27.4 %feed_forward_rise.1 = (f32[512,1152]{1,0:T(8,128)}, bf16[512,4608]{1,0:T(8,128)(2,1)}, bf16[4608,1152]{1,0:T(8,128)(2,1)}, bf16[1152,512]{1,0:T(8,128)(2,1)}, bf16[512,1152]{1,0:T(8,128)(2,1)}) custom-call(bf16[512,1152]{1,0:T(8,128)(2,1)} %multiply_convert_fusion.m_ref, bf16[256,1152]{1,0:T(8,128)(2,1)} %get-tuple-element.237.near_ref, ...), custom_call_target="tpu_custom_call" | custom-call | flops 1000000 | bytes 100000 | tf_op jit(solution)/shard_map/feed_forward_rise/pallas_call | solution.py:468
  99.9 29.7 %feed_forward_fall.1 = (f32[512,1152]{1,0:T(8,128)}, bf16[1152,2304]{1,0:T(8,128)(2,1)}, bf16[1152,2304]{1,0:T(8,128)(2,1)}) custom-call(s32[5]{0:T(128)} %stack.95.clock_ref.coord_ref, s32[2]{0:T(128)} %pad_add_fusion.1.tile_ref, bf16[1152,512]{1,0:T(8,128)(2,1)} %get-tuple-element.126.mt_ref, bf16[512,1152]{1,0:T(8,128)(2,1)} %get-tuple-element.127.g_ref, ...), custom_call_target="tpu_custom_call" | custom-call | flops 1000000 | bytes 100000 | tf_op jit(solution)/shard_map/feed_forward_fall/pallas_call | solution.py:526
  129.6 9.2 %middle.1 = (bf16[512,1152]{1,0:T(8,128)(2,1)}, f32[512,1152]{1,0:T(8,128)}, bf16[512,1152]{1,0:T(8,128)(2,1)}, f32[8,1152]{1,0:T(8,128)}) custom-call(s32[5]{0:T(128)} %stack.95.clock_ref.coord_ref, f32[512,1152]{1,0:T(8,128)} %get-tuple-element.129.gm_ref, f32[512,1152]{1,0:T(8,128)} %get-tuple-element.124.two_ref, ...), custom_call_target="tpu_custom_call" | custom-call | flops 1000000 | bytes 100000 | tf_op jit(solution)/shard_map/middle/pallas_call | solution.py:600
  139.2 3.1 collective-permute-done.7
  142.6 1.9 slice.161
  146.8 3.3 convolution_convert_fusion
  150.1 2.6 copy.45
  152.7 4.4 %convolution_convert_fusion.1 = bf16[576,1024]{1,0:T(8,128)(2,1)} fusion(bf16[1024,1152]{1,0:T(8,128)(2,1)} %copy-done.35, bf16[1152,1152]{1,0:T(8,128)(2,1)S(1)} %copy-done, s32[]{:T(128)S(6)} %select_n.199), kind=kOutput, calls=%fused_computation.10 | convolution fusion | flops 1359544320 | bytes 4866052 | tf_op jit(solution)/shard_map/dot_general | solution.py:30
  157.1 3.0 collective-permute-done.6
  160.2 5.7 %sum_pieces.10 = (bf16[1,2,2,2,72,1152]{5,4,3,2,1,0:T(8,128)(2,1)}, bf16[1,2,2,2,72,1152]{5,4,3,2,1,0:T(8,128)(2,1)}, bf16[1,2,2,2,72,576]{5,4,3,2,1,0:T(8,128)(2,1)}) custom-call(s32[5]{0:T(128)} %stack.95.clock_ref.coord_ref, bf16[2,2,2,2,72,2304]{5,4,3,2,1,0:T(8,128)(2,1)} %bitcast.126, ...), custom_call_target="tpu_custom_call" | custom-call | flops 1000000 | bytes 100000 | tf_op jit(solution)/shard_map/sum_pieces/pallas_call | solution.py:733
  169.0 1.8 collective-permute-start.11
  172.2 27.3 %attention_backward.1 = (bf16[3,8,72,1024]{3,2,1,0:T(8,128)(2,1)}, f32[8,64,64]{2,1,0:T(8,128)}, f32[2,8,16,72]{3,2,1,0:T(8,128)}) custom-call(s32[5]{0:T(128)} %stack.95.clock_ref.coord_ref, bf16[3,8,72,1024]{3,2,1,0:T(8,128)(2,1)} %get-tuple-element.114.p_ref.qkv_ref, bf16[8,72,1024]{2,1,0:T(8,128)(2,1)} %copy-done.10, bf16[8,72,1024]{2,1,0:T(8,128)(2,1)} %bitcast.146, ...), custom_call_target="tpu_custom_call" | custom-call | flops 1000000 | bytes 100000 | tf_op jit(solution)/shard_map/attention_backward/pallas_call | solution.py:400
  199.5 4.3 %collective-permute-done.9.refs_2_ = bf16[1,2,2,2,72,1152]{5,4,3,2,1,0:T(8,128)(2,1)S(1)} collective-permute-done((bf16[1,2,2,2,72,1152]{5,4,3,2,1,0:T(8,128)(2,1)}, bf16[1,2,2,2,72,1152]{5,4,3,2,1,0:T(8,128)(2,1)S(1)}, u32[]{:S(2)}, u32[]{:S(2)}) %collective-permute-start.9) | collective-permute-done | bytes 1327136 | tf_op jit(solution)/shard_map/ppermute | solution.py:748
  206.0 3.8 sum_pieces.11
  212.8 10.0 %project_weights.1 = bf16[3,1152,576]{2,1,0:T(8,128)(2,1)} custom-call(s32[5]{0:T(128)} %stack.95.clock_ref.coord_ref, bf16[1024,1152]{1,0:T(8,128)(2,1)} %get-tuple-element.150.in_ref, bf16[3,8,72,1024]{3,2,1,0:T(8,128)(2,1)} %get-tuple-element.145.d_ref), custom_call_target="tpu_custom_call" | custom-call | flops 1000000 | bytes 100000 | tf_op jit(solution)/shard_map/project_weights/pallas_call | solution.py:206
  223.7 4.6 %sum_pieces.12 = (bf16[1,2,2,2,72,576]{5,4,3,2,1,0:T(8,128)(2,1)}, bf16[1,2,2,2,72,576]{5,4,3,2,1,0:T(8,128)(2,1)}, bf16[1,2,2,2,72,576]{5,4,3,2,1,0:T(8,128)(2,1)}) custom-call(s32[5]{0:T(128)} %stack.95.clock_ref.coord_ref, bf16[3,2,2,2,2,72,576]{6,5,4,3,2,1,0:T(8,128)(2,1)} %bitcast.111, bf16[3,2,2,2,2,72,576]{6,5,4,3,2,1,0:T(8,128)(2,1)} %bitcast.112, ...), custom_call_target="tpu_custom_call" | custom-call | flops 1000000 | bytes 100000 | tf_op jit(solution)/shard_map/sum_pieces/pallas_call | solution.py:733
  230.0 1.7 collective-permute-start.18
  231.7 13.6 %project_back.1 = (f32[512,1152]{1,0:T(8,128)}, bf16[512,1152]{1,0:T(8,128)(2,1)}) custom-call(s32[5]{0:T(128)} %stack.95.clock_ref.coord_ref, s32[1]{0:T(128)} %bitcast.4.core_ref, bf16[3,8,72,1024]{3,2,1,0:T(8,128)(2,1)} %get-tuple-element.145.d_ref, bf16[1152,3456]{1,0:T(8,128)(2,1)} %w_ref.3), custom_call_target="tpu_custom_call" | custom-call | flops 1000000 | bytes 100000 | tf_op jit(solution)/shard_map/project_back/pallas_call | solution.py:266
  245.4 3.6 sum_pieces.13
  250.5 6.4 %collective-permute-done.18.refs_5_.refs_7_.refs_9_.refs_11_ = bf16[1,2,2,2,72,576]{5,4,3,2,1,0:T(8,128)(2,1)S(1)} collective-permute-done((bf16[1,2,2,2,72,576]{5,4,3,2,1,0:T(8,128)(2,1)}, bf16[1,2,2,2,72,576]{5,4,3,2,1,0:T(8,128)(2,1)S(1)}, u32[]{:S(2)}, u32[]{:S(2)}) %collective-permute-start.18) | collective-permute-done | bytes 663584 | tf_op jit(solution)/shard_map/ppermute | solution.py:748
  257.8 3.8 %sum_pieces.14 = (bf16[1,2,2,72,576]{4,3,2,1,0:T(8,128)(2,1)}, bf16[1,2,2,72,576]{4,3,2,1,0:T(8,128)(2,1)}, bf16[2,2,2,72,576]{4,3,2,1,0:T(8,128)(2,1)}) custom-call(s32[5]{0:T(128)} %stack.95.clock_ref.coord_ref, bf16[3,2,2,2,2,72,576]{6,5,4,3,2,1,0:T(8,128)(2,1)} %bitcast.114, bf16[1,2,2,2,72,576]{5,4,3,2,1,0:T(8,128)(2,1)} %copy-done.7, ...), custom_call_target="tpu_custom_call" | custom-call | flops 1000000 | bytes 100000 | tf_op jit(solution)/shard_map/sum_pieces/pallas_call | solution.py:733
  268.6 5.9 %last.1 = (bf16[512,1152]{1,0:T(8,128)(2,1)}, f32[8,1152]{1,0:T(8,128)}) custom-call(f32[512,1152]{1,0:T(8,128)} %get-tuple-element.159.back_ref, bf16[512,1152]{1,0:T(8,128)(2,1)} %collective-permute-done.15.far_ref, bf16[512,1152]{1,0:T(8,128)(2,1)} %get-tuple-element.121.x_ref, f32[512,1152]{1,0:T(8,128)} %get-tuple-element.166.grad_ref, ...), custom_call_target="tpu_custom_call" | custom-call | flops 1000000 | bytes 100000 | tf_op jit(solution)/shard_map/last/pallas_call | solution.py:639
  276.1 2.9 collective-permute-done.20.refs_5_.refs_6_.refs_7_
  280.6 3.3 sum_pieces.15
  288.0 3.1 sum_pieces.16
  295.3 2.4 collective-permute-start.35
  297.7 1.5 collective-permute-start.30
  300.0 1.5 collective-permute-start.22
  301.5 7.8 %collective-permute-done.30.refs_11_.refs_15_.refs_13_.refs_18_ = bf16[2,2,72,576]{3,2,1,0:T(8,128)(2,1)S(1)} collective-permute-done((bf16[2,2,72,576]{3,2,1,0:T(8,128)(2,1)S(1)}, bf16[2,2,72,576]{3,2,1,0:T(8,128)(2,1)S(1)}, u32[]{:S(2)}, u32[]{:S(2)}) %collective-permute-start.30) | collective-permute-done | bytes 331808 | tf_op jit(solution)/shard_map/ppermute | solution.py:847
  310.1 3.0 sum_pieces.17
  317.4 4.2 %collective-permute-done.40 = bf16[2,2,12,1152]{3,2,1,0:T(8,128)(2,1)S(1)} collective-permute-done((bf16[2,2,12,1152]{3,2,1,0:T(8,128)(2,1)S(1)}, bf16[2,2,12,1152]{3,2,1,0:T(8,128)(2,1)S(1)}, u32[]{:S(2)}, u32[]{:S(2)}) %collective-permute-start.40) | collective-permute-done | bytes 110624 | tf_op jit(solution)/shard_map/ppermute | solution.py:786
  321.7 4.3 %collective-permute-done.22 = bf16[256,1152]{1,0:T(8,128)(2,1)S(1)} collective-permute-done((bf16[256,1152]{1,0:T(8,128)(2,1)S(1)}, bf16[256,1152]{1,0:T(8,128)(2,1)S(1)}, u32[]{:S(2)}, u32[]{:S(2)}) %collective-permute-start.22) | collective-permute-done | bytes 589856 | tf_op jit(solution)/shard_map/ppermute | solution.py:847
  327.7 1.7 pad_maximum_fusion
  330.1 3.3 sum_pieces.18
  335.2 3.2 sum_pieces.19
  341.0 2.4 collective-permute-done.37
  343.9 1.6 collective-permute-start.41
  346.2 7.4 %collective-permute-done.38 = f32[4324]{0:T(1024)S(1)} collective-permute-done((f32[4324]{0:T(1024)S(1)}, f32[4324]{0:T(1024)S(1)}, u32[]{:S(2)}, u32[]{:S(2)}) %collective-permute-start.38) | collective-permute-done | bytes 17328 | tf_op jit(solution)/shard_map/ppermute | solution.py:804
  367.9 4.0 %concatenate.96 = f32[144,3456]{1,0:T(8,128)} concatenate(f32[144,576]{1,0:T(8,128)} %get-tuple-element.222, f32[144,576]{1,0:T(8,128)} %get-tuple-element.226, f32[144,576]{1,0:T(8,128)} %get-tuple-element.221, f32[144,576]{1,0:T(8,128)S(1)} %get-tuple-element.225, f32[144,576]{1,0:T(8,128)} %get-tuple-element.220, f32[144,576]{1,0:T(8,128)S(1)} %get-tuple-element.224), dimensions={1} | concatenate | bytes 3981312 | tf_op jit(solution)/shard_map/concatenate | solution.py:1096
  (279 shorter events, 81.2 us)
Async XLA Ops:
  7.2 59.5 %copy-start = (bf16[1152,1152]{1,0:T(8,128)(2,1)S(1)}, bf16[1152,1152]{1,0:T(8,128)(2,1)}, u32[]{:S(2)}) copy-start(bf16[1152,1152]{1,0:T(8,128)(2,1)} %param.25) | copy-start | bytes 7962628
  7.2 268.8 %reduce-scatter.2.cloned.1.call-start = ((), (), s32[]{:S(2)}) async-start(), calls=%async_computation.1 | async-start | bytes 10948608 | tf_op jit(solution)/shard_map/reduce_scatter | solution.py:948
  9.6 16.6 %collective-permute-start = (bf16[256,1152]{1,0:T(8,128)(2,1)}, bf16[256,1152]{1,0:T(8,128)(2,1)}, u32[]{:S(2)}, u32[]{:S(2)}) collective-permute-start(bf16[256,1152]{1,0:T(8,128)(2,1)} %get-tuple-element.235), channel_id=1, source_target_pairs={{0,2},{1,3},{2,0},{3,1},{4,6},{5,7},{6,4},{7,5},{8,10},{9,11},{10,... | collective-permute-start | bytes 1769480 | tf_op jit(solution)/shard_map/ppermute | solution.py:847
  12.6 16.6 %collective-permute-start.1 = (bf16[256,1152]{1,0:T(8,128)(2,1)S(1)}, bf16[256,1152]{1,0:T(8,128)(2,1)}, u32[]{:S(2)}, u32[]{:S(2)}) collective-permute-start(bf16[256,1152]{1,0:T(8,128)(2,1)S(1)} %get-tuple-element.236.a_ref), channel_id=1, source_target_pairs={{0,1},{1,0},{2,3},{3,2},{4,5},{5,4},{6,7},{7,6},{8,9},{9,8},{10,11... | collective-permute-start | bytes 1769480 | tf_op jit(solution)/shard_map/ppermute | solution.py:850
  26.2 3.0 collective-permute-start.2
  26.7 25.9 %collective-permute-start.3 = (bf16[256,1152]{1,0:T(8,128)(2,1)}, bf16[256,1152]{1,0:T(8,128)(2,1)}, u32[]{:S(2)}, u32[]{:S(2)}) collective-permute-start(bf16[256,1152]{1,0:T(8,128)(2,1)} %get-tuple-element.117), channel_id=1, source_target_pairs={{0,2},{1,3},{2,0},{3,1},{4,6},{5,7},{6,4},{7,5},{8,10},{9,11},{10,... | collective-permute-start | bytes 1769480 | tf_op jit(solution)/shard_map/ppermute | solution.py:847
  52.4 12.0 %collective-permute-start.4 = (bf16[4,72,1024]{2,1,0:T(8,128)(2,1)}, bf16[4,72,1024]{2,1,0:T(8,128)(2,1)S(1)}, u32[]{:S(2)}, u32[]{:S(2)}) collective-permute-start(bf16[4,72,1024]{2,1,0:T(8,128)(2,1)} %get-tuple-element.116), channel_id=1, source_target_pairs={{0,1},{1,0},{2,3},{3,2},{4,5},{5,4},{6,7},{7,6},{8,9},{9,8},{10,11... | collective-permute-start | bytes 1769480 | tf_op jit(solution)/shard_map/ppermute | solution.py:850
  61.9 2.6 collective-permute-start.5
  138.8 3.4 collective-permute-start.7
  142.2 17.9 %collective-permute-start.8 = (bf16[1152,2304]{1,0:T(8,128)(2,1)}, bf16[1152,2304]{1,0:T(8,128)(2,1)}, u32[]{:S(2)}, u32[]{:S(2)}) collective-permute-start(bf16[1152,2304]{1,0:T(8,128)(2,1)} %get-tuple-element.138), channel_id=1, source_target_pairs={{0,1},{1,0},{2,3},{3,2},{4,5},{5,4},{6,7},{7,6},{8,9},{9,8},{10,11... | collective-permute-start | bytes 15925256 | tf_op jit(solution)/shard_map/ppermute | solution.py:850
  144.5 15.6 %collective-permute-start.6 = (bf16[256,1152]{1,0:T(8,128)(2,1)}, bf16[256,1152]{1,0:T(8,128)(2,1)S(1)}, u32[]{:S(2)}, u32[]{:S(2)}) collective-permute-start(bf16[256,1152]{1,0:T(8,128)(2,1)} %slice.161), channel_id=1, source_target_pairs={{0,2},{1,3},{2,0},{3,1},{4,6},{5,7},{6,4},{7,5},{8,10},{9,11},{10,... | collective-permute-start | bytes 1769480 | tf_op jit(solution)/shard_map/ppermute | solution.py:847
  165.9 37.9 %collective-permute-start.9 = (bf16[1,2,2,2,72,1152]{5,4,3,2,1,0:T(8,128)(2,1)}, bf16[1,2,2,2,72,1152]{5,4,3,2,1,0:T(8,128)(2,1)S(1)}, u32[]{:S(2)}, u32[]{:S(2)}) collective-permute-start(bf16[1,2,2,2,72,1152]{5,4,3,2,1,0:T(8,128)(2,1)} %get-tuple-element.139), channel_id=1, source_target_pairs={{0,4},{4,0},{8,12},{12,8},{16,20},{20,16},{24,28},{28,24},{1,5},{5... | collective-permute-start | bytes 3981320 | tf_op jit(solution)/shard_map/ppermute | solution.py:748
  167.2 36.7 %collective-permute-start.10 = (bf16[1,2,2,2,72,1152]{5,4,3,2,1,0:T(8,128)(2,1)}, bf16[1,2,2,2,72,1152]{5,4,3,2,1,0:T(8,128)(2,1)S(1)}, u32[]{:S(2)}, u32[]{:S(2)}) collective-permute-start(bf16[1,2,2,2,72,1152]{5,4,3,2,1,0:T(8,128)(2,1)} %get-tuple-element.140), channel_id=1, source_target_pairs={{0,2},{1,3},{2,0},{3,1},{4,6},{5,7},{6,4},{7,5},{8,10},{9,11},{10,... | collective-permute-start | bytes 3981320 | tf_op jit(solution)/shard_map/ppermute | solution.py:847
  169.0 53.8 %collective-permute-start.11 = (bf16[1,2,2,2,72,576]{5,4,3,2,1,0:T(8,128)(2,1)}, bf16[1,2,2,2,72,576]{5,4,3,2,1,0:T(8,128)(2,1)S(1)}, u32[]{:S(2)}, u32[]{:S(2)}) collective-permute-start(bf16[1,2,2,2,72,576]{5,4,3,2,1,0:T(8,128)(2,1)} %get-tuple-element.141), channel_id=1, source_target_pairs={{0,8},{4,12},{8,0},{12,4},{16,24},{20,28},{24,16},{28,20},{1,9},{5... | collective-permute-start | bytes 1990664 | tf_op jit(solution)/shard_map/ppermute | solution.py:748
  209.7 35.6 %collective-permute-start.13 = (bf16[1,2,2,72,1152]{4,3,2,1,0:T(8,128)(2,1)}, bf16[1,2,2,72,1152]{4,3,2,1,0:T(8,128)(2,1)}, u32[]{:S(2)}, u32[]{:S(2)}) collective-permute-start(bf16[1,2,2,72,1152]{4,3,2,1,0:T(8,128)(2,1)} %get-tuple-element.147), channel_id=1, source_target_pairs={{0,8},{4,12},{8,0},{12,4},{16,24},{20,28},{24,16},{28,20},{1,9},{5... | collective-permute-start | bytes 1990664 | tf_op jit(solution)/shard_map/ppermute | solution.py:748
  209.7 35.6 %collective-permute-start.14 = (bf16[1,2,2,72,1152]{4,3,2,1,0:T(8,128)(2,1)}, bf16[1,2,2,72,1152]{4,3,2,1,0:T(8,128)(2,1)}, u32[]{:S(2)}, u32[]{:S(2)}) collective-permute-start(bf16[1,2,2,72,1152]{4,3,2,1,0:T(8,128)(2,1)} %get-tuple-element.148), channel_id=1, source_target_pairs={{0,4},{4,0},{8,12},{12,8},{16,20},{20,16},{24,28},{28,24},{1,5},{5... | collective-permute-start | bytes 1990664 | tf_op jit(solution)/shard_map/ppermute | solution.py:748
  212.1 10.7 %collective-permute-start.12 = (bf16[1,1,8,576]{3,2,1,0:T(8,128)(2,1)S(1)}, bf16[1,1,8,576]{3,2,1,0:T(8,128)(2,1)S(1)}, u32[]{:S(2)}, u32[]{:S(2)}) collective-permute-start(bf16[1,1,8,576]{3,2,1,0:T(8,128)(2,1)S(1)} %convert_element_type.61), channel_id=1, source_target_pairs={{0,1},{1,0},{2,3},{3,2},{4,5},{5,4},{6,7},{7,6},{8,9},{9,8},{10,11... | collective-permute-start | bytes 27656 | tf_op jit(solution)/shard_map/ppermute | solution.py:850
  228.3 21.8 %collective-permute-start.16 = (bf16[1,2,2,2,72,576]{5,4,3,2,1,0:T(8,128)(2,1)}, bf16[1,2,2,2,72,576]{5,4,3,2,1,0:T(8,128)(2,1)S(1)}, u32[]{:S(2)}, u32[]{:S(2)}) collective-permute-start(bf16[1,2,2,2,72,576]{5,4,3,2,1,0:T(8,128)(2,1)} %get-tuple-element.155), channel_id=1, source_target_pairs={{0,4},{4,0},{8,12},{12,8},{16,20},{20,16},{24,28},{28,24},{1,5},{5... | collective-permute-start | bytes 1990664 | tf_op jit(solution)/shard_map/ppermute | solution.py:748
  229.0 21.5 %collective-permute-start.17 = (bf16[1,2,2,2,72,576]{5,4,3,2,1,0:T(8,128)(2,1)}, bf16[1,2,2,2,72,576]{5,4,3,2,1,0:T(8,128)(2,1)S(1)}, u32[]{:S(2)}, u32[]{:S(2)}) collective-permute-start(bf16[1,2,2,2,72,576]{5,4,3,2,1,0:T(8,128)(2,1)} %get-tuple-element.156), channel_id=1, source_target_pairs={{0,2},{1,3},{2,0},{3,1},{4,6},{5,7},{6,4},{7,5},{8,10},{9,11},{10,... | collective-permute-start | bytes 1990664 | tf_op jit(solution)/shard_map/ppermute | solution.py:847
  230.0 26.9 %collective-permute-start.18 = (bf16[1,2,2,2,72,576]{5,4,3,2,1,0:T(8,128)(2,1)}, bf16[1,2,2,2,72,576]{5,4,3,2,1,0:T(8,128)(2,1)S(1)}, u32[]{:S(2)}, u32[]{:S(2)}) collective-permute-start(bf16[1,2,2,2,72,576]{5,4,3,2,1,0:T(8,128)(2,1)} %get-tuple-element.157), channel_id=1, source_target_pairs={{0,8},{4,12},{8,0},{12,4},{16,24},{20,28},{24,16},{28,20},{1,9},{5... | collective-permute-start | bytes 1990664 | tf_op jit(solution)/shard_map/ppermute | solution.py:748
  249.0 18.2 %collective-permute-start.15 = (bf16[512,1152]{1,0:T(8,128)(2,1)}, bf16[512,1152]{1,0:T(8,128)(2,1)}, u32[]{:S(2)}, u32[]{:S(2)}) collective-permute-start(bf16[512,1152]{1,0:T(8,128)(2,1)} %get-tuple-element.165), channel_id=1, source_target_pairs={{0,1},{1,0},{2,3},{3,2},{4,5},{5,4},{6,7},{7,6},{8,9},{9,8},{10,11... | collective-permute-start | bytes 3538952 | tf_op jit(solution)/shard_map/ppermute | solution.py:850
  250.0 13.1 %copy-start.42 = (s32[32,32]{1,0:T(8,128)S(1)}, s32[32,32]{1,0:T(8,128)}, u32[]{:S(2)}) copy-start(s32[32,32]{1,0:T(8,128)} %subtract_add_fusion) | copy-start | bytes 12292
  261.6 18.0 %collective-permute-start.21 = (bf16[2,2,2,72,576]{4,3,2,1,0:T(8,128)(2,1)}, bf16[2,2,2,72,576]{4,3,2,1,0:T(8,128)(2,1)S(1)}, u32[]{:S(2)}, u32[]{:S(2)}) collective-permute-start(bf16[2,2,2,72,576]{4,3,2,1,0:T(8,128)(2,1)} %get-tuple-element.170), channel_id=1, source_target_pairs={{0,4},{4,0},{8,12},{12,8},{16,20},{20,16},{24,28},{28,24},{1,5},{5... | collective-permute-start | bytes 1990664 | tf_op jit(solution)/shard_map/ppermute | solution.py:748
  263.8 12.3 %collective-permute-start.19 = (bf16[1,2,2,72,576]{4,3,2,1,0:T(8,128)(2,1)}, bf16[1,2,2,72,576]{4,3,2,1,0:T(8,128)(2,1)S(1)}, u32[]{:S(2)}, u32[]{:S(2)}) collective-permute-start(bf16[1,2,2,72,576]{4,3,2,1,0:T(8,128)(2,1)} %get-tuple-element.168), channel_id=1, source_target_pairs={{0,2},{1,3},{2,0},{3,1},{4,6},{5,7},{6,4},{7,5},{8,10},{9,11},{10,... | collective-permute-start | bytes 995336 | tf_op jit(solution)/shard_map/ppermute | solution.py:847
  264.2 14.8 %collective-permute-start.20 = (bf16[1,2,2,72,576]{4,3,2,1,0:T(8,128)(2,1)}, bf16[1,2,2,72,576]{4,3,2,1,0:T(8,128)(2,1)S(1)}, u32[]{:S(2)}, u32[]{:S(2)}) collective-permute-start(bf16[1,2,2,72,576]{4,3,2,1,0:T(8,128)(2,1)} %get-tuple-element.169), channel_id=1, source_target_pairs={{0,8},{4,12},{8,0},{12,4},{16,24},{20,28},{24,16},{28,20},{1,9},{5... | collective-permute-start | bytes 995336 | tf_op jit(solution)/shard_map/ppermute | solution.py:748
  265.9 20.7 %collective-permute-start.24 = (bf16[1,2,72,1152]{3,2,1,0:T(8,128)(2,1)}, bf16[1,2,72,1152]{3,2,1,0:T(8,128)(2,1)S(1)}, u32[]{:S(2)}, u32[]{:S(2)}) collective-permute-start(bf16[1,2,72,1152]{3,2,1,0:T(8,128)(2,1)} %get-tuple-element.162), channel_id=1, source_target_pairs={{0,2},{1,3},{2,0},{3,1},{4,6},{5,7},{6,4},{7,5},{8,10},{9,11},{10,... | collective-permute-start | bytes 995336 | tf_op jit(solution)/shard_map/ppermute | solution.py:847
  267.1 19.5 %collective-permute-start.25 = (bf16[1,2,72,1152]{3,2,1,0:T(8,128)(2,1)}, bf16[1,2,72,1152]{3,2,1,0:T(8,128)(2,1)S(1)}, u32[]{:S(2)}, u32[]{:S(2)}) collective-permute-start(bf16[1,2,72,1152]{3,2,1,0:T(8,128)(2,1)} %get-tuple-element.163), channel_id=1, source_target_pairs={{0,8},{4,12},{8,0},{12,4},{16,24},{20,28},{24,16},{28,20},{1,9},{5... | collective-permute-start | bytes 995336 | tf_op jit(solution)/shard_map/ppermute | solution.py:748
  276.0 15.1 %collective-permute-start.23 = (f32[4324]{0:T(1024)S(1)}, f32[4324]{0:T(1024)S(1)}, u32[]{:S(2)}, u32[]{:S(2)}) collective-permute-start(f32[4324]{0:T(1024)S(1)} %concatenate.87), channel_id=1, source_target_pairs={{0,1},{1,0},{2,3},{3,2},{4,5},{5,4},{6,7},{7,6},{8,9},{9,8},{10,11... | collective-permute-start | bytes 51896 | tf_op jit(solution)/shard_map/ppermute | solution.py:850
  283.9 7.3 %collective-permute-start.27 = (bf16[1,1,12,1152]{3,2,1,0:T(8,128)(2,1)S(1)}, bf16[1,1,12,1152]{3,2,1,0:T(8,128)(2,1)S(1)}, u32[]{:S(2)}, u32[]{:S(2)}) collective-permute-start(bf16[1,1,12,1152]{3,2,1,0:T(8,128)(2,1)S(1)} %pad_maximum_fusion.11), channel_id=1, source_target_pairs={{0,2},{1,3},{2,0},{3,1},{4,6},{5,7},{6,4},{7,5},{8,10},{9,11},{10,... | collective-permute-start | bytes 82952 | tf_op jit(solution)/shard_map/ppermute | solution.py:847
  291.2 8.0 %collective-permute-start.32 = (bf16[1,2,12,1152]{3,2,1,0:T(8,128)(2,1)S(1)}, bf16[1,2,12,1152]{3,2,1,0:T(8,128)(2,1)S(1)}, u32[]{:S(2)}, u32[]{:S(2)}) collective-permute-start(bf16[1,2,12,1152]{3,2,1,0:T(8,128)(2,1)S(1)} %pad_maximum_fusion.10), channel_id=1, source_target_pairs={{0,4},{4,0},{8,12},{12,8},{16,20},{20,16},{24,28},{28,24},{1,5},{5... | collective-permute-start | bytes 165896 | tf_op jit(solution)/shard_map/ppermute | solution.py:786
  292.5 5.2 %collective-permute-start.26 = (f32[4324]{0:T(1024)S(1)}, f32[4324]{0:T(1024)S(1)}, u32[]{:S(2)}, u32[]{:S(2)}) collective-permute-start(f32[4324]{0:T(1024)S(1)} %add.126), channel_id=1, source_target_pairs={{0,2},{1,3},{2,0},{3,1},{4,6},{5,7},{6,4},{7,5},{8,10},{9,11},{10,... | collective-permute-start | bytes 51896 | tf_op jit(solution)/shard_map/ppermute | solution.py:847
  293.2 6.8 %collective-permute-start.28 = (bf16[1,2,72,576]{3,2,1,0:T(8,128)(2,1)S(1)}, bf16[1,2,72,576]{3,2,1,0:T(8,128)(2,1)S(1)}, u32[]{:S(2)}, u32[]{:S(2)}) collective-permute-start(bf16[1,2,72,576]{3,2,1,0:T(8,128)(2,1)S(1)} %copy-done.51), channel_id=1, source_target_pairs={{0,8},{4,12},{8,0},{12,4},{16,24},{20,28},{24,16},{28,20},{1,9},{5... | collective-permute-start | bytes 497672 | tf_op jit(solution)/shard_map/ppermute | solution.py:748
  293.9 7.6 %collective-permute-start.29 = (bf16[1,2,72,576]{3,2,1,0:T(8,128)(2,1)S(1)}, bf16[1,2,72,576]{3,2,1,0:T(8,128)(2,1)S(1)}, u32[]{:S(2)}, u32[]{:S(2)}) collective-permute-start(bf16[1,2,72,576]{3,2,1,0:T(8,128)(2,1)S(1)} %copy-done.50), channel_id=1, source_target_pairs={{0,4},{4,0},{8,12},{12,8},{16,20},{20,16},{24,28},{28,24},{1,5},{5... | collective-permute-start | bytes 497672 | tf_op jit(solution)/shard_map/ppermute | solution.py:748
  295.3 34.1 %collective-permute-start.35 = (bf16[2,72,1152]{2,1,0:T(8,128)(2,1)}, bf16[2,72,1152]{2,1,0:T(8,128)(2,1)S(1)}, u32[]{:S(2)}, u32[]{:S(2)}) collective-permute-start(bf16[2,72,1152]{2,1,0:T(8,128)(2,1)} %sum_pieces.16), channel_id=1, source_target_pairs={{0,16},{4,20},{8,24},{12,28},{16,0},{20,4},{24,8},{28,12},{1,17},{... | collective-permute-start | bytes 995336 | tf_op jit(solution)/shard_map/ppermute | solution.py:748
  297.7 11.6 %collective-permute-start.30 = (bf16[2,2,72,576]{3,2,1,0:T(8,128)(2,1)S(1)}, bf16[2,2,72,576]{3,2,1,0:T(8,128)(2,1)S(1)}, u32[]{:S(2)}, u32[]{:S(2)}) collective-permute-start(bf16[2,2,72,576]{3,2,1,0:T(8,128)(2,1)S(1)} %copy-done.49), channel_id=1, source_target_pairs={{0,2},{1,3},{2,0},{3,1},{4,6},{5,7},{6,4},{7,5},{8,10},{9,11},{10,... | collective-permute-start | bytes 995336 | tf_op jit(solution)/shard_map/ppermute | solution.py:847
  299.3 17.2 %collective-permute-start.33 = (bf16[144,1152]{1,0:T(8,128)(2,1)S(1)}, bf16[144,1152]{1,0:T(8,128)(2,1)S(1)}, u32[]{:S(2)}, u32[]{:S(2)}) collective-permute-start(bf16[144,1152]{1,0:T(8,128)(2,1)S(1)} %copy-done.27), channel_id=1, source_target_pairs={{0,2},{1,3},{2,0},{3,1},{4,6},{5,7},{6,4},{7,5},{8,10},{9,11},{10,... | collective-permute-start | bytes 995336 | tf_op jit(solution)/shard_map/ppermute | solution.py:847
  300.0 26.0 %collective-permute-start.22 = (bf16[256,1152]{1,0:T(8,128)(2,1)S(1)}, bf16[256,1152]{1,0:T(8,128)(2,1)S(1)}, u32[]{:S(2)}, u32[]{:S(2)}) collective-permute-start(bf16[256,1152]{1,0:T(8,128)(2,1)S(1)} %slice.164), channel_id=1, source_target_pairs={{0,2},{1,3},{2,0},{3,1},{4,6},{5,7},{6,4},{7,5},{8,10},{9,11},{10,... | collective-permute-start | bytes 1769480 | tf_op jit(solution)/shard_map/ppermute | solution.py:847
  313.1 21.4 %collective-permute-start.36 = (bf16[4,72,576]{2,1,0:T(8,128)(2,1)}, bf16[4,72,576]{2,1,0:T(8,128)(2,1)S(1)}, u32[]{:S(2)}, u32[]{:S(2)}) collective-permute-start(bf16[4,72,576]{2,1,0:T(8,128)(2,1)} %sum_pieces.17), channel_id=1, source_target_pairs={{0,16},{4,20},{8,24},{12,28},{16,0},{20,4},{24,8},{28,12},{1,17},{... | collective-permute-start | bytes 995336 | tf_op jit(solution)/shard_map/ppermute | solution.py:748
  313.6 3.8 collective-permute-start.31
  316.4 5.1 %collective-permute-start.40 = (bf16[2,2,12,1152]{3,2,1,0:T(8,128)(2,1)S(1)}, bf16[2,2,12,1152]{3,2,1,0:T(8,128)(2,1)S(1)}, u32[]{:S(2)}, u32[]{:S(2)}) collective-permute-start(bf16[2,2,12,1152]{3,2,1,0:T(8,128)(2,1)S(1)} %pad_maximum_fusion.9), channel_id=1, source_target_pairs={{0,8},{4,12},{8,0},{12,4},{16,24},{20,28},{24,16},{28,20},{1,9},{5... | collective-permute-start | bytes 331784 | tf_op jit(solution)/shard_map/ppermute | solution.py:786
  317.4 9.9 %collective-permute-start.34 = (bf16[2,144,1152]{2,1,0:T(8,128)(2,1)S(1)}, bf16[2,144,1152]{2,1,0:T(8,128)(2,1)S(1)}, u32[]{:S(2)}, u32[]{:S(2)}) collective-permute-start(bf16[2,144,1152]{2,1,0:T(8,128)(2,1)S(1)} %maximum_select_fusion), channel_id=1, source_target_pairs={{0,1},{1,0},{2,3},{3,2},{4,5},{5,4},{6,7},{7,6},{8,9},{9,8},{10,11... | collective-permute-start | bytes 1990664 | tf_op jit(solution)/shard_map/ppermute | solution.py:850
  339.4 4.0 %collective-permute-start.37 = (f32[4324]{0:T(1024)S(1)}, f32[4324]{0:T(1024)S(1)}, u32[]{:S(2)}, u32[]{:S(2)}) collective-permute-start(f32[4324]{0:T(1024)S(1)} %add.128), channel_id=1, source_target_pairs={{0,8},{4,12},{8,0},{12,4},{16,24},{20,28},{24,16},{28,20},{1,9},{5... | collective-permute-start | bytes 51896 | tf_op jit(solution)/shard_map/ppermute | solution.py:804
  339.8 17.7 %collective-permute-start.43 = (bf16[4,2,12,1152]{3,2,1,0:T(8,128)(2,1)S(1)}, bf16[4,2,12,1152]{3,2,1,0:T(8,128)(2,1)S(1)}, u32[]{:S(2)}, u32[]{:S(2)}) collective-permute-start(bf16[4,2,12,1152]{3,2,1,0:T(8,128)(2,1)S(1)} %pad_maximum_fusion.7), channel_id=1, source_target_pairs={{0,16},{4,20},{8,24},{12,28},{16,0},{20,4},{24,8},{28,12},{1,17},{... | collective-permute-start | bytes 663560 | tf_op jit(solution)/shard_map/ppermute | solution.py:786
  343.4 10.2 %collective-permute-start.38 = (f32[4324]{0:T(1024)S(1)}, f32[4324]{0:T(1024)S(1)}, u32[]{:S(2)}, u32[]{:S(2)}) collective-permute-start(f32[4324]{0:T(1024)S(1)} %add.129), channel_id=1, source_target_pairs={{0,16},{4,20},{8,24},{12,28},{16,0},{20,4},{24,8},{28,12},{1,17},{... | collective-permute-start | bytes 51896 | tf_op jit(solution)/shard_map/ppermute | solution.py:804
  343.9 16.4 %collective-permute-start.41 = (bf16[72,2304]{1,0:T(8,128)(2,1)S(1)}, bf16[72,2304]{1,0:T(8,128)(2,1)S(1)}, u32[]{:S(2)}, u32[]{:S(2)}) collective-permute-start(bf16[72,2304]{1,0:T(8,128)(2,1)S(1)} %constant_dynamic-update-slice_fusion.4), channel_id=1, source_target_pairs={{0,2},{1,3},{2,0},{3,1},{4,6},{5,7},{6,4},{7,5},{8,10},{9,11},{10,... | collective-permute-start | bytes 995336 | tf_op jit(solution)/shard_map/ppermute | solution.py:847
  345.6 14.6 %collective-permute-start.39 = (bf16[72,2304]{1,0:T(8,128)(2,1)S(1)}, bf16[72,2304]{1,0:T(8,128)(2,1)S(1)}, u32[]{:S(2)}, u32[]{:S(2)}) collective-permute-start(bf16[72,2304]{1,0:T(8,128)(2,1)S(1)} %concatenate.92), channel_id=1, source_target_pairs={{0,2},{1,3},{2,0},{3,1},{4,6},{5,7},{6,4},{7,5},{8,10},{9,11},{10,... | collective-permute-start | bytes 995336 | tf_op jit(solution)/shard_map/ppermute | solution.py:847
  360.4 2.2 collective-permute-start.42
  360.6 4.3 %collective-permute-start.44 = (bf16[144,2304]{1,0:T(8,128)(2,1)S(1)}, bf16[144,2304]{1,0:T(8,128)(2,1)S(1)}, u32[]{:S(2)}, u32[]{:S(2)}) collective-permute-start(bf16[144,2304]{1,0:T(8,128)(2,1)S(1)} %pad_maximum_fusion.5), channel_id=1, source_target_pairs={{0,1},{1,0},{2,3},{3,2},{4,5},{5,4},{6,7},{7,6},{8,9},{9,8},{10,11... | collective-permute-start | bytes 1990664 | tf_op jit(solution)/shard_map/ppermute | solution.py:850
  (50 other events, 239.6 us)
Sparse Core Ops, SparseCore 0:
  100.0 175.1 reduce-scatter.1
